TPU v7x, 32 devices: a whole 2x2x4 slice. The times are simulated.
32 devices in a mesh: batch: 8 (over z, x), blk: 4 (over y, core).
Axes of the slice: x: 2, y: 2, z: 4, core: 2. Of those that a mesh axis runs over, the one named last changes fastest.
Arguments:
- tokens: bfloat16 [8, 512, 2048], P('batch', 'blk'), may hold values from -6 to 6
- lengths: int32 [8, 4], P('batch'), may hold values from 0 to 512, as said below
- ln1_gain: bfloat16 [2048], P(('batch', 'blk')), may hold values from 0.5 to 1.5
- w_query: bfloat16 [2048, 2048], P(('batch', 'blk')), may hold values from -0.125 to 0.125
- w_key: bfloat16 [2048, 2048], P(('batch', 'blk')), may hold values from -0.125 to 0.125
- w_value: bfloat16 [2048, 4096], P(('batch', 'blk')), may hold values from -0.125 to 0.125
- w_gate: bfloat16 [2048, 4096], P(('batch', 'blk')), may hold values from -0.125 to 0.125
- w_out: bfloat16 [4096, 2048], P(('batch', 'blk')), may hold values from -0.125 to 0.125
- ln2_gain: bfloat16 [2048], P(('batch', 'blk')), may hold values from 0.5 to 1.5
- w_up: bfloat16 [2048, 4096], P(('batch', 'blk')), may hold values from -0.125 to 0.125
- w_down: bfloat16 [4096, 2048], P(('batch', 'blk')), may hold values from -0.125 to 0.125
- cotangent: bfloat16 [8, 512, 2048], P('batch', 'blk'), may hold values from -6 to 6
Outputs:
- output: bfloat16 [8, 512, 2048], P('batch', 'blk')
- tokens_grad: float32 [8, 512, 2048], P('batch', 'blk')
- ln1_gain_grad: float32 [2048], P(('batch', 'blk'))
- w_query_grad: float32 [2048, 2048], P(('batch', 'blk'))
- w_key_grad: float32 [2048, 2048], P(('batch', 'blk'))
- w_value_grad: float32 [2048, 4096], P(('batch', 'blk'))
- w_gate_grad: float32 [2048, 4096], P(('batch', 'blk'))
- w_out_grad: float32 [4096, 2048], P(('batch', 'blk'))
- ln2_gain_grad: float32 [2048], P(('batch', 'blk'))
- w_up_grad: float32 [2048, 4096], P(('batch', 'blk'))
- w_down_grad: float32 [4096, 2048], P(('batch', 'blk'))
Inputs may be any that keep to these rules, and one draw needn't show every extreme that they name: `lengths`: each row's four entries sum to 512. A row either holds one sequence of 512 tokens and no padding (its other entries 0; at least one row does), or three sequences of 128 tokens or more each, followed by fewer than 128 tokens of padding.
All inputs are finite; a program needn't handle non-finite values.
Results may differ from a plain program's by a relative error of at most 0.014.
Values may be sent and summed in bfloat16 or wider, within the bound.
No kernel may reach another device: no remote copies, remote signals or barrier semaphores. Data moves between devices by JAX's collectives and lax.ppermute only.
A program may use at most 576 MiB of HBM per device.

v0:
```python
import math

import jax
import jax.numpy as jnp
from jax import lax
from jax.sharding import PartitionSpec as P

HEADS = 8
HK = 256
HV = 512


EPS = 1e-06
GN_EPS = 0.1
ROPE_BASE = 10000.0
DECAY_SCALE = 32.0


def passed_along(value, axis, steps):
    count = lax.axis_size(axis)
    first, last = (max(0, -steps), min(count, count - steps))
    return lax.ppermute(value, axis, [(source, source + steps) for source in range(first, last)])


def shortened(shard):
    return jax.tree.map(lambda a: a.astype(jnp.bfloat16) if a.dtype == jnp.float32 else a, shard)


def layer_norm(values, gain):
    centered = values - jnp.mean(values, axis=-1, keepdims=True)
    spread = jnp.mean(centered * centered, axis=-1, keepdims=True)
    return centered * lax.rsqrt(spread + EPS) * gain


def group_gate(mixed, gate):
    centered = mixed - jnp.mean(mixed, axis=-1, keepdims=True)
    spread = jnp.mean(centered * centered, axis=-1, keepdims=True)
    normed = centered * lax.rsqrt(spread + GN_EPS)
    return normed.reshape(gate.shape) * jax.nn.silu(gate)


def gelu_exact(values):
    return jax.nn.gelu(values, approximate=False)


def rotary_tables(positions, half):
    expo = jnp.arange(half, dtype=jnp.float32) / (half - 1)
    freq = jnp.exp(-math.log(ROPE_BASE) * expo)
    angle = positions[:, None] * freq[None, :]
    return (jnp.cos(angle), jnp.sin(angle))


def rotate(values, cosine, sine):
    half = values.shape[-1] // 2
    front = values[..., :half]
    back = values[..., half:]
    cosine = cosine[:, None, :]
    sine = sine[:, None, :]
    return jnp.concatenate([front * cosine - back * sine, back * cosine + front * sine], axis=-1)


def unrotate(grads, cosine, sine):
    half = grads.shape[-1] // 2
    front = grads[..., :half]
    back = grads[..., half:]
    cosine = cosine[:, None, :]
    sine = sine[:, None, :]
    return jnp.concatenate([front * cosine + back * sine, back * cosine - front * sine], axis=-1)


def segment_of(positions, first_cut, second_cut, third_cut):
    return (
        (positions >= first_cut).astype(jnp.int32)
        + (positions >= second_cut).astype(jnp.int32)
        + (positions >= third_cut).astype(jnp.int32)
    )


def block_terms(rotated_queries, rotated_keys, head_values, seg, valid, seg_prev, rates):
    tlen = rotated_queries.shape[0]
    loc = jnp.arange(tlen, dtype=jnp.int32)
    gap = (loc[:, None] - loc[None, :]).astype(jnp.float32)
    allowed = (seg[:, None] == seg[None, :]) & (gap >= 0) & valid[:, None] & valid[None, :]
    decay = jnp.where(
        allowed[None], jnp.exp(-rates[:, None, None] * jnp.maximum(gap, 0.0)[None]), 0.0
    )
    score_matrix = jnp.einsum(
        "svg,uvg->vsu", rotated_queries, rotated_keys, preferred_element_type=jnp.float32
    )
    weights = (score_matrix * decay).astype(jnp.bfloat16)
    inner = jnp.einsum("hnm,mhe->nhe", weights, head_values, preferred_element_type=jnp.float32)
    locf = loc.astype(jnp.float32)
    reads = ((seg == seg_prev) & valid).astype(jnp.float32)
    read_scale = jnp.exp(-(locf[:, None] + 1.0) * rates[None, :]) * reads[:, None]
    query_scaled = (rotated_queries.astype(jnp.float32) * read_scale[:, :, None]).astype(
        jnp.bfloat16
    )
    seg_last = seg[tlen - 1]
    writes = ((seg == seg_last) & valid).astype(jnp.float32)
    write_scale = jnp.exp(-(tlen - 1.0 - locf)[:, None] * rates[None, :]) * writes[:, None]
    scaled_key_rows = (rotated_keys.astype(jnp.float32) * write_scale[:, :, None]).astype(
        jnp.bfloat16
    )
    state_update = jnp.einsum(
        "yzj,yzw->zjw", scaled_key_rows, head_values, preferred_element_type=jnp.float32
    )
    carry_scale = jnp.exp(-tlen * rates) * (seg_last == seg_prev).astype(jnp.float32)
    return (
        decay,
        weights,
        inner,
        read_scale,
        query_scaled,
        write_scale,
        scaled_key_rows,
        state_update,
        carry_scale,
    )


def shards(
    tokens,
    lengths,
    ln1_gain,
    w_query,
    w_key,
    w_value,
    w_gate,
    w_out,
    ln2_gain,
    w_up,
    w_down,
    cotangent,
):
    single_float = jnp.float32
    bf16 = jnp.bfloat16
    tok = tokens[0]
    tlen = tok.shape[0]
    nblk = lax.axis_size("blk")
    index = lax.axis_index("blk")
    lens = lengths[0]
    w_q, w_k, w_v, w_g, w_o, gain_one = (
        lax.all_gather(w_query, ("batch", "blk"), axis=0, tiled=True),
        lax.all_gather(w_key, ("batch", "blk"), axis=0, tiled=True),
        lax.all_gather(w_value, ("batch", "blk"), axis=0, tiled=True),
        lax.all_gather(w_gate, ("batch", "blk"), axis=0, tiled=True),
        lax.all_gather(w_out, ("batch", "blk"), axis=0, tiled=True),
        lax.all_gather(ln1_gain, ("batch", "blk"), axis=0, tiled=True),
    )
    loc = jnp.arange(tlen, dtype=jnp.int32)
    first_cut = lens[0]
    second_cut = lens[0] + lens[1]
    third_cut = lens[0] + lens[1] + lens[2]
    pos = index * tlen + loc
    seg = segment_of(pos, first_cut, second_cut, third_cut)
    valid = seg < 3
    prev_pos = index * tlen - 1
    seg_before = segment_of(prev_pos, first_cut, second_cut, third_cut)
    seg_prev = jnp.where(index == 0, -1, seg_before)
    rates = DECAY_SCALE * jnp.exp2(-jnp.arange(HEADS, dtype=single_float)) / (tlen * nblk)
    cosine, sine = rotary_tables(pos.astype(single_float), HK // 2)
    key_norm = 1.0 / math.sqrt(HK)
    xf = tok.astype(single_float)
    h1, norm1_back = jax.vjp(layer_norm, xf, gain_one.astype(single_float))
    h1r = h1.astype(bf16)
    query = jnp.dot(h1r, w_q, preferred_element_type=single_float)
    key = jnp.dot(h1r, w_k, preferred_element_type=single_float)
    value = jnp.dot(h1r, w_v, preferred_element_type=single_float)
    gate = jnp.dot(h1r, w_g, preferred_element_type=single_float)
    rotated_queries = rotate(query.reshape(tlen, HEADS, HK), cosine, sine).astype(bf16)
    rotated_keys = (rotate(key.reshape(tlen, HEADS, HK), cosine, sine) * key_norm).astype(bf16)
    head_values = value.reshape(tlen, HEADS, HV).astype(bf16)
    (
        decay,
        weights,
        inner,
        read_scale,
        query_scaled,
        write_scale,
        scaled_key_rows,
        state_update,
        carry_scale,
    ) = block_terms(rotated_queries, rotated_keys, head_values, seg, valid, seg_prev, rates)
    state = jnp.zeros_like(state_update)
    for hop in range(nblk - 1):
        state = passed_along(carry_scale[:, None, None] * state + state_update, "blk", 1)
    past = state.astype(bf16)
    outer = jnp.einsum("nhd,hde->nhe", query_scaled, past, preferred_element_type=single_float)
    mixed = inner + outer
    gated, gate_back = jax.vjp(group_gate, mixed, gate)
    gated_r = gated.astype(bf16)
    residual = xf + jnp.dot(gated_r, w_o, preferred_element_type=single_float)
    w_u, w_d, gain_two = (
        lax.all_gather(w_up, ("batch", "blk"), axis=0, tiled=True),
        lax.all_gather(w_down, ("batch", "blk"), axis=0, tiled=True),
        lax.all_gather(ln2_gain, ("batch", "blk"), axis=0, tiled=True),
    )
    h2, norm2_back = jax.vjp(layer_norm, residual, gain_two.astype(single_float))
    h2r = h2.astype(bf16)
    hidden = jnp.dot(h2r, w_u, preferred_element_type=single_float)
    act, act_back = jax.vjp(gelu_exact, hidden)
    act_r = act.astype(bf16)
    output = residual + jnp.dot(act_r, w_d, preferred_element_type=single_float)
    up_back, down_back = (
        lax.all_gather(w_up, ("batch", "blk"), axis=0, tiled=True),
        lax.all_gather(w_down, ("batch", "blk"), axis=0, tiled=True),
    )
    dyr = cotangent[0]
    down_grad = jnp.einsum("nf,nd->fd", act_r, dyr, preferred_element_type=single_float)
    d_act = jnp.einsum("nd,fd->nf", dyr, down_back, preferred_element_type=single_float)
    d_hidden = act_back(d_act)[0].astype(bf16)
    up_grad = jnp.einsum("nd,nf->df", h2r, d_hidden, preferred_element_type=single_float)
    d_h2 = jnp.einsum("nf,df->nd", d_hidden, up_back, preferred_element_type=single_float)
    d_res_norm, gain2_grad = norm2_back(d_h2)
    d_res = dyr.astype(single_float) + d_res_norm
    up_g, down_g, gain2_g = (
        lax.psum_scatter(up_grad, ("batch", "blk"), scatter_dimension=0, tiled=True),
        lax.psum_scatter(down_grad, ("batch", "blk"), scatter_dimension=0, tiled=True),
        lax.psum_scatter(gain2_grad, ("batch", "blk"), scatter_dimension=0, tiled=True),
    )
    q_back, k_back, v_back, g_back, o_back = (
        lax.all_gather(w_query, ("batch", "blk"), axis=0, tiled=True),
        lax.all_gather(w_key, ("batch", "blk"), axis=0, tiled=True),
        lax.all_gather(w_value, ("batch", "blk"), axis=0, tiled=True),
        lax.all_gather(w_gate, ("batch", "blk"), axis=0, tiled=True),
        lax.all_gather(w_out, ("batch", "blk"), axis=0, tiled=True),
    )
    d_branch = d_res.astype(bf16)
    out_grad = jnp.einsum("nv,nd->vd", gated_r, d_branch, preferred_element_type=single_float)
    d_gated = jnp.einsum("nd,vd->nv", d_branch, o_back, preferred_element_type=single_float)
    d_mixed, d_gate = gate_back(d_gated)
    d_gate_r = d_gate.astype(bf16)
    d_mixed_r = d_mixed.astype(bf16)
    local_grad = jnp.einsum(
        "nhd,nhe->hde", query_scaled, d_mixed_r, preferred_element_type=single_float
    )
    later = jnp.zeros_like(local_grad)
    for hop in range(nblk - 1):
        later = passed_along(shortened(carry_scale[:, None, None] * later + local_grad), "blk", -1)
    later_rows = later.astype(bf16)
    d_weights = jnp.einsum(
        "nhe,mhe->hnm", d_mixed_r, head_values, preferred_element_type=single_float
    )
    scores_gradient = (d_weights * decay).astype(bf16)
    rotated_query_gradient = jnp.einsum(
        "xoc,cxr->oxr", scores_gradient, rotated_keys, preferred_element_type=single_float
    )
    rotated_query_gradient = rotated_query_gradient + read_scale[:, :, None] * jnp.einsum(
        "nhe,hde->nhd", d_mixed_r, past, preferred_element_type=single_float
    )
    rotated_key_gradient = jnp.einsum(
        "osv,soi->voi", scores_gradient, rotated_queries, preferred_element_type=single_float
    )
    rotated_key_gradient = rotated_key_gradient + write_scale[:, :, None] * jnp.einsum(
        "tyu,yqu->tyq", head_values, later_rows, preferred_element_type=single_float
    )
    head_value_gradient = jnp.einsum(
        "hnm,nhe->mhe", weights, d_mixed_r, preferred_element_type=single_float
    )
    head_value_gradient = head_value_gradient + jnp.einsum(
        "lyi,yiz->lyz", scaled_key_rows, later_rows, preferred_element_type=single_float
    )
    d_query = unrotate(rotated_query_gradient, cosine, sine).reshape(tlen, HEADS * HK).astype(bf16)
    d_key = (
        (unrotate(rotated_key_gradient, cosine, sine) * key_norm)
        .reshape(tlen, HEADS * HK)
        .astype(bf16)
    )
    d_value = head_value_gradient.reshape(tlen, HEADS * HV).astype(bf16)
    q_grad = jnp.einsum("nd,nk->dk", h1r, d_query, preferred_element_type=single_float)
    k_grad = jnp.einsum("nd,nk->dk", h1r, d_key, preferred_element_type=single_float)
    v_grad = jnp.einsum("nd,nk->dk", h1r, d_value, preferred_element_type=single_float)
    g_grad = jnp.einsum("nd,nk->dk", h1r, d_gate_r, preferred_element_type=single_float)
    d_h1 = jnp.einsum("nk,dk->nd", d_query, q_back, preferred_element_type=single_float)
    d_h1 = d_h1 + jnp.einsum("nk,dk->nd", d_key, k_back, preferred_element_type=single_float)
    d_h1 = d_h1 + jnp.einsum("nk,dk->nd", d_value, v_back, preferred_element_type=single_float)
    d_h1 = d_h1 + jnp.einsum("nk,dk->nd", d_gate_r, g_back, preferred_element_type=single_float)
    d_tok_norm, gain1_grad = norm1_back(d_h1)
    tokens_grad = d_res + d_tok_norm
    q_g, k_g, v_g, g_g, o_g, gain1_g = (
        lax.psum_scatter(q_grad, ("batch", "blk"), scatter_dimension=0, tiled=True),
        lax.psum_scatter(k_grad, ("batch", "blk"), scatter_dimension=0, tiled=True),
        lax.psum_scatter(v_grad, ("batch", "blk"), scatter_dimension=0, tiled=True),
        lax.psum_scatter(g_grad, ("batch", "blk"), scatter_dimension=0, tiled=True),
        lax.psum_scatter(out_grad, ("batch", "blk"), scatter_dimension=0, tiled=True),
        lax.psum_scatter(gain1_grad, ("batch", "blk"), scatter_dimension=0, tiled=True),
    )
    return (
        output.astype(bf16)[None],
        tokens_grad[None],
        gain1_g,
        q_g,
        k_g,
        v_g,
        g_g,
        o_g,
        gain2_g,
        up_g,
        down_g,
    )


def solution(mesh):
    placed = (
        P("batch", "blk", None),
        P("batch", None),
        P(("batch", "blk")),
        P(("batch", "blk"), None),
        P(("batch", "blk"), None),
        P(("batch", "blk"), None),
        P(("batch", "blk"), None),
        P(("batch", "blk"), None),
        P(("batch", "blk")),
        P(("batch", "blk"), None),
        P(("batch", "blk"), None),
        P("batch", "blk", None),
    )
    return jax.shard_map(
        shards,
        mesh=mesh,
        in_specs=placed,
        out_specs=(
            P("batch", "blk", None),
            P("batch", "blk", None),
            P(("batch", "blk")),
            P(("batch", "blk"), None),
            P(("batch", "blk"), None),
            P(("batch", "blk"), None),
            P(("batch", "blk"), None),
            P(("batch", "blk"), None),
            P(("batch", "blk")),
            P(("batch", "blk"), None),
            P(("batch", "blk"), None),
        ),
        check_vma=False,
    )
```

profile of v0, /device:TPU:0, one launch (start us, length us, event | category | flops | bytes accessed | tf_op | source)
XLA Modules:
  0.0 3094.7 jit_solution(13343744701806680853)
XLA Ops:
  12.5 42.6 %all-reduce.5 = (bf16[2048]{0:T(1024)(128)(2,1)S(1)}, bf16[2048]{0:T(1024)(128)(2,1)S(1)}) all-reduce(bf16[2048]{0:T(1024)(128)(2,1)S(1)} %dynamic-update-slice, bf16[2048]{0:T(1024)(128)(2,1)S(1)} %dynamic-update-slice.1), channel_id=1, replica_groups=mesh['batch'=8,'blk'=4] {'batch','blk'}, use_global_device_ids=true, to_apply=%add | all-reduce | flops 4096 | bytes 16384
  62.5 29.0 all-gather.10.cloned.1.call-done
  91.4 12.4 copy.66
  103.8 66.7 %all-gather.12.cloned.1.call-done = bf16[2048,2048]{1,0:T(8,128)(2,1)} async-done(((bf16[64,2048]{1,0:T(8,128)(2,1)}), bf16[2048,2048]{1,0:T(8,128)(2,1)}) %all-gather.12.cloned.1.call-update) | async-done | bytes 8388624 | tf_op jit(solution)/shard_map/all_gather | solution.py:144
  170.5 12.3 copy.67
  192.6 94.3 %all-gather.8.cloned.1.call-done = bf16[2048,4096]{1,0:T(8,128)(2,1)} async-done(((bf16[64,4096]{1,0:T(8,128)(2,1)}), bf16[2048,4096]{1,0:T(8,128)(2,1)}) %all-gather.8.cloned.1.call-update) | async-done | bytes 16777232 | tf_op jit(solution)/shard_map/all_gather | solution.py:145
  286.9 22.6 copy.65
  332.3 71.4 %collective-permute-start.1 = (f32[8,256,512]{2,1,0:T(8,128)S(1)}, f32[8,256,512]{2,1,0:T(8,128)S(1)}, u32[]{:S(2)}, u32[]{:S(2)}) collective-permute-start(f32[8,256,512]{2,1,0:T(8,128)S(1)} %multiply_add_fusion.1), channel_id=1, source_target_pairs={{0,1},{1,2},{2,3},{4,5},{5,6},{6,7},{8,9},{9,10},{10,11},{12,13},{... | collective-permute-start | bytes 12582920 | tf_op jit(solution)/shard_map/ppermute | solution.py:22
  411.4 54.4 %collective-permute-start.2 = (bf16[8,256,512]{2,1,0:T(8,128)(2,1)S(1)}, bf16[8,256,512]{2,1,0:T(8,128)(2,1)S(1)}, u32[]{:S(2)}, u32[]{:S(2)}) collective-permute-start(bf16[8,256,512]{2,1,0:T(8,128)(2,1)S(1)} %multiply_add_fusion), channel_id=1, source_target_pairs={{0,1},{1,2},{2,3},{4,5},{5,6},{6,7},{8,9},{9,10},{10,11},{12,13},{... | collective-permute-start | bytes 6291464 | tf_op jit(solution)/shard_map/ppermute | solution.py:22
  488.0 46.6 %all-gather.16.cloned.1.call-done = bf16[4096,2048]{1,0:T(8,128)(2,1)} async-done(((bf16[128,2048]{1,0:T(8,128)(2,1)}), bf16[4096,2048]{1,0:T(8,128)(2,1)}) %all-gather.16.cloned.1.call-update) | async-done | bytes 16777232 | tf_op jit(solution)/shard_map/all_gather | solution.py:147
  545.4 114.0 %all-gather.18.cloned.1.call-done = bf16[2048,4096]{1,0:T(8,128)(2,1)} async-done(((bf16[64,4096]{1,0:T(8,128)(2,1)}), bf16[2048,4096]{1,0:T(8,128)(2,1)}) %all-gather.18.cloned.1.call-update) | async-done | bytes 16777232 | tf_op jit(solution)/shard_map/all_gather | solution.py:194
  669.3 106.0 %all-gather.20.cloned.1.call-done = bf16[4096,2048]{1,0:T(8,128)(2,1)} async-done(((bf16[128,2048]{1,0:T(8,128)(2,1)}), bf16[4096,2048]{1,0:T(8,128)(2,1)}) %all-gather.20.cloned.1.call-update) | async-done | bytes 16777232 | tf_op jit(solution)/shard_map/all_gather | solution.py:195
  775.4 23.8 add_convert_fusion.5
  799.1 13.6 multiply_reduce_fusion.2
  817.4 14.8 fusion.60
  861.7 74.5 %collective-permute-done.4 = bf16[8,256,512]{2,1,0:T(8,128)(2,1)S(1)} collective-permute-done((bf16[8,256,512]{2,1,0:T(8,128)(2,1)S(1)}, bf16[8,256,512]{2,1,0:T(8,128)(2,1)S(1)}, u32[]{:S(2)}, u32[]{:S(2)}) %collective-permute-start.4) | collective-permute-done | bytes 2097184 | tf_op jit(solution)/shard_map/ppermute | solution.py:22
  939.2 69.8 %collective-permute-done.5 = bf16[8,256,512]{2,1,0:T(8,128)(2,1)S(1)} collective-permute-done((bf16[8,256,512]{2,1,0:T(8,128)(2,1)S(1)}, bf16[8,256,512]{2,1,0:T(8,128)(2,1)S(1)}, u32[]{:S(2)}, u32[]{:S(2)}) %collective-permute-start.5) | collective-permute-done | bytes 2097184 | tf_op jit(solution)/shard_map/ppermute | solution.py:22
  1020.5 13.4 fusion.71
  1035.2 14.4 fusion.93
  1050.8 14.8 fusion.76
  1065.8 16.6 fusion.40
  1086.0 13.7 fusion.53
  1108.0 12.9 fusion.92
  1121.0 14.1 fusion.3
  1135.1 12.8 fusion.91
  1155.9 113.7 %all-reduce.4 = (f32[2048]{0:T(1024)S(1)}, f32[2048]{0:T(1024)S(1)}) all-reduce(f32[2048]{0:T(1024)S(1)} %get-tuple-element.13, f32[2048]{0:T(1024)S(1)} %copy-done.54), channel_id=2, replica_groups=mesh['batch'=8,'blk'=4] {'batch','blk'}, use_global_device_ids=true, to_apply=%region_13.14.clone | all-reduce | flops 4096 | bytes 32768
  1273.3 14.9 reduce-scatter.10.cloned.1.call-done
  1288.2 357.8 %reduce-scatter.14.cloned.1.call-done = f32[64,4096]{1,0:T(8,128)} async-done(((f32[2048,4096]{1,0:T(8,128)}), f32[64,4096]{1,0:T(8,128)}) %reduce-scatter.14.cloned.1.call-update) | async-done | bytes 1048592 | tf_op jit(solution)/shard_map/reduce_scatter | solution.py:284
  1646.1 360.5 %reduce-scatter.16.cloned.1.call-done = f32[128,2048]{1,0:T(8,128)} async-done(((f32[4096,2048]{1,0:T(8,128)}), f32[128,2048]{1,0:T(8,128)}) %reduce-scatter.16.cloned.1.call-update) | async-done | bytes 1048592 | tf_op jit(solution)/shard_map/reduce_scatter | solution.py:285
  2006.6 360.3 %reduce-scatter.18.cloned.1.call-done = f32[64,4096]{1,0:T(8,128)} async-done(((f32[2048,4096]{1,0:T(8,128)}), f32[64,4096]{1,0:T(8,128)}) %reduce-scatter.18.cloned.1.call-update) | async-done | bytes 1048592 | tf_op jit(solution)/shard_map/reduce_scatter | solution.py:217
  2366.9 360.5 %reduce-scatter.20.cloned.1.call-done = f32[128,2048]{1,0:T(8,128)} async-done(((f32[4096,2048]{1,0:T(8,128)}), f32[128,2048]{1,0:T(8,128)}) %reduce-scatter.20.cloned.1.call-update) | async-done | bytes 1048592 | tf_op jit(solution)/shard_map/reduce_scatter | solution.py:218
  2727.4 360.3 %reduce-scatter.12.cloned.1.call-done = f32[64,4096]{1,0:T(8,128)} async-done(((f32[2048,4096]{1,0:T(8,128)}), f32[64,4096]{1,0:T(8,128)}) %reduce-scatter.12.cloned.1.call-update) | async-done | bytes 1048592 | tf_op jit(solution)/shard_map/reduce_scatter | solution.py:283
  (265 shorter events, 166.5 us)
Async XLA Ops:
  7.2 84.2 %all-gather.10.cloned.1.call-start = ((), (), s32[]{:S(2)}) async-start(), calls=%async_computation.8 | async-start | bytes 8650752 | tf_op jit(solution)/shard_map/all_gather | solution.py:143
  8.0 162.6 %all-gather.12.cloned.1.call-start = ((), (), s32[]{:S(2)}) async-start(), calls=%async_computation.9 | async-start | bytes 8650752 | tf_op jit(solution)/shard_map/all_gather | solution.py:144
  8.7 278.2 %all-gather.8.cloned.1.call-start = ((), (), s32[]{:S(2)}) async-start(), calls=%async_computation.7 | async-start | bytes 17301504 | tf_op jit(solution)/shard_map/all_gather | solution.py:145
  9.4 466.6 %all-gather.14.cloned.1.call-start = ((), (), s32[]{:S(2)}) async-start(), calls=%async_computation.10 | async-start | bytes 17301504 | tf_op jit(solution)/shard_map/all_gather | solution.py:146
  10.0 524.6 %all-gather.16.cloned.1.call-start = ((), (), s32[]{:S(2)}) async-start(), calls=%async_computation.11 | async-start | bytes 17301504 | tf_op jit(solution)/shard_map/all_gather | solution.py:147
  10.6 648.8 %all-gather.18.cloned.1.call-start = ((), (), s32[]{:S(2)}) async-start(), calls=%async_computation.12 | async-start | bytes 17301504 | tf_op jit(solution)/shard_map/all_gather | solution.py:194
  11.2 764.2 %all-gather.20.cloned.1.call-start = ((), (), s32[]{:S(2)}) async-start(), calls=%async_computation.13 | async-start | bytes 17301504 | tf_op jit(solution)/shard_map/all_gather | solution.py:195
  11.9 1261.4 %reduce-scatter.8.cloned.1.call-start = ((), (), s32[]{:S(2)}) async-start(), calls=%async_computation.14 | async-start | bytes 17301504 | tf_op jit(solution)/shard_map/reduce_scatter | solution.py:281
  60.3 260.7 %copy-start.63 = (f32[8]{0:T(128)}, f32[8]{0:T(128)S(1)}, u32[]{:S(2)}) copy-start(f32[8]{0:T(128)S(1)} %broadcast_multiply_fusion.1) | copy-start | bytes 100
  60.5 249.0 %copy-start.30 = (f32[128]{0:T(128)}, f32[128]{0:T(128)S(1)}, u32[]{:S(2)}) copy-start(f32[128]{0:T(128)S(1)} %broadcast_multiply_fusion.4) | copy-start | bytes 1540
  60.8 248.7 %copy-start.36 = (f32[128]{0:T(128)}, f32[128]{0:T(128)S(1)}, u32[]{:S(2)}) copy-start(f32[128]{0:T(128)S(1)} %fusion.68) | copy-start | bytes 1540
  62.2 258.8 %copy-start.45 = (f32[128,8]{0,1:T(8,128)}, f32[128,8]{0,1:T(8,128)S(1)}, u32[]{:S(2)}) copy-start(f32[128,8]{0,1:T(8,128)S(1)} %get-tuple-element.38) | copy-start | bytes 12292
  192.5 273.5 %copy-start.22 = (bf16[128,8,128]{2,0,1:T(8,128)(2,1)}, bf16[128,8,128]{2,0,1:T(8,128)(2,1)S(1)}, u32[]{:S(2)}) copy-start(bf16[128,8,128]{2,0,1:T(8,128)(2,1)S(1)} %get-tuple-element.30) | copy-start | bytes 786436
  321.0 145.4 %copy-start.5 = (bf16[128,8,512]{2,0,1:T(8,128)(2,1)}, bf16[128,8,512]{2,0,1:T(8,128)(2,1)S(1)}, u32[]{:S(2)}) copy-start(bf16[128,8,512]{2,0,1:T(8,128)(2,1)S(1)} %convolution_convert_fusion) | copy-start | bytes 3145732
  322.3 8.9 collective-permute-start
  324.9 85.2 %copy-start.58 = (f32[8]{0:T(128)}, f32[8]{0:T(128)S(1)}, u32[]{:S(2)}) copy-start(f32[8]{0:T(128)S(1)} %exponential_multiply_fusion.2) | copy-start | bytes 100
  332.3 77.9 %collective-permute-start.1 = (f32[8,256,512]{2,1,0:T(8,128)S(1)}, f32[8,256,512]{2,1,0:T(8,128)S(1)}, u32[]{:S(2)}, u32[]{:S(2)}) collective-permute-start(f32[8,256,512]{2,1,0:T(8,128)S(1)} %multiply_add_fusion.1), channel_id=1, source_target_pairs={{0,1},{1,2},{2,3},{4,5},{5,6},{6,7},{8,9},{9,10},{10,11},{12,13},{... | collective-permute-start | bytes 12582920 | tf_op jit(solution)/shard_map/ppermute | solution.py:22
  411.4 58.1 %collective-permute-start.2 = (bf16[8,256,512]{2,1,0:T(8,128)(2,1)S(1)}, bf16[8,256,512]{2,1,0:T(8,128)(2,1)S(1)}, u32[]{:S(2)}, u32[]{:S(2)}) collective-permute-start(bf16[8,256,512]{2,1,0:T(8,128)(2,1)S(1)} %multiply_add_fusion), channel_id=1, source_target_pairs={{0,1},{1,2},{2,3},{4,5},{5,6},{6,7},{8,9},{9,10},{10,11},{12,13},{... | collective-permute-start | bytes 6291464 | tf_op jit(solution)/shard_map/ppermute | solution.py:22
  851.1 437.2 %reduce-scatter.10.cloned.1.call-start = ((), (), s32[]{:S(2)}) async-start(), calls=%async_computation.15 | async-start | bytes 17301504 | tf_op jit(solution)/shard_map/reduce_scatter | solution.py:282
  853.3 6.1 collective-permute-start.3
  860.2 78.6 %copy-start.27 = (bf16[8,128,128]{2,1,0:T(8,128)(2,1)S(1)}, bf16[8,128,128]{2,1,0:T(8,128)(2,1)}, u32[]{:S(2)}) copy-start(bf16[8,128,128]{2,1,0:T(8,128)(2,1)} %copy-done.26) | copy-start | bytes 786436
  860.2 148.8 %copy-start.46 = (f32[128,8]{0,1:T(8,128)S(1)}, f32[128,8]{0,1:T(8,128)}, u32[]{:S(2)}) copy-start(f32[128,8]{0,1:T(8,128)} %copy-done.45) | copy-start | bytes 12292
  860.2 75.9 %collective-permute-start.4 = (bf16[8,256,512]{2,1,0:T(8,128)(2,1)S(1)}, bf16[8,256,512]{2,1,0:T(8,128)(2,1)S(1)}, u32[]{:S(2)}, u32[]{:S(2)}) collective-permute-start(bf16[8,256,512]{2,1,0:T(8,128)(2,1)S(1)} %add_convert_fusion.1), channel_id=1, source_target_pairs={{1,0},{2,1},{3,2},{5,4},{6,5},{7,6},{9,8},{10,9},{11,10},{13,12},{... | collective-permute-start | bytes 6291464 | tf_op jit(solution)/shard_map/ppermute | solution.py:22
  937.0 72.0 %copy-start.7 = (bf16[128,8,512]{2,0,1:T(8,128)(2,1)S(1)}, bf16[128,8,512]{2,0,1:T(8,128)(2,1)}, u32[]{:S(2)}) copy-start(bf16[128,8,512]{2,0,1:T(8,128)(2,1)} %copy-done.5) | copy-start | bytes 3145732
  937.0 72.0 %collective-permute-start.5 = (bf16[8,256,512]{2,1,0:T(8,128)(2,1)S(1)}, bf16[8,256,512]{2,1,0:T(8,128)(2,1)S(1)}, u32[]{:S(2)}, u32[]{:S(2)}) collective-permute-start(bf16[8,256,512]{2,1,0:T(8,128)(2,1)S(1)} %add_convert_fusion), channel_id=1, source_target_pairs={{1,0},{2,1},{3,2},{5,4},{6,5},{7,6},{9,8},{10,9},{11,10},{13,12},{... | collective-permute-start | bytes 6291464 | tf_op jit(solution)/shard_map/ppermute | solution.py:22
  1019.3 626.8 %reduce-scatter.14.cloned.1.call-start = ((), (), s32[]{:S(2)}) async-start(), calls=%async_computation.17 | async-start | bytes 34603008 | tf_op jit(solution)/shard_map/reduce_scatter | solution.py:284
  1033.9 972.6 %reduce-scatter.16.cloned.1.call-start = ((), (), s32[]{:S(2)}) async-start(), calls=%async_computation.18 | async-start | bytes 34603008 | tf_op jit(solution)/shard_map/reduce_scatter | solution.py:285
  1049.6 1317.3 %reduce-scatter.18.cloned.1.call-start = ((), (), s32[]{:S(2)}) async-start(), calls=%async_computation.19 | async-start | bytes 34603008 | tf_op jit(solution)/shard_map/reduce_scatter | solution.py:217
  1065.6 1661.8 %reduce-scatter.20.cloned.1.call-start = ((), (), s32[]{:S(2)}) async-start(), calls=%async_computation.20 | async-start | bytes 34603008 | tf_op jit(solution)/shard_map/reduce_scatter | solution.py:218
  1082.4 2005.3 %reduce-scatter.12.cloned.1.call-start = ((), (), s32[]{:S(2)}) async-start(), calls=%async_computation.16 | async-start | bytes 34603008 | tf_op jit(solution)/shard_map/reduce_scatter | solution.py:283
  1147.8 122.9 %copy-start.62 = (f32[128]{0:T(128)S(1)}, f32[128]{0:T(128)}, u32[]{:S(2)}) copy-start(f32[128]{0:T(128)} %copy-done.61) | copy-start | bytes 1540
  1155.3 115.5 %copy-start.11 = (f32[128,2048]{1,0:T(8,128)S(1)}, f32[128,2048]{1,0:T(8,128)}, u32[]{:S(2)}) copy-start(f32[128,2048]{1,0:T(8,128)} %copy-done.10) | copy-start | bytes 3145732
  (60 other events, 241.0 us)
Sparse Core Ops, SparseCore 0:
  10.9 80.4 all-gather.9
  94.3 76.1 all-gather.11
  173.4 113.4 all-gather.7
  289.6 113.0 all-gather.13
  405.4 129.1 all-gather.15
  537.4 122.0 all-gather.17
  662.3 113.0 all-gather.19
  851.2 247.5 reduce-scatter.7
  1101.7 186.5 reduce-scatter.9
  1291.0 355.0 reduce-scatter.13
  1649.0 357.5 reduce-scatter.15
  2009.3 357.5 reduce-scatter.17
  2369.8 357.5 reduce-scatter.19
  2730.1 357.5 reduce-scatter.11
where the time goes:
time: 3110 us; the launch traced here: 3090 us
  waiting for transfers between devices  2440 us (78%)
  matrix products  256 us (8%)
  blocking collectives  156 us (5%)
  starting transfers between devices  134 us (4%)
  local copies, waits for them, and re-layouts  70.7 us (2%)
    reduce_scatter x1, waiting for transfers between devices, shards(): lax.psum_scatter(out_grad, ('batch', 'blk'), scatter_dimension=0, tiled=T...  360 us
    reduce_scatter x1, waiting for transfers between devices, shards(): lax.psum_scatter(down_grad, ('batch', 'blk'), scatter_dimension=0, tiled=...  360 us
    reduce_scatter x1, waiting for transfers between devices, shards(): lax.psum_scatter(v_grad, ('batch', 'blk'), scatter_dimension=0, tiled=True)  360 us
    reduce_scatter x1, waiting for transfers between devices, shards(): lax.psum_scatter(up_grad, ('batch', 'blk'), scatter_dimension=0, tiled=True)  360 us
    reduce_scatter x1, waiting for transfers between devices, shards(): lax.psum_scatter(g_grad, ('batch', 'blk'), scatter_dimension=0, tiled=True)  358 us
    ppermute x6, waiting for transfers between devices, passed_along(): lax.ppermute(value, axis, [(source, source + steps) for source in range(f...  164 us
    unnamed x2, blocking collectives  156 us
    ppermute x6, starting transfers between devices, passed_along(): lax.ppermute(value, axis, [(source, source + steps) for source in range(f...  133 us
  transfers between devices with their start and end apart: 20, of which 18 were waited for; matrix products, arithmetic and copies ran while one was open for 8% of the time, Pallas kernels for 0%

commit v1 on v0

v1 whole, which is shorter than its diff:
```python
import math

import jax
import jax.numpy as jnp
from jax import lax
from jax.sharding import Mesh, PartitionSpec as P

HEADS = 8
HK = 256
HV = 512
EPS = 1e-06
GN_EPS = 0.1
ROPE_BASE = 10000.0
DECAY_SCALE = 32.0

F32 = jnp.float32
BF16 = jnp.bfloat16
TP = ("x", "k")
ALL = ("z", "x", "k")


def dot(a, b):
    return jnp.dot(a, b, preferred_element_type=F32)


def dot_nt(a, b):
    return lax.dot_general(a, b, (((1,), (1,)), ((), ())), preferred_element_type=F32)


def dot_tn(a, b):
    return lax.dot_general(a, b, (((0,), (0,)), ((), ())), preferred_element_type=F32)


def group_gate(mixed, gate):
    centered = mixed - jnp.mean(mixed, axis=-1, keepdims=True)
    spread = jnp.mean(centered * centered, axis=-1, keepdims=True)
    normed = centered * lax.rsqrt(spread + GN_EPS)
    return normed * jax.nn.silu(gate)


def gelu_exact(values):
    return jax.nn.gelu(values, approximate=False)


def normed_rows(values):
    centered = values - jnp.mean(values, axis=-1, keepdims=True)
    scale = lax.rsqrt(jnp.mean(centered * centered, axis=-1, keepdims=True) + EPS)
    return centered * scale, scale


def norm_back(grads, normed, scale):
    shift = jnp.mean(grads, axis=-1, keepdims=True)
    along = jnp.mean(grads * normed, axis=-1, keepdims=True)
    return scale * (grads - shift - normed * along)


def along(own):
    return lax.all_gather(own, "z", axis=0, tiled=True)


def summed_along(parts):
    return lax.psum_scatter(parts.astype(BF16), "z", scatter_dimension=0, tiled=True)


def after(value, *others):
    return lax.optimization_barrier((value, *others))[0]


class Plane:
    def __init__(self):
        self.rows = lax.axis_size("x")
        self.blocks = lax.axis_size("k")
        self.size = self.rows * self.blocks
        self.fast = self.rows == 2 and self.blocks == 4
        if self.fast:
            self.order = lax.axis_index("k") ^ jnp.arange(4, dtype=jnp.int32)
        else:
            self.order = jnp.arange(self.blocks, dtype=jnp.int32)

    def swap(self, v, mask):
        return lax.ppermute(v, TP, [(j, j ^ mask) for j in range(self.size)])

    def lengths(self, own):
        if self.fast:
            return jnp.stack([own, self.swap(own, 4)])
        return lax.all_gather(own, "x", axis=0, tiled=False)

    def gather(self, own):
        if not self.fast:
            return lax.all_gather(own, TP, axis=0, tiled=True)
        held = {0: own}
        for mask in (6, 4, 2):
            held[mask] = self.swap(own, mask)
        for mask in (0, 4, 2, 6):
            held[mask ^ 1] = self.swap(held[mask], 1)
        return jnp.concatenate([held[m] for m in range(8)], axis=0)

    def scatter(self, product, left, *fill):
        if not self.fast:
            return lax.psum_scatter(
                product(left).astype(BF16), TP, scatter_dimension=0, tiled=True
            ).astype(F32)
        paired = left.reshape(4, 2, left.shape[0] // 8, left.shape[1])
        away = product(paired[:, 1].reshape(-1, left.shape[1])).astype(BF16)
        come = self.swap(away, 1)
        kept = product(paired[:, 0].reshape(-1, left.shape[1])) + come.astype(F32)
        kept = kept.reshape(4, left.shape[0] // 8, -1)
        total = after(kept[0], *fill) if fill else kept[0]
        for i in (3, 2, 1):
            total = total + self.swap(kept[i].astype(BF16), 2 * i).astype(F32)
        return total

    def out_moves(self, turn):
        return [(4 * x + k, 2 * (k ^ turn) + x) for x in range(2) for k in range(4)]

    def out_in(self, own):
        nz = lax.axis_size("z")
        if not (self.fast and nz == 4):
            pairs = [(j * nz + i, i * self.size + j) for i in range(nz) for j in range(self.size)]
            return along(lax.ppermute(own, ALL, pairs))
        whole = along(own)
        rows = own.shape[0]
        k, pair = lax.axis_index("k"), lax.axis_index(TP) // 2
        got = jnp.zeros_like(whole)
        for turn in range(4):
            part = lax.dynamic_slice_in_dim(whole, (k ^ turn) * rows, rows, 0)
            part = lax.ppermute(part, TP, self.out_moves(turn))
            got = lax.dynamic_update_slice_in_dim(got, part, (pair ^ turn) * rows, 0)
        return got

    def out_back(self, parts):
        nz = lax.axis_size("z")
        if not (self.fast and nz == 4):
            pairs = [(i * self.size + j, j * nz + i) for i in range(nz) for j in range(self.size)]
            return lax.ppermute(summed_along(parts), ALL, pairs)
        rows = parts.shape[0] // 4
        k, pair = lax.axis_index("k"), lax.axis_index(TP) // 2
        got = jnp.zeros_like(parts)
        for turn in range(4):
            part = lax.dynamic_slice_in_dim(parts, (pair ^ turn) * rows, rows, 0)
            part = lax.ppermute(part, TP, [(b, a) for a, b in self.out_moves(turn)])
            got = lax.dynamic_update_slice_in_dim(got, part, (k ^ turn) * rows, 0)
        return summed_along(got)

    def exchange(self, v):
        return lax.all_to_all(v, TP, 0, 0, tiled=True)


def rotate(values, cosine, sine):
    half = values.shape[-1] // 2
    front = values[..., :half]
    back = values[..., half:]
    return jnp.concatenate([front * cosine - back * sine, back * cosine + front * sine], axis=-1)


def unrotate(grads, cosine, sine):
    half = grads.shape[-1] // 2
    front = grads[..., :half]
    back = grads[..., half:]
    return jnp.concatenate([front * cosine + back * sine, back * cosine - front * sine], axis=-1)


def shards(
    tokens,
    lengths,
    ln1_gain,
    w_query,
    w_key,
    w_value,
    w_gate,
    w_out,
    ln2_gain,
    w_up,
    w_down,
    cotangent,
):
    plane = Plane()
    nz, np_ = lax.axis_size("z"), plane.size
    head = lax.axis_index(TP)
    nrow = plane.rows
    tok = tokens[0]
    tlen, dim = tok.shape
    row_len = tlen * plane.blocks
    width = w_query.shape[0]
    units = w_down.shape[0]

    gain_one = ln1_gain.astype(F32)[:, None]
    gain_two = ln2_gain.astype(F32)[:, None]

    def by_head(w):
        scaled = (w.astype(F32) * gain_one).astype(BF16)
        return scaled.reshape(width, np_, -1).transpose(1, 0, 2)

    up_scaled = (w_up.astype(F32) * gain_two).astype(BF16)
    up_send = up_scaled.reshape(width, nz, np_, units).transpose(2, 0, 1, 3).reshape(np_, width, -1)
    sent = [by_head(w) for w in (w_query, w_key, w_value, w_gate)] + [up_send]
    got = plane.exchange(jnp.concatenate(sent, axis=2)).reshape(np_ * width, -1)
    cut = 2 * HK + HV
    w_o = plane.out_in(w_out)
    w_qkv = along(got[:, :cut])
    w_g = along(got[:, cut : cut + HV])
    w_u = along(got[:, cut + HV :])
    w_d = along(after(w_down, w_g))

    loc = jnp.arange(tlen, dtype=jnp.int32)
    pos = (plane.order[:, None] * tlen + loc[None, :]).reshape(-1)
    lens = plane.lengths(lengths[0])
    cut, seg = 0, 0
    for i in range(3):
        cut = cut + lens[:, i : i + 1]
        seg = seg + (pos[None, :] >= cut).astype(jnp.int32)
    valid = seg < 3
    rate = DECAY_SCALE * jnp.exp2(-head.astype(F32)) / row_len
    gap = (pos[:, None] - pos[None, :]).astype(F32)
    allowed = (seg[:, :, None] == seg[:, None, :]) & (gap >= 0)[None] & valid[:, :, None] & valid[:, None, :]
    decay = jnp.where(allowed, jnp.exp(-rate * jnp.maximum(gap, 0.0))[None], 0.0)
    half = HK // 2
    freq = jnp.exp(-math.log(ROPE_BASE) * (jnp.arange(half, dtype=F32) / (half - 1)))
    angle = pos.astype(F32)[:, None] * freq[None, :]
    cosine, sine = jnp.cos(angle)[None], jnp.sin(angle)[None]
    key_norm = 1.0 / math.sqrt(HK)

    xf = tok.astype(F32)
    hat1, scale1 = normed_rows(xf)
    h1 = plane.gather(hat1.astype(BF16))
    dy = plane.gather(after(cotangent[0], h1, got))
    heads = dot(after(h1, dy), w_qkv)
    qk = heads[:, : 2 * HK].reshape(nrow, row_len, 2 * HK)
    queries = rotate(qk[..., :HK], cosine, sine).astype(BF16)
    keys = (rotate(qk[..., HK:], cosine, sine) * key_norm).astype(BF16)
    values = heads[:, 2 * HK :].astype(BF16).reshape(nrow, row_len, HV)
    scores = jnp.einsum("rnd,rmd->rnm", queries, keys, preferred_element_type=F32)
    weights = (scores * decay).astype(BF16)
    mixed = jnp.einsum("rnm,rme->rne", weights, values, preferred_element_type=F32)
    gate = dot(h1, w_g)
    gated, gate_back = jax.vjp(group_gate, mixed.reshape(-1, HV), gate)
    gated = gated.astype(BF16)
    x2 = xf + plane.scatter(lambda a: dot(a, w_o), gated)

    hat2, scale2 = normed_rows(x2)
    h2 = plane.gather(hat2.astype(BF16))
    hidden, act_back = jax.vjp(gelu_exact, dot(h2, w_u))
    act = hidden.astype(BF16)

    down_parts = dot_tn(act, dy).astype(BF16)
    down_rows = summed_along(down_parts)
    d_hidden = act_back(dot_nt(dy, w_d))[0].astype(BF16)
    d_hidden = after(d_hidden, down_parts)
    up_parts = dot_tn(h2, d_hidden).astype(BF16)
    t2 = plane.scatter(lambda a: dot_nt(a, w_u), d_hidden, up_parts)
    up_rows = summed_along(up_parts)
    d_x2 = cotangent[0].astype(F32) + norm_back(t2, hat2, scale2)
    d_branch = plane.gather(after(d_x2.astype(BF16), down_rows))

    d_mixed, d_gate = gate_back(dot_nt(d_branch, w_o))
    d_gate = d_gate.astype(BF16)
    out_rows = plane.out_back(dot_tn(gated, d_branch).astype(BF16))
    d_mixed = d_mixed.astype(BF16).reshape(nrow, row_len, HV)
    d_values = jnp.einsum("rnm,rne->rme", weights, d_mixed, preferred_element_type=F32)
    d_values = d_values.astype(BF16).reshape(-1, HV)
    d_scores = jnp.einsum("rne,rme->rnm", d_mixed, values, preferred_element_type=F32)
    d_scores = (d_scores * decay).astype(BF16)
    d_query = jnp.einsum("rnm,rmd->rnd", d_scores, keys, preferred_element_type=F32)
    d_key = jnp.einsum("rnm,rnd->rmd", d_scores, queries, preferred_element_type=F32)
    d_query = unrotate(d_query, cosine, sine).astype(BF16)
    d_key = (unrotate(d_key, cosine, sine) * key_norm).astype(BF16)
    d_qk = jnp.concatenate([d_query, d_key], axis=-1).reshape(-1, 2 * HK)
    d_vg = after(jnp.concatenate([d_values, d_gate], axis=1), up_rows)
    vg_rows = summed_along(dot_tn(h1, d_vg))
    qk_rows = summed_along(dot_tn(h1, d_qk))
    qkv_cut = 2 * HK + HV
    d_heads = jnp.concatenate([d_qk, d_vg], axis=1)
    u1 = plane.scatter(
        lambda a: dot_nt(a[:, :qkv_cut], w_qkv) + dot_nt(a[:, qkv_cut:], w_g), after(d_heads, out_rows)
    )
    tokens_grad = d_x2 + norm_back(u1, hat1, scale1)
    output = x2 + plane.scatter(lambda a: dot(a, w_d), after(act, tokens_grad))

    out_grad = out_rows.astype(F32)

    def by_rows(rows):
        return plane.exchange(rows.reshape(np_, width, -1)).astype(F32).transpose(1, 0, 2)

    up_sum = by_rows(up_rows).reshape(width, np_, nz, units).transpose(0, 2, 1, 3).reshape(width, -1)
    vg_sum = by_rows(vg_rows)
    v_sum = vg_sum[:, :, :HV].reshape(width, -1)
    g_sum = vg_sum[:, :, HV:].reshape(width, -1)
    qk_sum = by_rows(after(qk_rows, output))
    q_sum = qk_sum[:, :, :HK].reshape(width, -1)
    k_sum = qk_sum[:, :, HK:].reshape(width, -1)

    def gain_sum(pairs):
        return sum(jnp.sum(w.astype(F32) * g, axis=1) for w, g in pairs)

    gain1_grad = gain_sum([(w_query, q_sum), (w_key, k_sum), (w_value, v_sum), (w_gate, g_sum)])
    gain2_grad = gain_sum([(w_up, up_sum)])
    return (
        output.astype(BF16)[None],
        tokens_grad[None],
        gain1_grad,
        q_sum * gain_one,
        k_sum * gain_one,
        v_sum * gain_one,
        g_sum * gain_one,
        out_grad,
        gain2_grad,
        up_sum * gain_two,
        down_rows.astype(F32),
    )


def solution(mesh):
    batch, blocks = mesh.shape["batch"], mesh.shape["blk"]
    rows = HEADS // blocks
    split = Mesh(mesh.devices.reshape(batch // rows, rows, blocks), ALL)
    by_token = P(("z", "x"), "k", None)
    by_row = P(ALL, None)
    by_one = P(ALL)
    return jax.shard_map(
        shards,
        mesh=split,
        in_specs=(
            by_token,
            P(("z", "x"), None),
            by_one,
            by_row,
            by_row,
            by_row,
            by_row,
            by_row,
            by_one,
            by_row,
            by_row,
            by_token,
        ),
        out_specs=(
            by_token,
            by_token,
            by_one,
            by_row,
            by_row,
            by_row,
            by_row,
            by_row,
            by_one,
            by_row,
            by_row,
        ),
        check_vma=False,
    )
```

time: 3110 us -> 611 us (0.20)
  waiting for transfers between devices: 2440 us -> 279 us
  matrix products: 256 us -> 100 us
  blocking collectives: 156 us -> 31 us
  starting transfers between devices: 134 us -> 58.9 us
    reduce_scatter x7 -> x5, waiting for transfers between devices: 1810 us -> 24.3 us  [summed_along(): lax.psum_scatter(parts.astype(BF16), 'z', scatter_dimension=0, tiled=True)]
    all_gather x7 -> x5, waiting for transfers between devices: 457 us -> 34.6 us  [along(): return lax.all_gather(own, 'z', axis=0, tiled=True)]
    unnamed x2 -> x0, blocking collectives: 156 us -> none
    dot_general x33 -> x26, matrix products: 256 us -> 100 us  [the longest x7 38.7 us: dot(): return jnp.dot(a, b, preferred_element_type=F32)]
    ppermute x6 -> x53, starting transfers between devices: 133 us -> 45.2 us  [the longest x45 30.1 us: swap(): return lax.ppermute(v, TP, [(j, j ^ mask) for j in range(self.size)])]
    dot_general x3 -> x0, local copies, waits for them, and re-layouts: 47.2 us -> none  [the longest x1 22.6 us: shards(): value = jnp.dot(h1r, w_v, preferred_element_type=single_float)]
    ppermute x6 -> x53, waiting for transfers between devices: 164 us -> 205 us  [the longest x45 173 us: swap(): return lax.ppermute(v, TP, [(j, j ^ mask) for j in range(self.size)])]
  transfers between devices with their start and end apart: 20 -> 66, of which waited for: 18 -> 39; matrix products, arithmetic and copies ran while one was open for 8% -> 29% of each run, Pallas kernels for 0% -> 0%
where the time goes in v1:
time: 611 us; the launch traced here: 603 us
  waiting for transfers between devices  279 us (46%)
  matrix products  100 us (16%)
  local copies, waits for them, and re-layouts  75.9 us (12%)
  starting transfers between devices  58.9 us (10%)
  other arithmetic  43 us (7%)
  blocking collectives  31 us (5%)
  between operations  15.6 us (3%)
    ppermute x45, waiting for transfers between devices, swap(): return lax.ppermute(v, TP, [(j, j ^ mask) for j in range(self.size)])  173 us
    unnamed x149, local copies, waits for them, and re-layouts  41.9 us
    dot_general x7, matrix products, dot(): return jnp.dot(a, b, preferred_element_type=F32)  38.7 us
    all_gather x5, waiting for transfers between devices, along(): return lax.all_gather(own, 'z', axis=0, tiled=True)  34.6 us
    dot_general x8, matrix products, dot_nt(): lax.dot_general(a, b, (((1,), (1,)), ((), ())), preferred_element_type=F32)  32.8 us
    all_to_all x1, blocking collectives, exchange(): return lax.all_to_all(v, TP, 0, 0, tiled=True)  31 us
    ppermute x45, starting transfers between devices, swap(): return lax.ppermute(v, TP, [(j, j ^ mask) for j in range(self.size)])  30.1 us
    reduce_scatter x5, waiting for transfers between devices, summed_along(): lax.psum_scatter(parts.astype(BF16), 'z', scatter_dimension=0, tiled=True)  24.3 us
  transfers between devices with their start and end apart: 66, of which 39 were waited for; matrix products, arithmetic and copies ran while one was open for 29% of the time, Pallas kernels for 0%

profile of v1, /device:TPU:0, one launch (start us, length us, event | category | flops | bytes accessed | tf_op | source)
XLA Modules:
  0.0 603.4 jit_solution(5196615404032140812)
XLA Ops:
  14.2 31.0 %all_to_all.20 = bf16[8,64,2048]{2,1,0:T(8,128)(2,1)S(1)} all-to-all(bf16[8,64,2048]{2,1,0:T(8,128)(2,1)S(1)} %copy.46), channel_id=1, replica_groups=mesh['z'=4,'x'=2,'k'=4] {'x','k'}, dimensions={0} | all-to-all | bytes 4194304 | tf_op jit(solution)/shard_map/all_to_all | solution.py:146
  56.1 6.5 %collective-permute-done.1 = bf16[128,2048]{1,0:T(8,128)(2,1)S(1)} collective-permute-done((bf16[128,2048]{1,0:T(8,128)(2,1)}, bf16[128,2048]{1,0:T(8,128)(2,1)S(1)}, u32[]{:S(2)}, u32[]{:S(2)}) %collective-permute-start.1) | collective-permute-done | bytes 524320 | tf_op jit(solution)/shard_map/ppermute | solution.py:81
  62.5 12.4 %collective-permute-done.14 = s32[4]{0:T(128)S(1)} collective-permute-done((s32[4]{0:T(128)S(1)}, s32[4]{0:T(128)S(1)}, u32[]{:S(2)}, u32[]{:S(2)}) %collective-permute-start.14) | collective-permute-done | bytes 48 | tf_op jit(solution)/shard_map/ppermute | solution.py:81
  89.6 9.0 %collective-permute-done.8 = bf16[128,2048]{1,0:T(8,128)(2,1)} collective-permute-done((bf16[128,2048]{1,0:T(8,128)(2,1)S(1)}, bf16[128,2048]{1,0:T(8,128)(2,1)}, u32[]{:S(2)}, u32[]{:S(2)}) %collective-permute-start.8) | collective-permute-done | bytes 524320 | tf_op jit(solution)/shard_map/ppermute | solution.py:81
  100.4 11.7 %collective-permute-done.12 = bf16[128,2048]{1,0:T(8,128)(2,1)} collective-permute-done((bf16[128,2048]{1,0:T(8,128)(2,1)S(1)}, bf16[128,2048]{1,0:T(8,128)(2,1)}, u32[]{:S(2)}, u32[]{:S(2)}) %collective-permute-start.12) | collective-permute-done | bytes 524320 | tf_op jit(solution)/shard_map/ppermute | solution.py:81
  133.5 10.6 %collective-permute-done.16 = bf16[128,2048]{1,0:T(8,128)(2,1)S(1)} collective-permute-done((bf16[128,2048]{1,0:T(8,128)(2,1)S(1)}, bf16[128,2048]{1,0:T(8,128)(2,1)S(1)}, u32[]{:S(2)}, u32[]{:S(2)}) %collective-permute-start.16) | collective-permute-done | bytes 524320 | tf_op jit(solution)/shard_map/ppermute | solution.py:127
  152.1 7.5 %fusion.97 = f32[1024,1024]{1,0:T(8,128)S(1)} fusion(bf16[1024,2048]{1,0:T(8,128)(2,1)} %constant_dynamic-update-slice_fusion, bf16[2048,1024]{1,0:T(8,128)(2,1)} %all-gather.6.cloned.1.call-done), kind=kOutput, calls=%fused_computation.253 | convolution fusion | flops 4294967296 | bytes 12582912 | tf_op jit(solution)/shard_map/dot_general | solution.py:23
  164.6 22.0 %all-gather.8.cloned.1.call-done = bf16[2048,512]{1,0:T(8,128)(2,1)} async-done(((bf16[512,512]{1,0:T(8,128)(2,1)}), bf16[2048,512]{1,0:T(8,128)(2,1)}) %all-gather.8.cloned.1.call-update) | async-done | bytes 2097168 | tf_op jit(solution)/shard_map/all_gather | solution.py:58
  186.6 6.8 %multiply_convert_fusion.1 = (bf16[1024,512]{1,0:T(8,128)(2,1)S(1)}, f32[1024,512]{1,0:T(8,128)}) fusion(f32[2,512,512]{2,1,0:T(8,128)S(1)} %get-tuple-element.128, f32[1024]{0:T(1024)S(1)} %rsqrt.27, f32[1024]{0:T(1024)S(1)} %bitcast.229, bf16[1024,2048]{1,0:T(8,128)(2,1)} %constant_dynamic-update-slice_fusion, ...), kind=kOutput, calls=%fused_computation.45 | convolution fusion | flops 2151677952 | bytes 11542528 | tf_op jit(solution)/shard_map/dot_general | solution.py:23
  213.1 12.2 %collective-permute-done.20 = bf16[128,2048]{1,0:T(8,128)(2,1)S(1)} collective-permute-done((bf16[128,2048]{1,0:T(8,128)(2,1)}, bf16[128,2048]{1,0:T(8,128)(2,1)S(1)}, u32[]{:S(2)}, u32[]{:S(2)}) %collective-permute-start.20) | collective-permute-done | bytes 524320 | tf_op jit(solution)/shard_map/ppermute | solution.py:81
  225.3 10.3 %collective-permute-done.21 = bf16[128,2048]{1,0:T(8,128)(2,1)S(1)} collective-permute-done((bf16[128,2048]{1,0:T(8,128)(2,1)}, bf16[128,2048]{1,0:T(8,128)(2,1)S(1)}, u32[]{:S(2)}, u32[]{:S(2)}) %collective-permute-start.21) | collective-permute-done | bytes 524320 | tf_op jit(solution)/shard_map/ppermute | solution.py:81
  243.5 10.5 %collective-permute-done.24 = bf16[128,2048]{1,0:T(8,128)(2,1)S(1)} collective-permute-done((bf16[128,2048]{1,0:T(8,128)(2,1)S(1)}, bf16[128,2048]{1,0:T(8,128)(2,1)S(1)}, u32[]{:S(2)}, u32[]{:S(2)}) %collective-permute-start.24) | collective-permute-done | bytes 524320 | tf_op jit(solution)/shard_map/ppermute | solution.py:81
  257.2 8.4 %collective-permute-done.28 = bf16[128,2048]{1,0:T(8,128)(2,1)S(1)} collective-permute-done((bf16[128,2048]{1,0:T(8,128)(2,1)S(1)}, bf16[128,2048]{1,0:T(8,128)(2,1)S(1)}, u32[]{:S(2)}, u32[]{:S(2)}) %collective-permute-start.28) | collective-permute-done | bytes 524320 | tf_op jit(solution)/shard_map/ppermute | solution.py:81
  269.8 6.5 %fusion.98 = f32[1024,512]{1,0:T(8,128)} fusion(bf16[1024,2048]{1,0:T(8,128)(2,1)} %constant_dynamic-update-slice_fusion.16, bf16[2048,512]{1,0:T(8,128)(2,1)} %all-gather.12.cloned.1.call-done), kind=kOutput, calls=%fused_computation.254 | convolution fusion | flops 2147483648 | bytes 8388608 | tf_op jit(solution)/shard_map/dot_general | solution.py:23
  276.4 12.6 %all-gather.14.cloned.1.call-done = bf16[512,2048]{1,0:T(8,128)(2,1)} async-done(((bf16[128,2048]{1,0:T(8,128)(2,1)}), bf16[512,2048]{1,0:T(8,128)(2,1)}) %all-gather.14.cloned.1.call-update) | async-done | bytes 2097168 | tf_op jit(solution)/shard_map/all_gather | solution.py:58
  289.0 10.5 %add_convert_fusion.2 = (bf16[1024,512]{1,0:T(8,128)(2,1)}, f32[1024,512]{1,0:T(8,128)S(1)}) fusion(f32[1024,512]{1,0:T(8,128)} %fusion.98, bf16[1024,2048]{1,0:T(8,128)(2,1)} %constant_dynamic-update-slice_fusion.8, bf16[512,2048]{1,0:T(8,128)(2,1)} %all-gather.14.cloned.1.call-done), kind=kOutput, calls=%fused_computation.31 | convolution fusion | flops 2185232384 | bytes 11534336 | tf_op jit(solution)/shard_map/dot_general | solution.py:27
  315.1 5.9 fusion.78
  325.7 5.9 convolution_convert_fusion.3
  338.2 10.6 %collective-permute-done.32 = bf16[128,2048]{1,0:T(8,128)(2,1)} collective-permute-done((bf16[128,2048]{1,0:T(8,128)(2,1)}, bf16[128,2048]{1,0:T(8,128)(2,1)}, u32[]{:S(2)}, u32[]{:S(2)}) %collective-permute-start.32) | collective-permute-done | bytes 524320 | tf_op jit(solution)/shard_map/ppermute | solution.py:81
  357.1 10.6 %collective-permute-done.35 = bf16[128,2048]{1,0:T(8,128)(2,1)} collective-permute-done((bf16[128,2048]{1,0:T(8,128)(2,1)}, bf16[128,2048]{1,0:T(8,128)(2,1)}, u32[]{:S(2)}, u32[]{:S(2)}) %collective-permute-start.35) | collective-permute-done | bytes 524320 | tf_op jit(solution)/shard_map/ppermute | solution.py:81
  372.3 7.3 %collective-permute-done.39 = bf16[128,2048]{1,0:T(8,128)(2,1)S(1)} collective-permute-done((bf16[128,2048]{1,0:T(8,128)(2,1)}, bf16[128,2048]{1,0:T(8,128)(2,1)S(1)}, u32[]{:S(2)}, u32[]{:S(2)}) %collective-permute-start.39) | collective-permute-done | bytes 524320 | tf_op jit(solution)/shard_map/ppermute | solution.py:81
  394.7 6.0 collective-permute-done.42
  401.5 6.0 collective-permute-done.43
  413.9 6.4 %multiply_reduce_fusion = (f32[1024]{0:T(1024)S(1)}, f32[1024,512]{1,0:T(8,128)S(1)}) fusion(f32[2,512,512]{2,1,0:T(8,128)S(1)} %get-tuple-element.128, f32[1024]{0:T(1024)S(1)} %bitcast.230, f32[1024,512]{1,0:T(8,128)} %get-tuple-element.130, bf16[1024,2048]{1,0:T(8,128)(2,1)} %copy-done.46, bf16[512,2048]{1,0:T(8,128)(2,1)} %constant_dynamic-update-slice_fusion.36), kind=kOutput, calls=%fused_computation.30 | convolution fusion | flops 2151676928 | bytes 12591104 | tf_op jit(solution)/shard_map/dot_general | solution.py:27
  432.6 6.3 %convolution_convert_fusion = bf16[2048,1024]{1,0:T(8,128)(2,1)} fusion(bf16[1024,2048]{1,0:T(8,128)(2,1)S(1)} %copy-done.47, bf16[1024,1024]{1,0:T(8,128)(2,1)S(1)} %pad_maximum_fusion.1), kind=kOutput, calls=%fused_computation.5 | convolution fusion | flops 4297064448 | bytes 10485760 | tf_op jit(solution)/shard_map/dot_general | solution.py:31
  443.9 11.9 %reduce-scatter.10.cloned.1.call-done = bf16[128,2048]{1,0:T(8,128)(2,1)} async-done(((bf16[512,2048]{1,0:T(8,128)(2,1)}), bf16[128,2048]{1,0:T(8,128)(2,1)}) %reduce-scatter.10.cloned.1.call-update) | async-done | bytes 524304 | tf_op jit(solution)/shard_map/reduce_scatter | solution.py:62
  471.9 12.2 %collective-permute-done.46 = bf16[128,2048]{1,0:T(8,128)(2,1)S(1)} collective-permute-done((bf16[128,2048]{1,0:T(8,128)(2,1)S(1)}, bf16[128,2048]{1,0:T(8,128)(2,1)S(1)}, u32[]{:S(2)}, u32[]{:S(2)}) %collective-permute-start.46) | collective-permute-done | bytes 524320 | tf_op jit(solution)/shard_map/ppermute | solution.py:81
  484.2 10.5 %collective-permute-done.47 = bf16[128,2048]{1,0:T(8,128)(2,1)S(1)} collective-permute-done((bf16[128,2048]{1,0:T(8,128)(2,1)S(1)}, bf16[128,2048]{1,0:T(8,128)(2,1)S(1)}, u32[]{:S(2)}, u32[]{:S(2)}) %collective-permute-start.47) | collective-permute-done | bytes 524320 | tf_op jit(solution)/shard_map/ppermute | solution.py:81
  511.3 6.7 %all-to-all-done.3 = bf16[8,64,512]{2,1,0:T(8,128)(2,1)} async-done(((bf16[8,64,512]{2,1,0:T(8,128)(2,1)}), bf16[8,64,512]{2,1,0:T(8,128)(2,1)}, u32[]{:S(2)}, u32[]{:S(2)}) %all-to-all-start.3) | async-done | bytes 524320 | tf_op jit(solution)/shard_map/all_to_all | solution.py:146
  525.6 8.8 %reduce-scatter.14.cloned.1.call-done = bf16[512,1024]{1,0:T(8,128)(2,1)} async-done(((bf16[2048,1024]{1,0:T(8,128)(2,1)}), bf16[512,1024]{1,0:T(8,128)(2,1)}) %reduce-scatter.14.cloned.1.call-update) | async-done | bytes 1048592 | tf_op jit(solution)/shard_map/reduce_scatter | solution.py:62
  555.0 10.7 %collective-permute-done.50 = bf16[128,2048]{1,0:T(8,128)(2,1)} collective-permute-done((bf16[128,2048]{1,0:T(8,128)(2,1)}, bf16[128,2048]{1,0:T(8,128)(2,1)}, u32[]{:S(2)}, u32[]{:S(2)}) %collective-permute-start.50) | collective-permute-done | bytes 524320 | tf_op jit(solution)/shard_map/ppermute | solution.py:81
  565.7 9.9 %collective-permute-done.51 = bf16[128,2048]{1,0:T(8,128)(2,1)} collective-permute-done((bf16[128,2048]{1,0:T(8,128)(2,1)}, bf16[128,2048]{1,0:T(8,128)(2,1)}, u32[]{:S(2)}, u32[]{:S(2)}) %collective-permute-start.51) | collective-permute-done | bytes 524320 | tf_op jit(solution)/shard_map/ppermute | solution.py:81
  (378 shorter events, 263.9 us)
Async XLA Ops:
  7.2 111.4 %all-gather.10.cloned.1.call-start = ((), (), s32[]{:S(2)}) async-start(), calls=%async_computation.11 | async-start | bytes 2621440 | tf_op jit(solution)/shard_map/all_gather | solution.py:58
  7.9 144.2 %all-gather.6.cloned.1.call-start = ((), (), s32[]{:S(2)}) async-start(), calls=%async_computation.9 | async-start | bytes 5242880 | tf_op jit(solution)/shard_map/all_gather | solution.py:58
  46.3 140.3 %all-gather.8.cloned.1.call-start = ((), (), s32[]{:S(2)}) async-start(), calls=%async_computation.10 | async-start | bytes 2621440 | tf_op jit(solution)/shard_map/all_gather | solution.py:58
  48.0 27.1 %collective-permute-start = (bf16[128,2048]{1,0:T(8,128)(2,1)}, bf16[128,2048]{1,0:T(8,128)(2,1)}, u32[]{:S(2)}, u32[]{:S(2)}) collective-permute-start(bf16[128,2048]{1,0:T(8,128)(2,1)} %get-tuple-element.55), channel_id=1, source_target_pairs={{0,1},{1,0},{2,3},{3,2},{4,5},{5,4},{6,7},{7,6},{8,9},{9,8},{10,11... | collective-permute-start | bytes 1572872 | tf_op jit(solution)/shard_map/ppermute | solution.py:81
  49.5 25.5 %collective-permute-start.3 = (bf16[128,2048]{1,0:T(8,128)(2,1)}, bf16[128,2048]{1,0:T(8,128)(2,1)}, u32[]{:S(2)}, u32[]{:S(2)}) collective-permute-start(bf16[128,2048]{1,0:T(8,128)(2,1)} %get-tuple-element.55), channel_id=1, source_target_pairs={{0,4},{1,5},{2,6},{3,7},{4,0},{5,1},{6,2},{7,3},{8,12},{9,13},{10,... | collective-permute-start | bytes 1572872 | tf_op jit(solution)/shard_map/ppermute | solution.py:81
  50.1 27.7 %collective-permute-start.5 = (bf16[128,2048]{1,0:T(8,128)(2,1)}, bf16[128,2048]{1,0:T(8,128)(2,1)}, u32[]{:S(2)}, u32[]{:S(2)}) collective-permute-start(bf16[128,2048]{1,0:T(8,128)(2,1)} %get-tuple-element.55), channel_id=1, source_target_pairs={{0,6},{1,7},{2,4},{3,5},{4,2},{5,3},{6,0},{7,1},{8,14},{9,15},{10,... | collective-permute-start | bytes 1572872 | tf_op jit(solution)/shard_map/ppermute | solution.py:81
  51.5 23.5 %collective-permute-start.14 = (s32[4]{0:T(128)S(1)}, s32[4]{0:T(128)S(1)}, u32[]{:S(2)}, u32[]{:S(2)}) collective-permute-start(s32[4]{0:T(128)S(1)} %bitcast.232), channel_id=1, source_target_pairs={{0,4},{1,5},{2,6},{3,7},{4,0},{5,1},{6,2},{7,3},{8,12},{9,13},{10,... | collective-permute-start | bytes 56 | tf_op jit(solution)/shard_map/ppermute | solution.py:81
  85.4 26.7 %collective-permute-start.7 = (bf16[128,2048]{1,0:T(8,128)(2,1)S(1)}, bf16[128,2048]{1,0:T(8,128)(2,1)}, u32[]{:S(2)}, u32[]{:S(2)}) collective-permute-start(bf16[128,2048]{1,0:T(8,128)(2,1)S(1)} %bitcast.204), channel_id=1, source_target_pairs={{0,1},{1,0},{2,3},{3,2},{4,5},{5,4},{6,7},{7,6},{8,9},{9,8},{10,11... | collective-permute-start | bytes 1572872 | tf_op jit(solution)/shard_map/ppermute | solution.py:81
  86.7 25.4 %collective-permute-start.12 = (bf16[128,2048]{1,0:T(8,128)(2,1)S(1)}, bf16[128,2048]{1,0:T(8,128)(2,1)}, u32[]{:S(2)}, u32[]{:S(2)}) collective-permute-start(bf16[128,2048]{1,0:T(8,128)(2,1)S(1)} %bitcast.206), channel_id=1, source_target_pairs={{0,6},{1,7},{2,4},{3,5},{4,2},{5,3},{6,0},{7,1},{8,14},{9,15},{10,... | collective-permute-start | bytes 1572872 | tf_op jit(solution)/shard_map/ppermute | solution.py:81
  99.5 170.4 %all-gather.12.cloned.1.call-start = ((), (), s32[]{:S(2)}) async-start(), calls=%async_computation.12 | async-start | bytes 2621440 | tf_op jit(solution)/shard_map/all_gather | solution.py:58
  121.9 22.2 %collective-permute-start.16 = (bf16[128,2048]{1,0:T(8,128)(2,1)S(1)}, bf16[128,2048]{1,0:T(8,128)(2,1)S(1)}, u32[]{:S(2)}, u32[]{:S(2)}) collective-permute-start(bf16[128,2048]{1,0:T(8,128)(2,1)S(1)} %get-tuple-element.87), channel_id=1, source_target_pairs={{0,2},{1,0},{2,6},{3,4},{4,3},{5,1},{6,7},{7,5},{8,10},{9,8},{10,1... | collective-permute-start | bytes 1572872 | tf_op jit(solution)/shard_map/ppermute | solution.py:127
  127.0 21.1 %collective-permute-start.17 = (bf16[128,2048]{1,0:T(8,128)(2,1)S(1)}, bf16[128,2048]{1,0:T(8,128)(2,1)S(1)}, u32[]{:S(2)}, u32[]{:S(2)}) collective-permute-start(bf16[128,2048]{1,0:T(8,128)(2,1)S(1)} %get-tuple-element.86), channel_id=1, source_target_pairs={{0,4},{1,6},{2,0},{3,2},{4,5},{5,7},{6,1},{7,3},{8,12},{9,14},{10,... | collective-permute-start | bytes 1572872 | tf_op jit(solution)/shard_map/ppermute | solution.py:127
  128.7 22.5 %collective-permute-start.18 = (bf16[128,2048]{1,0:T(8,128)(2,1)S(1)}, bf16[128,2048]{1,0:T(8,128)(2,1)S(1)}, u32[]{:S(2)}, u32[]{:S(2)}) collective-permute-start(bf16[128,2048]{1,0:T(8,128)(2,1)S(1)} %get-tuple-element.85), channel_id=1, source_target_pairs={{0,6},{1,4},{2,2},{3,0},{4,7},{5,5},{6,3},{7,1},{8,14},{9,12},{10,... | collective-permute-start | bytes 1572872 | tf_op jit(solution)/shard_map/ppermute | solution.py:127
  197.9 91.1 %all-gather.14.cloned.1.call-start = ((), (), s32[]{:S(2)}) async-start(), calls=%async_computation.13 | async-start | bytes 2621440 | tf_op jit(solution)/shard_map/all_gather | solution.py:58
  211.6 24.0 %collective-permute-start.21 = (bf16[128,2048]{1,0:T(8,128)(2,1)}, bf16[128,2048]{1,0:T(8,128)(2,1)S(1)}, u32[]{:S(2)}, u32[]{:S(2)}) collective-permute-start(bf16[128,2048]{1,0:T(8,128)(2,1)} %get-tuple-element.84), channel_id=1, source_target_pairs={{0,4},{1,5},{2,6},{3,7},{4,0},{5,1},{6,2},{7,3},{8,12},{9,13},{10,... | collective-permute-start | bytes 1572872 | tf_op jit(solution)/shard_map/ppermute | solution.py:81
  212.2 23.5 %collective-permute-start.22 = (bf16[128,2048]{1,0:T(8,128)(2,1)}, bf16[128,2048]{1,0:T(8,128)(2,1)}, u32[]{:S(2)}, u32[]{:S(2)}) collective-permute-start(bf16[128,2048]{1,0:T(8,128)(2,1)} %get-tuple-element.83), channel_id=1, source_target_pairs={{0,2},{1,3},{2,0},{3,1},{4,6},{5,7},{6,4},{7,5},{8,10},{9,11},{10,... | collective-permute-start | bytes 1572872 | tf_op jit(solution)/shard_map/ppermute | solution.py:81
  212.8 140.7 %reduce-scatter.6.cloned.1.call-start = ((), (), s32[]{:S(2)}) async-start(), calls=%async_computation.14 | async-start | bytes 2621440 | tf_op jit(solution)/shard_map/reduce_scatter | solution.py:62
  242.2 23.5 %collective-permute-start.28 = (bf16[128,2048]{1,0:T(8,128)(2,1)S(1)}, bf16[128,2048]{1,0:T(8,128)(2,1)S(1)}, u32[]{:S(2)}, u32[]{:S(2)}) collective-permute-start(bf16[128,2048]{1,0:T(8,128)(2,1)S(1)} %get-tuple-element.51), channel_id=1, source_target_pairs={{0,6},{1,7},{2,4},{3,5},{4,2},{5,3},{6,0},{7,1},{8,14},{9,15},{10,... | collective-permute-start | bytes 1572872 | tf_op jit(solution)/shard_map/ppermute | solution.py:81
  310.6 114.1 %reduce-scatter.8.cloned.1.call-start = ((), (), s32[]{:S(2)}) async-start(), calls=%async_computation.15 | async-start | bytes 2621440 | tf_op jit(solution)/shard_map/reduce_scatter | solution.py:62
  324.7 24.1 %collective-permute-start.32 = (bf16[128,2048]{1,0:T(8,128)(2,1)}, bf16[128,2048]{1,0:T(8,128)(2,1)}, u32[]{:S(2)}, u32[]{:S(2)}) collective-permute-start(bf16[128,2048]{1,0:T(8,128)(2,1)} %get-tuple-element.79), channel_id=1, source_target_pairs={{0,4},{1,5},{2,6},{3,7},{4,0},{5,1},{6,2},{7,3},{8,12},{9,13},{10,... | collective-permute-start | bytes 1572872 | tf_op jit(solution)/shard_map/ppermute | solution.py:81
  325.3 23.5 %collective-permute-start.33 = (bf16[128,2048]{1,0:T(8,128)(2,1)}, bf16[128,2048]{1,0:T(8,128)(2,1)}, u32[]{:S(2)}, u32[]{:S(2)}) collective-permute-start(bf16[128,2048]{1,0:T(8,128)(2,1)} %get-tuple-element.78), channel_id=1, source_target_pairs={{0,2},{1,3},{2,0},{3,1},{4,6},{5,7},{6,4},{7,5},{8,10},{9,11},{10,... | collective-permute-start | bytes 1572872 | tf_op jit(solution)/shard_map/ppermute | solution.py:81
  356.5 99.3 %reduce-scatter.10.cloned.1.call-start = ((), (), s32[]{:S(2)}) async-start(), calls=%async_computation.16 | async-start | bytes 2621440 | tf_op jit(solution)/shard_map/reduce_scatter | solution.py:62
  356.5 23.1 %collective-permute-start.39 = (bf16[128,2048]{1,0:T(8,128)(2,1)}, bf16[128,2048]{1,0:T(8,128)(2,1)S(1)}, u32[]{:S(2)}, u32[]{:S(2)}) collective-permute-start(bf16[128,2048]{1,0:T(8,128)(2,1)} %get-tuple-element.26), channel_id=1, source_target_pairs={{0,6},{1,7},{2,4},{3,5},{4,2},{5,3},{6,0},{7,1},{8,14},{9,15},{10,... | collective-permute-start | bytes 1572872 | tf_op jit(solution)/shard_map/ppermute | solution.py:81
  388.0 24.8 %collective-permute-start.44 = (bf16[128,2048]{1,0:T(8,128)(2,1)S(1)}, bf16[128,2048]{1,0:T(8,128)(2,1)S(1)}, u32[]{:S(2)}, u32[]{:S(2)}) collective-permute-start(bf16[128,2048]{1,0:T(8,128)(2,1)S(1)} %get-tuple-element.73), channel_id=1, source_target_pairs={{6,0},{4,1},{2,2},{0,3},{7,4},{5,5},{3,6},{1,7},{14,8},{12,9},{10,... | collective-permute-start | bytes 1572872 | tf_op jit(solution)/shard_map/ppermute | solution.py:141
  413.7 120.7 %reduce-scatter.14.cloned.1.call-start = ((), (), s32[]{:S(2)}) async-start(), calls=%async_computation.18 | async-start | bytes 5242880 | tf_op jit(solution)/shard_map/reduce_scatter | solution.py:62
  438.9 141.9 %reduce-scatter.12.cloned.1.call-start = ((), (), s32[]{:S(2)}) async-start(), calls=%async_computation.17 | async-start | bytes 2621440 | tf_op jit(solution)/shard_map/reduce_scatter | solution.py:62
  470.8 23.8 %collective-permute-start.47 = (bf16[128,2048]{1,0:T(8,128)(2,1)S(1)}, bf16[128,2048]{1,0:T(8,128)(2,1)S(1)}, u32[]{:S(2)}, u32[]{:S(2)}) collective-permute-start(bf16[128,2048]{1,0:T(8,128)(2,1)S(1)} %get-tuple-element.72), channel_id=1, source_target_pairs={{0,4},{1,5},{2,6},{3,7},{4,0},{5,1},{6,2},{7,3},{8,12},{9,13},{10,... | collective-permute-start | bytes 1572872 | tf_op jit(solution)/shard_map/ppermute | solution.py:81
  471.4 23.2 %collective-permute-start.48 = (bf16[128,2048]{1,0:T(8,128)(2,1)S(1)}, bf16[128,2048]{1,0:T(8,128)(2,1)S(1)}, u32[]{:S(2)}, u32[]{:S(2)}) collective-permute-start(bf16[128,2048]{1,0:T(8,128)(2,1)S(1)} %get-tuple-element.71), channel_id=1, source_target_pairs={{0,2},{1,3},{2,0},{3,1},{4,6},{5,7},{6,4},{7,5},{8,10},{9,11},{10,... | collective-permute-start | bytes 1572872 | tf_op jit(solution)/shard_map/ppermute | solution.py:81
  500.7 37.8 %collective-permute-start.49 = (bf16[512,2048]{1,0:T(8,128)(2,1)}, bf16[512,2048]{1,0:T(8,128)(2,1)S(1)}, u32[]{:S(2)}, u32[]{:S(2)}) collective-permute-start(bf16[512,2048]{1,0:T(8,128)(2,1)} %convolution_convert_fusion.5), channel_id=1, source_target_pairs={{0,1},{1,0},{2,3},{3,2},{4,5},{5,4},{6,7},{7,6},{8,9},{9,8},{10,11... | collective-permute-start | bytes 6291464 | tf_op jit(solution)/shard_map/ppermute | solution.py:81
  544.8 20.9 %collective-permute-start.50 = (bf16[128,2048]{1,0:T(8,128)(2,1)}, bf16[128,2048]{1,0:T(8,128)(2,1)}, u32[]{:S(2)}, u32[]{:S(2)}) collective-permute-start(bf16[128,2048]{1,0:T(8,128)(2,1)} %get-tuple-element.67), channel_id=1, source_target_pairs={{0,6},{1,7},{2,4},{3,5},{4,2},{5,3},{6,0},{7,1},{8,14},{9,15},{10,... | collective-permute-start | bytes 1572872 | tf_op jit(solution)/shard_map/ppermute | solution.py:81
  547.6 27.9 %collective-permute-start.51 = (bf16[128,2048]{1,0:T(8,128)(2,1)}, bf16[128,2048]{1,0:T(8,128)(2,1)}, u32[]{:S(2)}, u32[]{:S(2)}) collective-permute-start(bf16[128,2048]{1,0:T(8,128)(2,1)} %get-tuple-element.69), channel_id=1, source_target_pairs={{0,4},{1,5},{2,6},{3,7},{4,0},{5,1},{6,2},{7,3},{8,12},{9,13},{10,... | collective-permute-start | bytes 1572872 | tf_op jit(solution)/shard_map/ppermute | solution.py:81
  548.2 27.4 %collective-permute-start.52 = (bf16[128,2048]{1,0:T(8,128)(2,1)}, bf16[128,2048]{1,0:T(8,128)(2,1)}, u32[]{:S(2)}, u32[]{:S(2)}) collective-permute-start(bf16[128,2048]{1,0:T(8,128)(2,1)} %get-tuple-element.68), channel_id=1, source_target_pairs={{0,2},{1,3},{2,0},{3,1},{4,6},{5,7},{6,4},{7,5},{8,10},{9,11},{10,... | collective-permute-start | bytes 1572872 | tf_op jit(solution)/shard_map/ppermute | solution.py:81
  (89 other events, 725.8 us)
Sparse Core Ops, SparseCore 0:
  9.6 48.6 all-gather.9
  60.4 79.4 all-gather.5
  142.1 44.4 all-gather.7
  198.0 44.7 all-gather.11
  244.3 44.6 all-gather.13
  310.7 42.7 reduce-scatter.5
  356.6 42.4 reduce-scatter.7
  413.8 41.9 reduce-scatter.9
  458.2 76.0 reduce-scatter.13
  536.5 44.3 reduce-scatter.11

commit v2 on v1

--- a/solution.py
+++ b/solution.py
@@ -31,15 +31,10 @@
     return lax.dot_general(a, b, (((0,), (0,)), ((), ())), preferred_element_type=F32)
 
 
-def group_gate(mixed, gate):
-    centered = mixed - jnp.mean(mixed, axis=-1, keepdims=True)
-    spread = jnp.mean(centered * centered, axis=-1, keepdims=True)
-    normed = centered * lax.rsqrt(spread + GN_EPS)
-    return normed * jax.nn.silu(gate)
-
-
-def gelu_exact(values):
-    return jax.nn.gelu(values, approximate=False)
+def gelu_and_slope(values):
+    below = 0.5 + 0.5 * lax.erf(values * math.sqrt(0.5))
+    density = jnp.exp(-0.5 * values * values) * (1.0 / math.sqrt(2.0 * math.pi))
+    return (values * below).astype(BF16), below + values * density
 
 
 def normed_rows(values):
@@ -60,6 +55,23 @@
 
 def summed_along(parts):
     return lax.psum_scatter(parts.astype(BF16), "z", scatter_dimension=0, tiled=True)
+
+
+def along_by_hops(own):
+    me = lax.axis_index("z")
+
+    def hop(v, *pairs):
+        return lax.ppermute(v, "z", pairs)
+
+    near = hop(own, (0, 1), (1, 0), (2, 3), (3, 2))
+    mid = hop(own, (1, 2), (2, 1))
+    far = hop(near, (1, 2), (2, 1))
+    out_mid = hop(mid, (1, 0), (2, 3))
+    out_far = hop(far, (1, 0), (2, 3))
+    inside = (me == 1) | (me == 2)
+    held = [own, near, jnp.where(inside, mid, out_mid), jnp.where(inside, far, out_far)]
+    places = jnp.array([[0, 1, 2, 3], [1, 0, 2, 3], [3, 2, 0, 1], [3, 2, 1, 0]], jnp.int32)
+    return jnp.concatenate(held, axis=0), lax.dynamic_index_in_dim(places, me, keepdims=False)
 
 
 def after(value, *others):
@@ -100,25 +112,55 @@
             return lax.psum_scatter(
                 product(left).astype(BF16), TP, scatter_dimension=0, tiled=True
             ).astype(F32)
-        paired = left.reshape(4, 2, left.shape[0] // 8, left.shape[1])
-        away = product(paired[:, 1].reshape(-1, left.shape[1])).astype(BF16)
-        come = self.swap(away, 1)
-        kept = product(paired[:, 0].reshape(-1, left.shape[1])) + come.astype(F32)
-        kept = kept.reshape(4, left.shape[0] // 8, -1)
-        total = after(kept[0], *fill) if fill else kept[0]
-        for i in (3, 2, 1):
-            total = total + self.swap(kept[i].astype(BF16), 2 * i).astype(F32)
+        rows = left.shape[0] // 8
+        blocks = [left[i * rows : (i + 1) * rows] for i in range(8)]
+        come = {}
+        for pair in ((6, 4), (2, 0)):
+            away = product(jnp.concatenate([blocks[m ^ 1] for m in pair], axis=0)).astype(BF16)
+            away = self.swap(away, 1)
+            for i, m in enumerate(pair):
+                come[m] = away[i * rows : (i + 1) * rows]
+        sent = [
+            self.swap((product(blocks[m]) + come[m].astype(F32)).astype(BF16), m) for m in (6, 4, 2)
+        ]
+        total = product(blocks[0]) + come[0].astype(F32)
+        total = after(total, *fill) if fill else total
+        for part in sent:
+            total = total + part.astype(F32)
         return total
+
+    def gather_parts(self, own):
+        if not self.fast:
+            whole = self.gather(own)
+            return [whole], whole
+        held = {0: own}
+        for mask in (6, 4, 2):
+            held[mask] = self.swap(own, mask)
+        for mask in (0, 4, 2, 6):
+            held[mask ^ 1] = self.swap(held[mask], 1)
+        parts = [jnp.concatenate([held[m], held[m + 1]], axis=0) for m in (0, 4, 2, 6)]
+        return parts, self.joined(parts)
+
+    def joined(self, parts):
+        if not self.fast:
+            return parts[0]
+        return jnp.concatenate([parts[i] for i in (0, 2, 1, 3)], axis=0)
+
+    def parts_of(self, *arrays):
+        if not self.fast:
+            return [arrays]
+        rows = arrays[0].shape[0] // 4
+        return [[a[i * rows : (i + 1) * rows] for a in arrays] for i in (0, 2, 1, 3)]
 
     def out_moves(self, turn):
         return [(4 * x + k, 2 * (k ^ turn) + x) for x in range(2) for k in range(4)]
 
-    def out_in(self, own):
+    def out_in(self, own, first):
         nz = lax.axis_size("z")
         if not (self.fast and nz == 4):
             pairs = [(j * nz + i, i * self.size + j) for i in range(nz) for j in range(self.size)]
             return along(lax.ppermute(own, ALL, pairs))
-        whole = along(own)
+        whole = after(along(own), first)
         rows = own.shape[0]
         k, pair = lax.axis_index("k"), lax.axis_index(TP) // 2
         got = jnp.zeros_like(whole)
@@ -128,7 +170,7 @@
             got = lax.dynamic_update_slice_in_dim(got, part, (pair ^ turn) * rows, 0)
         return got
 
-    def out_back(self, parts):
+    def out_back(self, parts, last):
         nz = lax.axis_size("z")
         if not (self.fast and nz == 4):
             pairs = [(i * self.size + j, j * nz + i) for i in range(nz) for j in range(self.size)]
@@ -140,7 +182,7 @@
             part = lax.dynamic_slice_in_dim(parts, (pair ^ turn) * rows, rows, 0)
             part = lax.ppermute(part, TP, [(b, a) for a, b in self.out_moves(turn)])
             got = lax.dynamic_update_slice_in_dim(got, part, (k ^ turn) * rows, 0)
-        return summed_along(got)
+        return summed_along(after(got, last))
 
     def exchange(self, v):
         return lax.all_to_all(v, TP, 0, 0, tiled=True)
@@ -193,22 +235,20 @@
 
     up_scaled = (w_up.astype(F32) * gain_two).astype(BF16)
     up_send = up_scaled.reshape(width, nz, np_, units).transpose(2, 0, 1, 3).reshape(np_, width, -1)
+    cut = 2 * HK + HV
     sent = [by_head(w) for w in (w_query, w_key, w_value, w_gate)] + [up_send]
     got = plane.exchange(jnp.concatenate(sent, axis=2)).reshape(np_ * width, -1)
-    cut = 2 * HK + HV
-    w_o = plane.out_in(w_out)
-    w_qkv = along(got[:, :cut])
-    w_g = along(got[:, cut : cut + HV])
+    w_h = along(got[:, : cut + HV])
     w_u = along(got[:, cut + HV :])
-    w_d = along(after(w_down, w_g))
+    w_d = along(after(w_down, w_h))
 
     loc = jnp.arange(tlen, dtype=jnp.int32)
     pos = (plane.order[:, None] * tlen + loc[None, :]).reshape(-1)
     lens = plane.lengths(lengths[0])
-    cut, seg = 0, 0
+    edge, seg = 0, 0
     for i in range(3):
-        cut = cut + lens[:, i : i + 1]
-        seg = seg + (pos[None, :] >= cut).astype(jnp.int32)
+        edge = edge + lens[:, i : i + 1]
+        seg = seg + (pos[None, :] >= edge).astype(jnp.int32)
     valid = seg < 3
     rate = DECAY_SCALE * jnp.exp2(-head.astype(F32)) / row_len
     gap = (pos[:, None] - pos[None, :]).astype(F32)
@@ -224,38 +264,49 @@
     hat1, scale1 = normed_rows(xf)
     h1 = plane.gather(hat1.astype(BF16))
     dy = plane.gather(after(cotangent[0], h1, got))
-    heads = dot(after(h1, dy), w_qkv)
+    w_o = plane.out_in(w_out, dy)
+    heads = dot(after(h1, dy), w_h)
     qk = heads[:, : 2 * HK].reshape(nrow, row_len, 2 * HK)
     queries = rotate(qk[..., :HK], cosine, sine).astype(BF16)
     keys = (rotate(qk[..., HK:], cosine, sine) * key_norm).astype(BF16)
-    values = heads[:, 2 * HK :].astype(BF16).reshape(nrow, row_len, HV)
+    values = heads[:, 2 * HK : cut].astype(BF16).reshape(nrow, row_len, HV)
+    gate = heads[:, cut:]
     scores = jnp.einsum("rnd,rmd->rnm", queries, keys, preferred_element_type=F32)
     weights = (scores * decay).astype(BF16)
-    mixed = jnp.einsum("rnm,rme->rne", weights, values, preferred_element_type=F32)
-    gate = dot(h1, w_g)
-    gated, gate_back = jax.vjp(group_gate, mixed.reshape(-1, HV), gate)
-    gated = gated.astype(BF16)
-    x2 = xf + plane.scatter(lambda a: dot(a, w_o), gated)
+    mixed = jnp.einsum("rnm,rme->rne", weights, values, preferred_element_type=F32).reshape(-1, HV)
+    centered = mixed - jnp.mean(mixed, axis=-1, keepdims=True)
+    group_scale = lax.rsqrt(jnp.mean(centered * centered, axis=-1, keepdims=True) + GN_EPS)
+    normed = centered * group_scale
+    sig = jax.nn.sigmoid(gate)
+    swish = gate * sig
+    gated = (normed * swish).astype(BF16)
+    x2 = xf + plane.scatter(lambda a: dot(a, w_o), gated, w_u)
 
     hat2, scale2 = normed_rows(x2)
-    h2 = plane.gather(hat2.astype(BF16))
-    hidden, act_back = jax.vjp(gelu_exact, dot(h2, w_u))
-    act = hidden.astype(BF16)
+    h2_parts, h2 = plane.gather_parts(hat2.astype(BF16))
+    acts, slopes = zip(*[gelu_and_slope(dot(a, w_u)) for a in h2_parts])
+    act, slope = plane.joined(acts), plane.joined(slopes)
+    act, slope = lax.optimization_barrier((act, slope))
 
     down_parts = dot_tn(act, dy).astype(BF16)
     down_rows = summed_along(down_parts)
-    d_hidden = act_back(dot_nt(dy, w_d))[0].astype(BF16)
+    d_hidden = (dot_nt(dy, w_d) * slope).astype(BF16)
     d_hidden = after(d_hidden, down_parts)
     up_parts = dot_tn(h2, d_hidden).astype(BF16)
     t2 = plane.scatter(lambda a: dot_nt(a, w_u), d_hidden, up_parts)
     up_rows = summed_along(up_parts)
     d_x2 = cotangent[0].astype(F32) + norm_back(t2, hat2, scale2)
-    d_branch = plane.gather(after(d_x2.astype(BF16), down_rows))
-
-    d_mixed, d_gate = gate_back(dot_nt(d_branch, w_o))
-    d_gate = d_gate.astype(BF16)
-    out_rows = plane.out_back(dot_tn(gated, d_branch).astype(BF16))
-    d_mixed = d_mixed.astype(BF16).reshape(nrow, row_len, HV)
+    d_branch_parts, d_branch = plane.gather_parts(after(d_x2.astype(BF16), down_rows))
+    gate_slope = normed * sig * (1.0 + gate * (1.0 - sig))
+    d_mixed, d_gate = [], []
+    for part, at in zip(d_branch_parts, plane.parts_of(normed, swish, gate_slope, group_scale)):
+        n_at, swish_at, slope_at, scale_at = at
+        d_gated = dot_nt(part, w_o)
+        d_gate.append((d_gated * slope_at).astype(BF16))
+        d_mixed.append(norm_back(d_gated * swish_at, n_at, scale_at).astype(BF16))
+    d_mixed, d_gate = plane.joined(d_mixed), plane.joined(d_gate)
+    g_rows = summed_along(dot_tn(h1, d_gate))
+    d_mixed = d_mixed.reshape(nrow, row_len, HV)
     d_values = jnp.einsum("rnm,rne->rme", weights, d_mixed, preferred_element_type=F32)
     d_values = d_values.astype(BF16).reshape(-1, HV)
     d_scores = jnp.einsum("rne,rme->rnm", d_mixed, values, preferred_element_type=F32)
@@ -264,16 +315,16 @@
     d_key = jnp.einsum("rnm,rnd->rmd", d_scores, queries, preferred_element_type=F32)
     d_query = unrotate(d_query, cosine, sine).astype(BF16)
     d_key = (unrotate(d_key, cosine, sine) * key_norm).astype(BF16)
-    d_qk = jnp.concatenate([d_query, d_key], axis=-1).reshape(-1, 2 * HK)
-    d_vg = after(jnp.concatenate([d_values, d_gate], axis=1), up_rows)
-    vg_rows = summed_along(dot_tn(h1, d_vg))
-    qk_rows = summed_along(dot_tn(h1, d_qk))
-    qkv_cut = 2 * HK + HV
-    d_heads = jnp.concatenate([d_qk, d_vg], axis=1)
+    d_qkv = jnp.concatenate([d_query.reshape(-1, HK), d_key.reshape(-1, HK), d_values], axis=1)
+    qkv_parts = dot_tn(h1, after(d_qkv, up_rows)).astype(BF16)
+    qkv_rows = summed_along(qkv_parts)
+    d_heads = jnp.concatenate([d_qkv, d_gate], axis=1)
     u1 = plane.scatter(
-        lambda a: dot_nt(a[:, :qkv_cut], w_qkv) + dot_nt(a[:, qkv_cut:], w_g), after(d_heads, out_rows)
+        lambda a: dot_nt(a, w_h), after(d_heads, up_rows)
     )
     tokens_grad = d_x2 + norm_back(u1, hat1, scale1)
+    gated_last, _ = lax.optimization_barrier((gated, qkv_parts))
+    out_rows = plane.out_back(dot_tn(gated_last, d_branch).astype(BF16), u1)
     output = x2 + plane.scatter(lambda a: dot(a, w_d), after(act, tokens_grad))
 
     out_grad = out_rows.astype(F32)
@@ -281,13 +332,12 @@
     def by_rows(rows):
         return plane.exchange(rows.reshape(np_, width, -1)).astype(F32).transpose(1, 0, 2)
 
-    up_sum = by_rows(up_rows).reshape(width, np_, nz, units).transpose(0, 2, 1, 3).reshape(width, -1)
-    vg_sum = by_rows(vg_rows)
-    v_sum = vg_sum[:, :, :HV].reshape(width, -1)
-    g_sum = vg_sum[:, :, HV:].reshape(width, -1)
-    qk_sum = by_rows(after(qk_rows, output))
-    q_sum = qk_sum[:, :, :HK].reshape(width, -1)
-    k_sum = qk_sum[:, :, HK:].reshape(width, -1)
+    up_sum = by_rows(after(up_rows, tokens_grad)).reshape(width, np_, nz, units).transpose(0, 2, 1, 3).reshape(width, -1)
+    g_sum = by_rows(after(g_rows, tokens_grad)).reshape(width, -1)
+    qkv_sum = by_rows(after(qkv_rows, output))
+    q_sum = qkv_sum[:, :, :HK].reshape(width, -1)
+    k_sum = qkv_sum[:, :, HK : 2 * HK].reshape(width, -1)
+    v_sum = qkv_sum[:, :, 2 * HK :].reshape(width, -1)
 
     def gain_sum(pairs):
         return sum(jnp.sum(w.astype(F32) * g, axis=1) for w, g in pairs)

time: 611 us -> 559 us (0.915)
  waiting for transfers between devices: 279 us -> 216 us
  matrix products: 100 us -> 112 us
  local copies, waits for them, and re-layouts: 75.9 us -> 66.9 us
    ppermute x45 -> x49, waiting for transfers between devices: 173 us -> 114 us  [swap(): return lax.ppermute(v, TP, [(j, j ^ mask) for j in range(self.size)])]
    ppermute x4, waiting for transfers between devices: 16.4 us -> 1.05 us  [out_back(): part = lax.ppermute(part, TP, [(b, a) for a, b in self.out_moves(turn)])]
    dot_general x8 -> x17, matrix products: 32.8 us -> 45 us  [dot_nt(): lax.dot_general(a, b, (((1,), (1,)), ((), ())), preferred_element_type=F32)]
    all_to_all x3, waiting for transfers between devices: 14.1 us -> 22.4 us  [exchange(): return lax.all_to_all(v, TP, 0, 0, tiled=True)]
    slice x11 -> x7, local copies, waits for them, and re-layouts: 11.5 us -> 3.65 us  [the longest x4 2.25 us: scatter(): blocks = [left[i * rows:(i + 1) * rows] for i in range(8)]]
    all_gather x5 -> x4, waiting for transfers between devices: 34.6 us -> 42.1 us  [along(): return lax.all_gather(own, 'z', axis=0, tiled=True)]
    reduce_scatter x5, waiting for transfers between devices: 24.3 us -> 17.3 us  [summed_along(): lax.psum_scatter(parts.astype(BF16), 'z', scatter_dimension=0, tiled=True)]
    ppermute x45 -> x49, starting transfers between devices: 30.1 us -> 34.9 us  [swap(): return lax.ppermute(v, TP, [(j, j ^ mask) for j in range(self.size)])]
  transfers between devices with their start and end apart: 66 -> 69, of which waited for: 39 -> 29; matrix products, arithmetic and copies ran while one was open for 29% -> 37% of each run, Pallas kernels for 0% -> 0%
where the time goes in v2:
time: 559 us; the launch traced here: 551 us
  waiting for transfers between devices  216 us (39%)
  matrix products  112 us (20%)
  local copies, waits for them, and re-layouts  66.9 us (12%)
  starting transfers between devices  61.8 us (11%)
  other arithmetic  47.8 us (9%)
  blocking collectives  31 us (6%)
  between operations  16.1 us (3%)
    ppermute x49, waiting for transfers between devices, swap(): return lax.ppermute(v, TP, [(j, j ^ mask) for j in range(self.size)])  114 us
    unnamed x217, local copies, waits for them, and re-layouts  46.6 us
    dot_general x17, matrix products, dot_nt(): lax.dot_general(a, b, (((1,), (1,)), ((), ())), preferred_element_type=F32)  45 us
    all_gather x4, waiting for transfers between devices, along(): return lax.all_gather(own, 'z', axis=0, tiled=True)  42.1 us
    dot_general x17, matrix products, dot(): return jnp.dot(a, b, preferred_element_type=F32)  37.1 us
    ppermute x49, starting transfers between devices, swap(): return lax.ppermute(v, TP, [(j, j ^ mask) for j in range(self.size)])  34.9 us
    all_to_all x1, blocking collectives, exchange(): return lax.all_to_all(v, TP, 0, 0, tiled=True)  31 us
    dot_general x5, matrix products, dot_tn(): lax.dot_general(a, b, (((0,), (0,)), ((), ())), preferred_element_type=F32)  25.3 us
  transfers between devices with their start and end apart: 69, of which 29 were waited for; matrix products, arithmetic and copies ran while one was open for 37% of the time, Pallas kernels for 0%

profile of v2, /device:TPU:0, one launch (start us, length us, event | category | flops | bytes accessed | tf_op | source)
XLA Modules:
  0.0 551.3 jit_solution(8674477447895587489)
XLA Ops:
  14.2 31.0 %all_to_all.20 = bf16[8,64,2048]{2,1,0:T(8,128)(2,1)S(1)} all-to-all(bf16[8,64,2048]{2,1,0:T(8,128)(2,1)S(1)} %copy.46), channel_id=1, replica_groups=mesh['z'=4,'x'=2,'k'=4] {'x','k'}, dimensions={0} | all-to-all | bytes 4194304 | tf_op jit(solution)/shard_map/all_to_all | solution.py:188
  52.9 9.5 %collective-permute-done.1 = bf16[128,2048]{1,0:T(8,128)(2,1)S(1)} collective-permute-done((bf16[128,2048]{1,0:T(8,128)(2,1)}, bf16[128,2048]{1,0:T(8,128)(2,1)S(1)}, u32[]{:S(2)}, u32[]{:S(2)}) %collective-permute-start.1) | collective-permute-done | bytes 524320 | tf_op jit(solution)/shard_map/ppermute | solution.py:93
  67.7 6.9 %collective-permute-done.5 = bf16[128,2048]{1,0:T(8,128)(2,1)S(1)} collective-permute-done((bf16[128,2048]{1,0:T(8,128)(2,1)}, bf16[128,2048]{1,0:T(8,128)(2,1)S(1)}, u32[]{:S(2)}, u32[]{:S(2)}) %collective-permute-start.5) | collective-permute-done | bytes 524320 | tf_op jit(solution)/shard_map/ppermute | solution.py:93
  85.9 8.4 %collective-permute-done.8 = bf16[128,2048]{1,0:T(8,128)(2,1)} collective-permute-done((bf16[128,2048]{1,0:T(8,128)(2,1)S(1)}, bf16[128,2048]{1,0:T(8,128)(2,1)}, u32[]{:S(2)}, u32[]{:S(2)}) %collective-permute-start.8) | collective-permute-done | bytes 524320 | tf_op jit(solution)/shard_map/ppermute | solution.py:93
  100.3 6.7 %collective-permute-done.12 = bf16[128,2048]{1,0:T(8,128)(2,1)S(1)} collective-permute-done((bf16[128,2048]{1,0:T(8,128)(2,1)S(1)}, bf16[128,2048]{1,0:T(8,128)(2,1)S(1)}, u32[]{:S(2)}, u32[]{:S(2)}) %collective-permute-start.12) | collective-permute-done | bytes 524320 | tf_op jit(solution)/shard_map/ppermute | solution.py:93
  126.7 14.1 %collective-permute-done.16 = bf16[128,2048]{1,0:T(8,128)(2,1)} collective-permute-done((bf16[128,2048]{1,0:T(8,128)(2,1)}, bf16[128,2048]{1,0:T(8,128)(2,1)}, u32[]{:S(2)}, u32[]{:S(2)}) %collective-permute-start.16) | collective-permute-done | bytes 524320 | tf_op jit(solution)/shard_map/ppermute | solution.py:169
  146.7 27.2 %all-gather.5.cloned.1.call-done = bf16[2048,1536]{1,0:T(8,128)(2,1)} async-done(((bf16[512,1536]{1,0:T(8,128)(2,1)}), bf16[2048,1536]{1,0:T(8,128)(2,1)}) %all-gather.5.cloned.1.call-update) | async-done | bytes 6291472 | tf_op jit(solution)/shard_map/all_gather | solution.py:53
  173.9 10.0 %fusion.212 = f32[1024,1536]{1,0:T(8,128)S(1)} fusion(bf16[1024,2048]{1,0:T(8,128)(2,1)} %constant_dynamic-update-slice_fusion, bf16[2048,1536]{1,0:T(8,128)(2,1)} %all-gather.5.cloned.1.call-done), kind=kOutput, calls=%fused_computation.388 | convolution fusion | flops 6442450944 | bytes 16777216 | tf_op jit(solution)/shard_map/dot_general | solution.py:23
  205.4 14.9 %all-gather.9.cloned.1.call-done = bf16[2048,512]{1,0:T(8,128)(2,1)} async-done(((bf16[512,512]{1,0:T(8,128)(2,1)}), bf16[2048,512]{1,0:T(8,128)(2,1)}) %all-gather.9.cloned.1.call-update) | async-done | bytes 2097168 | tf_op jit(solution)/shard_map/all_gather | solution.py:53
  220.3 4.0 collective-permute-done.22
  232.8 10.3 %collective-permute-done.25 = bf16[128,2048]{1,0:T(8,128)(2,1)} collective-permute-done((bf16[128,2048]{1,0:T(8,128)(2,1)}, bf16[128,2048]{1,0:T(8,128)(2,1)}, u32[]{:S(2)}, u32[]{:S(2)}) %collective-permute-start.25) | collective-permute-done | bytes 524320 | tf_op jit(solution)/shard_map/ppermute | solution.py:93
  244.7 10.1 %collective-permute-done.29 = bf16[128,2048]{1,0:T(8,128)(2,1)} collective-permute-done((bf16[128,2048]{1,0:T(8,128)(2,1)}, bf16[128,2048]{1,0:T(8,128)(2,1)}, u32[]{:S(2)}, u32[]{:S(2)}) %collective-permute-start.29) | collective-permute-done | bytes 524320 | tf_op jit(solution)/shard_map/ppermute | solution.py:93
  269.8 5.9 %convolution_convert_fusion.4 = bf16[512,2048]{1,0:T(8,128)(2,1)} fusion(bf16[1024,512]{1,0:T(8,128)(2,1)S(1)} %pad_maximum_fusion.2, bf16[1024,2048]{1,0:T(8,128)(2,1)} %constant_dynamic-update-slice_fusion.8), kind=kOutput, calls=%fused_computation.4 | convolution fusion | flops 2148532224 | bytes 7340032 | tf_op jit(solution)/shard_map/dot_general | solution.py:31
  277.6 5.9 %multiply_convert_fusion = bf16[1024,512]{1,0:T(8,128)(2,1)S(1)} fusion(f32[1024,512]{1,0:T(8,128)} %pad_maximum_fusion, bf16[1024,2048]{1,0:T(8,128)(2,1)} %constant_dynamic-update-slice_fusion.8, bf16[512,2048]{1,0:T(8,128)(2,1)} %all-gather.11.cloned.1.call-done), kind=kOutput, calls=%fused_computation.31 | convolution fusion | flops 2148532224 | bytes 9437184 | tf_op jit(solution)/shard_map/dot_general | solution.py:27
  298.1 3.8 convolution_convert_fusion.3
  307.4 10.2 %collective-permute-done.34 = bf16[128,2048]{1,0:T(8,128)(2,1)} collective-permute-done((bf16[128,2048]{1,0:T(8,128)(2,1)}, bf16[128,2048]{1,0:T(8,128)(2,1)}, u32[]{:S(2)}, u32[]{:S(2)}) %collective-permute-start.34) | collective-permute-done | bytes 524320 | tf_op jit(solution)/shard_map/ppermute | solution.py:93
  325.1 10.3 %collective-permute-done.37 = bf16[128,2048]{1,0:T(8,128)(2,1)} collective-permute-done((bf16[128,2048]{1,0:T(8,128)(2,1)}, bf16[128,2048]{1,0:T(8,128)(2,1)}, u32[]{:S(2)}, u32[]{:S(2)}) %collective-permute-start.37) | collective-permute-done | bytes 524320 | tf_op jit(solution)/shard_map/ppermute | solution.py:93
  338.0 10.1 %collective-permute-done.41 = bf16[128,2048]{1,0:T(8,128)(2,1)S(1)} collective-permute-done((bf16[128,2048]{1,0:T(8,128)(2,1)}, bf16[128,2048]{1,0:T(8,128)(2,1)S(1)}, u32[]{:S(2)}, u32[]{:S(2)}) %collective-permute-start.41) | collective-permute-done | bytes 524320 | tf_op jit(solution)/shard_map/ppermute | solution.py:93
  353.3 4.8 fusion.90
  359.1 3.8 convolution_convert_fusion.2
  377.7 9.4 %convolution_convert_fusion = bf16[2048,1024]{1,0:T(8,128)(2,1)} fusion(bf16[1024,2048]{1,0:T(8,128)(2,1)} %constant_dynamic-update-slice_fusion, bf16[1024,1024]{1,0:T(8,128)(2,1)} %pad_maximum_fusion.1), kind=kOutput, calls=%fused_computation | convolution fusion | flops 4297064448 | bytes 10485760 | tf_op jit(solution)/shard_map/dot_general | solution.py:31
  392.9 4.8 convolution_convert_fusion.11
  418.7 4.0 add_convert_fusion.5
  424.4 3.9 add_convert_fusion.4
  428.3 4.2 add_convert_fusion.3
  437.8 9.2 %collective-permute-done.45 = bf16[128,2048]{1,0:T(8,128)(2,1)S(1)} collective-permute-done((bf16[128,2048]{1,0:T(8,128)(2,1)}, bf16[128,2048]{1,0:T(8,128)(2,1)S(1)}, u32[]{:S(2)}, u32[]{:S(2)}) %collective-permute-start.45) | collective-permute-done | bytes 524320 | tf_op jit(solution)/shard_map/ppermute | solution.py:93
  447.0 6.7 %collective-permute-done.46 = bf16[128,2048]{1,0:T(8,128)(2,1)} collective-permute-done((bf16[128,2048]{1,0:T(8,128)(2,1)}, bf16[128,2048]{1,0:T(8,128)(2,1)}, u32[]{:S(2)}, u32[]{:S(2)}) %collective-permute-start.46) | collective-permute-done | bytes 524320 | tf_op jit(solution)/shard_map/ppermute | solution.py:93
  474.1 4.1 all-to-all-start.3
  480.5 16.8 %all-to-all-done.3 = bf16[8,64,512]{2,1,0:T(8,128)(2,1)} async-done(((bf16[8,64,512]{2,1,0:T(8,128)(2,1)}), bf16[8,64,512]{2,1,0:T(8,128)(2,1)}, u32[]{:S(2)}, u32[]{:S(2)}) %all-to-all-start.3) | async-done | bytes 524320 | tf_op jit(solution)/shard_map/all_to_all | solution.py:188
  503.9 5.7 %all-to-all-done.2 = bf16[8,64,512]{2,1,0:T(8,128)(2,1)S(1)} async-done(((bf16[8,64,512]{2,1,0:T(8,128)(2,1)}), bf16[8,64,512]{2,1,0:T(8,128)(2,1)S(1)}, u32[]{:S(2)}, u32[]{:S(2)}) %all-to-all-start.2) | async-done | bytes 524320 | tf_op jit(solution)/shard_map/all_to_all | solution.py:188
  509.6 3.9 all-to-all-start.1
  519.8 17.3 %reduce-scatter.14.cloned.1.call-done = bf16[128,2048]{1,0:T(8,128)(2,1)} async-done(((bf16[512,2048]{1,0:T(8,128)(2,1)}), bf16[128,2048]{1,0:T(8,128)(2,1)}) %reduce-scatter.14.cloned.1.call-update) | async-done | bytes 524304 | tf_op jit(solution)/shard_map/reduce_scatter | solution.py:57
  (476 shorter events, 237.3 us)
Async XLA Ops:
  7.2 105.0 %all-gather.7.cloned.1.call-start = ((), (), s32[]{:S(2)}) async-start(), calls=%async_computation.10 | async-start | bytes 2621440 | tf_op jit(solution)/shard_map/all_gather | solution.py:53
  7.9 166.0 %all-gather.5.cloned.1.call-start = ((), (), s32[]{:S(2)}) async-start(), calls=%async_computation.9 | async-start | bytes 7864320 | tf_op jit(solution)/shard_map/all_gather | solution.py:53
  46.5 173.8 %all-gather.9.cloned.1.call-start = ((), (), s32[]{:S(2)}) async-start(), calls=%async_computation.11 | async-start | bytes 2621440 | tf_op jit(solution)/shard_map/all_gather | solution.py:53
  50.3 24.3 %collective-permute-start.5 = (bf16[128,2048]{1,0:T(8,128)(2,1)}, bf16[128,2048]{1,0:T(8,128)(2,1)S(1)}, u32[]{:S(2)}, u32[]{:S(2)}) collective-permute-start(bf16[128,2048]{1,0:T(8,128)(2,1)} %get-tuple-element.77), channel_id=1, source_target_pairs={{0,6},{1,7},{2,4},{3,5},{4,2},{5,3},{6,0},{7,1},{8,14},{9,15},{10,... | collective-permute-start | bytes 1572872 | tf_op jit(solution)/shard_map/ppermute | solution.py:93
  51.7 65.6 %collective-permute-start.14 = (s32[4]{0:T(128)S(1)}, s32[4]{0:T(128)S(1)}, u32[]{:S(2)}, u32[]{:S(2)}) collective-permute-start(s32[4]{0:T(128)S(1)} %bitcast.223), channel_id=1, source_target_pairs={{0,4},{1,5},{2,6},{3,7},{4,0},{5,1},{6,2},{7,3},{8,12},{9,13},{10,... | collective-permute-start | bytes 56 | tf_op jit(solution)/shard_map/ppermute | solution.py:93
  84.5 22.4 %collective-permute-start.12 = (bf16[128,2048]{1,0:T(8,128)(2,1)S(1)}, bf16[128,2048]{1,0:T(8,128)(2,1)S(1)}, u32[]{:S(2)}, u32[]{:S(2)}) collective-permute-start(bf16[128,2048]{1,0:T(8,128)(2,1)S(1)} %bitcast.203), channel_id=1, source_target_pairs={{0,6},{1,7},{2,4},{3,5},{4,2},{5,3},{6,0},{7,1},{8,14},{9,15},{10,... | collective-permute-start | bytes 1572872 | tf_op jit(solution)/shard_map/ppermute | solution.py:93
  117.3 23.5 %collective-permute-start.16 = (bf16[128,2048]{1,0:T(8,128)(2,1)}, bf16[128,2048]{1,0:T(8,128)(2,1)}, u32[]{:S(2)}, u32[]{:S(2)}) collective-permute-start(bf16[128,2048]{1,0:T(8,128)(2,1)} %get-tuple-element.111), channel_id=1, source_target_pairs={{0,2},{1,0},{2,6},{3,4},{4,3},{5,1},{6,7},{7,5},{8,10},{9,8},{10,1... | collective-permute-start | bytes 1572872 | tf_op jit(solution)/shard_map/ppermute | solution.py:169
  120.7 23.2 %collective-permute-start.17 = (bf16[128,2048]{1,0:T(8,128)(2,1)}, bf16[128,2048]{1,0:T(8,128)(2,1)}, u32[]{:S(2)}, u32[]{:S(2)}) collective-permute-start(bf16[128,2048]{1,0:T(8,128)(2,1)} %get-tuple-element.110), channel_id=1, source_target_pairs={{0,4},{1,6},{2,0},{3,2},{4,5},{5,7},{6,1},{7,3},{8,12},{9,14},{10,... | collective-permute-start | bytes 1572872 | tf_op jit(solution)/shard_map/ppermute | solution.py:169
  122.3 155.3 %all-gather.11.cloned.1.call-start = ((), (), s32[]{:S(2)}) async-start(), calls=%async_computation.12 | async-start | bytes 2621440 | tf_op jit(solution)/shard_map/all_gather | solution.py:53
  122.3 24.3 %collective-permute-start.18 = (bf16[128,2048]{1,0:T(8,128)(2,1)}, bf16[128,2048]{1,0:T(8,128)(2,1)S(1)}, u32[]{:S(2)}, u32[]{:S(2)}) collective-permute-start(bf16[128,2048]{1,0:T(8,128)(2,1)} %get-tuple-element.109), channel_id=1, source_target_pairs={{0,6},{1,4},{2,2},{3,0},{4,7},{5,5},{6,3},{7,1},{8,14},{9,12},{10,... | collective-permute-start | bytes 1572872 | tf_op jit(solution)/shard_map/ppermute | solution.py:169
  201.6 22.7 %collective-permute-start.22 = (bf16[128,2048]{1,0:T(8,128)(2,1)}, bf16[128,2048]{1,0:T(8,128)(2,1)S(1)}, u32[]{:S(2)}, u32[]{:S(2)}) collective-permute-start(bf16[128,2048]{1,0:T(8,128)(2,1)} %fusion.1), channel_id=1, source_target_pairs={{0,4},{1,5},{2,6},{3,7},{4,0},{5,1},{6,2},{7,3},{8,12},{9,13},{10,... | collective-permute-start | bytes 1572872 | tf_op jit(solution)/shard_map/ppermute | solution.py:93
  231.1 23.8 %collective-permute-start.29 = (bf16[128,2048]{1,0:T(8,128)(2,1)}, bf16[128,2048]{1,0:T(8,128)(2,1)}, u32[]{:S(2)}, u32[]{:S(2)}) collective-permute-start(bf16[128,2048]{1,0:T(8,128)(2,1)} %get-tuple-element.71), channel_id=1, source_target_pairs={{0,6},{1,7},{2,4},{3,5},{4,2},{5,3},{6,0},{7,1},{8,14},{9,15},{10,... | collective-permute-start | bytes 1572872 | tf_op jit(solution)/shard_map/ppermute | solution.py:93
  232.4 22.5 %collective-permute-start.24 = (bf16[128,2048]{1,0:T(8,128)(2,1)}, bf16[128,2048]{1,0:T(8,128)(2,1)}, u32[]{:S(2)}, u32[]{:S(2)}) collective-permute-start(bf16[128,2048]{1,0:T(8,128)(2,1)} %get-tuple-element.71), channel_id=1, source_target_pairs={{0,1},{1,0},{2,3},{3,2},{4,5},{5,4},{6,7},{7,6},{8,9},{9,8},{10,11... | collective-permute-start | bytes 1572872 | tf_op jit(solution)/shard_map/ppermute | solution.py:93
  232.4 88.9 %reduce-scatter.6.cloned.1.call-start = ((), (), s32[]{:S(2)}) async-start(), calls=%async_computation.13 | async-start | bytes 2621440 | tf_op jit(solution)/shard_map/reduce_scatter | solution.py:57
  275.7 102.0 %reduce-scatter.8.cloned.1.call-start = ((), (), s32[]{:S(2)}) async-start(), calls=%async_computation.14 | async-start | bytes 2621440 | tf_op jit(solution)/shard_map/reduce_scatter | solution.py:57
  295.2 22.4 %collective-permute-start.34 = (bf16[128,2048]{1,0:T(8,128)(2,1)}, bf16[128,2048]{1,0:T(8,128)(2,1)}, u32[]{:S(2)}, u32[]{:S(2)}) collective-permute-start(bf16[128,2048]{1,0:T(8,128)(2,1)} %add_convert_fusion.7), channel_id=1, source_target_pairs={{0,4},{1,5},{2,6},{3,7},{4,0},{5,1},{6,2},{7,3},{8,12},{9,13},{10,... | collective-permute-start | bytes 1572872 | tf_op jit(solution)/shard_map/ppermute | solution.py:93
  322.6 157.9 %reduce-scatter.12.cloned.1.call-start = ((), (), s32[]{:S(2)}) async-start(), calls=%async_computation.16 | async-start | bytes 2621440 | tf_op jit(solution)/shard_map/reduce_scatter | solution.py:57
  324.4 23.6 %collective-permute-start.41 = (bf16[128,2048]{1,0:T(8,128)(2,1)}, bf16[128,2048]{1,0:T(8,128)(2,1)S(1)}, u32[]{:S(2)}, u32[]{:S(2)}) collective-permute-start(bf16[128,2048]{1,0:T(8,128)(2,1)} %get-tuple-element.38), channel_id=1, source_target_pairs={{0,6},{1,7},{2,4},{3,5},{4,2},{5,3},{6,0},{7,1},{8,14},{9,15},{10,... | collective-permute-start | bytes 1572872 | tf_op jit(solution)/shard_map/ppermute | solution.py:93
  325.1 23.0 %collective-permute-start.36 = (bf16[128,2048]{1,0:T(8,128)(2,1)}, bf16[128,2048]{1,0:T(8,128)(2,1)S(1)}, u32[]{:S(2)}, u32[]{:S(2)}) collective-permute-start(bf16[128,2048]{1,0:T(8,128)(2,1)} %get-tuple-element.38), channel_id=1, source_target_pairs={{0,1},{1,0},{2,3},{3,2},{4,5},{5,4},{6,7},{7,6},{8,9},{9,8},{10,11... | collective-permute-start | bytes 1572872 | tf_op jit(solution)/shard_map/ppermute | solution.py:93
  362.9 141.0 %reduce-scatter.10.cloned.1.call-start = ((), (), s32[]{:S(2)}) async-start(), calls=%async_computation.15 | async-start | bytes 5242880 | tf_op jit(solution)/shard_map/reduce_scatter | solution.py:57
  387.2 149.9 %reduce-scatter.14.cloned.1.call-start = ((), (), s32[]{:S(2)}) async-start(), calls=%async_computation.17 | async-start | bytes 2621440 | tf_op jit(solution)/shard_map/reduce_scatter | solution.py:57
  405.1 23.2 %collective-permute-start.43 = (bf16[256,2048]{1,0:T(8,128)(2,1)S(1)}, bf16[256,2048]{1,0:T(8,128)(2,1)S(1)}, u32[]{:S(2)}, u32[]{:S(2)}) collective-permute-start(bf16[256,2048]{1,0:T(8,128)(2,1)S(1)} %convolution_convert_fusion.12), channel_id=1, source_target_pairs={{0,1},{1,0},{2,3},{3,2},{4,5},{5,4},{6,7},{7,6},{8,9},{9,8},{10,11... | collective-permute-start | bytes 3145736 | tf_op jit(solution)/shard_map/ppermute | solution.py:93
  408.0 24.5 %collective-permute-start.54 = (bf16[128,2048]{1,0:T(8,128)(2,1)S(1)}, bf16[128,2048]{1,0:T(8,128)(2,1)S(1)}, u32[]{:S(2)}, u32[]{:S(2)}) collective-permute-start(bf16[128,2048]{1,0:T(8,128)(2,1)S(1)} %get-tuple-element.93), channel_id=1, source_target_pairs={{2,0},{0,1},{6,2},{4,3},{3,4},{1,5},{7,6},{5,7},{10,8},{8,9},{14,1... | collective-permute-start | bytes 1572872 | tf_op jit(solution)/shard_map/ppermute | solution.py:183
  408.1 26.9 %collective-permute-start.55 = (bf16[128,2048]{1,0:T(8,128)(2,1)S(1)}, bf16[128,2048]{1,0:T(8,128)(2,1)S(1)}, u32[]{:S(2)}, u32[]{:S(2)}) collective-permute-start(bf16[128,2048]{1,0:T(8,128)(2,1)S(1)} %get-tuple-element.92), channel_id=1, source_target_pairs={{4,0},{6,1},{0,2},{2,3},{5,4},{7,5},{1,6},{3,7},{12,8},{14,9},{8,1... | collective-permute-start | bytes 1572872 | tf_op jit(solution)/shard_map/ppermute | solution.py:183
  413.2 23.7 %collective-permute-start.56 = (bf16[128,2048]{1,0:T(8,128)(2,1)S(1)}, bf16[128,2048]{1,0:T(8,128)(2,1)S(1)}, u32[]{:S(2)}, u32[]{:S(2)}) collective-permute-start(bf16[128,2048]{1,0:T(8,128)(2,1)S(1)} %get-tuple-element.91), channel_id=1, source_target_pairs={{6,0},{4,1},{2,2},{0,3},{7,4},{5,5},{3,6},{1,7},{14,8},{12,9},{10,... | collective-permute-start | bytes 1572872 | tf_op jit(solution)/shard_map/ppermute | solution.py:183
  422.7 24.3 %collective-permute-start.45 = (bf16[128,2048]{1,0:T(8,128)(2,1)}, bf16[128,2048]{1,0:T(8,128)(2,1)S(1)}, u32[]{:S(2)}, u32[]{:S(2)}) collective-permute-start(bf16[128,2048]{1,0:T(8,128)(2,1)} %add_convert_fusion.5), channel_id=1, source_target_pairs={{0,6},{1,7},{2,4},{3,5},{4,2},{5,3},{6,0},{7,1},{8,14},{9,15},{10,... | collective-permute-start | bytes 1572872 | tf_op jit(solution)/shard_map/ppermute | solution.py:93
  428.3 25.4 %collective-permute-start.46 = (bf16[128,2048]{1,0:T(8,128)(2,1)}, bf16[128,2048]{1,0:T(8,128)(2,1)}, u32[]{:S(2)}, u32[]{:S(2)}) collective-permute-start(bf16[128,2048]{1,0:T(8,128)(2,1)} %add_convert_fusion.4), channel_id=1, source_target_pairs={{0,4},{1,5},{2,6},{3,7},{4,0},{5,1},{6,2},{7,3},{8,12},{9,13},{10,... | collective-permute-start | bytes 1572872 | tf_op jit(solution)/shard_map/ppermute | solution.py:93
  465.3 35.5 %collective-permute-start.50 = (bf16[128,2048]{1,0:T(8,128)(2,1)}, bf16[128,2048]{1,0:T(8,128)(2,1)}, u32[]{:S(2)}, u32[]{:S(2)}) collective-permute-start(bf16[128,2048]{1,0:T(8,128)(2,1)} %add_convert_fusion.2), channel_id=1, source_target_pairs={{0,6},{1,7},{2,4},{3,5},{4,2},{5,3},{6,0},{7,1},{8,14},{9,15},{10,... | collective-permute-start | bytes 1572872 | tf_op jit(solution)/shard_map/ppermute | solution.py:93
  468.3 32.5 %collective-permute-start.51 = (bf16[128,2048]{1,0:T(8,128)(2,1)}, bf16[128,2048]{1,0:T(8,128)(2,1)}, u32[]{:S(2)}, u32[]{:S(2)}) collective-permute-start(bf16[128,2048]{1,0:T(8,128)(2,1)} %add_convert_fusion.1), channel_id=1, source_target_pairs={{0,4},{1,5},{2,6},{3,7},{4,0},{5,1},{6,2},{7,3},{8,12},{9,13},{10,... | collective-permute-start | bytes 1572872 | tf_op jit(solution)/shard_map/ppermute | solution.py:93
  473.4 27.5 %collective-permute-start.52 = (bf16[128,2048]{1,0:T(8,128)(2,1)}, bf16[128,2048]{1,0:T(8,128)(2,1)}, u32[]{:S(2)}, u32[]{:S(2)}) collective-permute-start(bf16[128,2048]{1,0:T(8,128)(2,1)} %add_convert_fusion), channel_id=1, source_target_pairs={{0,2},{1,3},{2,0},{3,1},{4,6},{5,7},{6,4},{7,5},{8,10},{9,11},{10,... | collective-permute-start | bytes 1572872 | tf_op jit(solution)/shard_map/ppermute | solution.py:93
  474.1 23.3 %all-to-all-start.3 = ((bf16[8,64,512]{2,1,0:T(8,128)(2,1)}), bf16[8,64,512]{2,1,0:T(8,128)(2,1)}, u32[]{:S(2)}, u32[]{:S(2)}) async-start(bf16[8,64,512]{2,1,0:T(8,128)(2,1)} %bitcast.214), calls=%async_computation.8 | async-start | bytes 1048576 | tf_op jit(solution)/shard_map/all_to_all | solution.py:188
  509.6 29.6 %all-to-all-start.1 = ((bf16[8,64,1024]{2,1,0:T(8,128)(2,1)}), bf16[8,64,1024]{2,1,0:T(8,128)(2,1)S(1)}, u32[]{:S(2)}, u32[]{:S(2)}) async-start(bf16[8,64,1024]{2,1,0:T(8,128)(2,1)} %bitcast.208), calls=%async_computation.4 | async-start | bytes 2097152 | tf_op jit(solution)/shard_map/all_to_all | solution.py:188
  (124 other events, 873.3 us)
Sparse Core Ops, SparseCore 0:
  9.6 48.6 all-gather.6
  59.8 114.0 all-gather.4
  176.1 44.1 all-gather.8
  232.5 43.5 all-gather.10
  278.3 42.5 reduce-scatter.5
  323.2 43.1 reduce-scatter.7
  368.7 43.2 reduce-scatter.11
  414.3 76.0 reduce-scatter.9
  492.7 44.3 reduce-scatter.13

commit v3 on v2

--- a/solution.py
+++ b/solution.py
@@ -71,7 +71,12 @@
     inside = (me == 1) | (me == 2)
     held = [own, near, jnp.where(inside, mid, out_mid), jnp.where(inside, far, out_far)]
     places = jnp.array([[0, 1, 2, 3], [1, 0, 2, 3], [3, 2, 0, 1], [3, 2, 1, 0]], jnp.int32)
-    return jnp.concatenate(held, axis=0), lax.dynamic_index_in_dim(places, me, keepdims=False)
+    places = lax.dynamic_index_in_dim(places, me, keepdims=False)
+    held = jnp.concatenate(held, axis=0)
+    rows = own.shape[0]
+    return jnp.concatenate(
+        [lax.dynamic_slice_in_dim(held, places[i] * rows, rows, 0) for i in range(4)], axis=0
+    )
 
 
 def after(value, *others):
@@ -107,11 +112,12 @@
             held[mask ^ 1] = self.swap(held[mask], 1)
         return jnp.concatenate([held[m] for m in range(8)], axis=0)
 
-    def scatter(self, product, left, *fill):
+    def scatter(self, product, left, *fill, late=None):
         if not self.fast:
-            return lax.psum_scatter(
+            total = lax.psum_scatter(
                 product(left).astype(BF16), TP, scatter_dimension=0, tiled=True
             ).astype(F32)
+            return total if late is None else (total, late[0](late[1]))
         rows = left.shape[0] // 8
         blocks = [left[i * rows : (i + 1) * rows] for i in range(8)]
         come = {}
@@ -120,26 +126,30 @@
             away = self.swap(away, 1)
             for i, m in enumerate(pair):
                 come[m] = away[i * rows : (i + 1) * rows]
-        sent = [
-            self.swap((product(blocks[m]) + come[m].astype(F32)).astype(BF16), m) for m in (6, 4, 2)
-        ]
+        sums = [(product(blocks[m]) + come[m].astype(F32)).astype(BF16) for m in (6, 4, 2)]
+        if late is not None:
+            held = lax.optimization_barrier((*sums, *late[1]))
+            sums, filled = held[:3], late[0](held[3:])
+        sent = [self.swap(part, m) for part, m in zip(sums, (6, 4, 2))]
         total = product(blocks[0]) + come[0].astype(F32)
+        if late is not None:
+            total = after(total, filled)
         total = after(total, *fill) if fill else total
         for part in sent:
             total = total + part.astype(F32)
-        return total
+        return total if late is None else (total, filled)
 
     def gather_parts(self, own):
         if not self.fast:
             whole = self.gather(own)
-            return [whole], whole
+            return [whole], [whole]
         held = {0: own}
         for mask in (6, 4, 2):
             held[mask] = self.swap(own, mask)
         for mask in (0, 4, 2, 6):
             held[mask ^ 1] = self.swap(held[mask], 1)
         parts = [jnp.concatenate([held[m], held[m + 1]], axis=0) for m in (0, 4, 2, 6)]
-        return parts, self.joined(parts)
+        return parts, [held[m] for m in range(8)]
 
     def joined(self, parts):
         if not self.fast:
@@ -155,13 +165,16 @@
     def out_moves(self, turn):
         return [(4 * x + k, 2 * (k ^ turn) + x) for x in range(2) for k in range(4)]
 
+    def out_along(self, own):
+        return along_by_hops(own) if self.fast and lax.axis_size("z") == 4 else own
+
     def out_in(self, own, first):
         nz = lax.axis_size("z")
         if not (self.fast and nz == 4):
             pairs = [(j * nz + i, i * self.size + j) for i in range(nz) for j in range(self.size)]
             return along(lax.ppermute(own, ALL, pairs))
-        whole = after(along(own), first)
-        rows = own.shape[0]
+        whole = after(own, first)
+        rows = own.shape[0] // 4
         k, pair = lax.axis_index("k"), lax.axis_index(TP) // 2
         got = jnp.zeros_like(whole)
         for turn in range(4):
@@ -236,10 +249,12 @@
     up_scaled = (w_up.astype(F32) * gain_two).astype(BF16)
     up_send = up_scaled.reshape(width, nz, np_, units).transpose(2, 0, 1, 3).reshape(np_, width, -1)
     cut = 2 * HK + HV
-    sent = [by_head(w) for w in (w_query, w_key, w_value, w_gate)] + [up_send]
+    sent = [by_head(w) for w in (w_query, w_key, w_value, w_gate)]
+    out_held = plane.out_along(w_out)
     got = plane.exchange(jnp.concatenate(sent, axis=2)).reshape(np_ * width, -1)
-    w_h = along(got[:, : cut + HV])
-    w_u = along(got[:, cut + HV :])
+    w_h = along(after(got, out_held))
+    up_got = plane.exchange(after(up_send, got)).reshape(np_ * width, -1)
+    w_u = along(up_got)
     w_d = along(after(w_down, w_h))
 
     loc = jnp.arange(tlen, dtype=jnp.int32)
@@ -262,9 +277,9 @@
 
     xf = tok.astype(F32)
     hat1, scale1 = normed_rows(xf)
-    h1 = plane.gather(hat1.astype(BF16))
+    h1 = plane.gather(after(hat1.astype(BF16), up_got))
     dy = plane.gather(after(cotangent[0], h1, got))
-    w_o = plane.out_in(w_out, dy)
+    w_o = plane.out_in(out_held, dy)
     heads = dot(after(h1, dy), w_h)
     qk = heads[:, : 2 * HK].reshape(nrow, row_len, 2 * HK)
     queries = rotate(qk[..., :HK], cosine, sine).astype(BF16)
@@ -283,20 +298,24 @@
     x2 = xf + plane.scatter(lambda a: dot(a, w_o), gated, w_u)
 
     hat2, scale2 = normed_rows(x2)
-    h2_parts, h2 = plane.gather_parts(hat2.astype(BF16))
+    h2_parts, h2_blocks = plane.gather_parts(hat2.astype(BF16))
     acts, slopes = zip(*[gelu_and_slope(dot(a, w_u)) for a in h2_parts])
-    act, slope = plane.joined(acts), plane.joined(slopes)
-    act, slope = lax.optimization_barrier((act, slope))
+    act = plane.joined(acts)
 
     down_parts = dot_tn(act, dy).astype(BF16)
     down_rows = summed_along(down_parts)
+    slope = plane.joined(lax.optimization_barrier((*slopes, down_parts))[:-1])
     d_hidden = (dot_nt(dy, w_d) * slope).astype(BF16)
-    d_hidden = after(d_hidden, down_parts)
-    up_parts = dot_tn(h2, d_hidden).astype(BF16)
-    t2 = plane.scatter(lambda a: dot_nt(a, w_u), d_hidden, up_parts)
+
+    def up_product(held):
+        return dot_tn(jnp.concatenate(held[:-1], axis=0), held[-1]).astype(BF16)
+
+    t2, up_parts = plane.scatter(
+        lambda a: dot_nt(a, w_u), d_hidden, late=(up_product, (*h2_blocks, d_hidden))
+    )
     up_rows = summed_along(up_parts)
     d_x2 = cotangent[0].astype(F32) + norm_back(t2, hat2, scale2)
-    d_branch_parts, d_branch = plane.gather_parts(after(d_x2.astype(BF16), down_rows))
+    d_branch_parts, d_branch_blocks = plane.gather_parts(after(d_x2.astype(BF16), down_rows))
     gate_slope = normed * sig * (1.0 + gate * (1.0 - sig))
     d_mixed, d_gate = [], []
     for part, at in zip(d_branch_parts, plane.parts_of(normed, swish, gate_slope, group_scale)):
@@ -323,7 +342,8 @@
         lambda a: dot_nt(a, w_h), after(d_heads, up_rows)
     )
     tokens_grad = d_x2 + norm_back(u1, hat1, scale1)
-    gated_last, _ = lax.optimization_barrier((gated, qkv_parts))
+    gated_last, *rest = lax.optimization_barrier((gated, *d_branch_blocks, qkv_parts))
+    d_branch = jnp.concatenate(rest[:-1], axis=0)
     out_rows = plane.out_back(dot_tn(gated_last, d_branch).astype(BF16), u1)
     output = x2 + plane.scatter(lambda a: dot(a, w_d), after(act, tokens_grad))
 

time: 559 us -> 553 us (0.989)
  blocking collectives: 31 us -> 0 us
  waiting for transfers between devices: 216 us -> 238 us
  local copies, waits for them, and re-layouts: 66.9 us -> 47 us
  starting transfers between devices: 61.8 us -> 76.9 us
  matrix products: 112 us -> 119 us
    all_to_all x1 -> x0, blocking collectives: 31 us -> none  [exchange(): return lax.all_to_all(v, TP, 0, 0, tiled=True)]
    ppermute x0 -> x5, waiting for transfers between devices: none -> 23.7 us  [hop(): return lax.ppermute(v, 'z', pairs)]
    all_gather x4 -> x3, waiting for transfers between devices: 42.1 us -> 20.2 us  [along(): return lax.all_gather(own, 'z', axis=0, tiled=True)]
    unnamed x217 -> x247, local copies, waits for them, and re-layouts: 46.6 us -> 29 us
    ppermute x49, waiting for transfers between devices: 114 us -> 127 us  [swap(): return lax.ppermute(v, TP, [(j, j ^ mask) for j in range(self.size)])]
    all_to_all x3 -> x5, waiting for transfers between devices: 22.4 us -> 33.7 us  [exchange(): return lax.all_to_all(v, TP, 0, 0, tiled=True)]
    all_to_all x3 -> x5, starting transfers between devices: 11.5 us -> 19.8 us  [exchange(): return lax.all_to_all(v, TP, 0, 0, tiled=True)]
    dot_general x17, matrix products: 45 us -> 52.9 us  [dot_nt(): lax.dot_general(a, b, (((1,), (1,)), ((), ())), preferred_element_type=F32)]
  transfers between devices with their start and end apart: 69 -> 75, of which waited for: 29 -> 34; matrix products, arithmetic and copies ran while one was open for 37% -> 34% of each run, Pallas kernels for 0% -> 0%
where the time goes in v3:
time: 553 us; the launch traced here: 545 us
  waiting for transfers between devices  238 us (43%)
  matrix products  119 us (22%)
  starting transfers between devices  76.9 us (14%)
  local copies, waits for them, and re-layouts  47 us (8%)
  other arithmetic  45.6 us (8%)
  between operations  19 us (3%)
    ppermute x49, waiting for transfers between devices, swap(): return lax.ppermute(v, TP, [(j, j ^ mask) for j in range(self.size)])  127 us
    dot_general x17, matrix products, dot_nt(): lax.dot_general(a, b, (((1,), (1,)), ((), ())), preferred_element_type=F32)  52.9 us
    ppermute x49, starting transfers between devices, swap(): return lax.ppermute(v, TP, [(j, j ^ mask) for j in range(self.size)])  36.1 us
    dot_general x17, matrix products, dot(): return jnp.dot(a, b, preferred_element_type=F32)  35.5 us
    all_to_all x5, waiting for transfers between devices, exchange(): return lax.all_to_all(v, TP, 0, 0, tiled=True)  33.7 us
    unnamed x247, local copies, waits for them, and re-layouts  29 us
    dot_general x5, matrix products, dot_tn(): lax.dot_general(a, b, (((0,), (0,)), ((), ())), preferred_element_type=F32)  25.4 us
    ppermute x5, waiting for transfers between devices, hop(): return lax.ppermute(v, 'z', pairs)  23.7 us
  transfers between devices with their start and end apart: 75, of which 34 were waited for; matrix products, arithmetic and copies ran while one was open for 34% of the time, Pallas kernels for 0%

profile of v3, /device:TPU:0, one launch (start us, length us, event | category | flops | bytes accessed | tf_op | source)
XLA Modules:
  0.0 544.6 jit_solution(12389092274727167029)
XLA Ops:
  13.1 9.3 %collective-permute-done.14 = bf16[128,2048]{1,0:T(8,128)(2,1)S(1)} collective-permute-done((bf16[128,2048]{1,0:T(8,128)(2,1)}, bf16[128,2048]{1,0:T(8,128)(2,1)S(1)}, u32[]{:S(2)}, u32[]{:S(2)}) %collective-permute-start.14) | collective-permute-done | bytes 524320 | tf_op jit(solution)/shard_map/ppermute | solution.py:64
  26.8 4.3 all-to-all-start
  40.4 10.5 %collective-permute-done.18 = bf16[128,2048]{1,0:T(8,128)(2,1)S(1)} collective-permute-done((bf16[128,2048]{1,0:T(8,128)(2,1)S(1)}, bf16[128,2048]{1,0:T(8,128)(2,1)S(1)}, u32[]{:S(2)}, u32[]{:S(2)}) %collective-permute-start.18) | collective-permute-done | bytes 524320 | tf_op jit(solution)/shard_map/ppermute | solution.py:64
  54.5 4.2 all-to-all-start.1
  59.0 8.5 %all-to-all-done.1 = bf16[8,64,512]{2,1,0:T(8,128)(2,1)} async-done(((bf16[8,64,512]{2,1,0:T(8,128)(2,1)}), bf16[8,64,512]{2,1,0:T(8,128)(2,1)}, u32[]{:S(2)}, u32[]{:S(2)}) %all-to-all-start.1) | async-done | bytes 524320 | tf_op jit(solution)/shard_map/all_to_all | solution.py:201
  72.5 8.4 %collective-permute-done.1 = bf16[128,2048]{1,0:T(8,128)(2,1)S(1)} collective-permute-done((bf16[128,2048]{1,0:T(8,128)(2,1)S(1)}, bf16[128,2048]{1,0:T(8,128)(2,1)S(1)}, u32[]{:S(2)}, u32[]{:S(2)}) %collective-permute-start.1) | collective-permute-done | bytes 524320 | tf_op jit(solution)/shard_map/ppermute | solution.py:98
  84.4 11.7 %collective-permute-done.5 = bf16[128,2048]{1,0:T(8,128)(2,1)S(1)} collective-permute-done((bf16[128,2048]{1,0:T(8,128)(2,1)S(1)}, bf16[128,2048]{1,0:T(8,128)(2,1)S(1)}, u32[]{:S(2)}, u32[]{:S(2)}) %collective-permute-start.5) | collective-permute-done | bytes 524320 | tf_op jit(solution)/shard_map/ppermute | solution.py:98
  103.9 8.2 %collective-permute-done.8 = bf16[128,2048]{1,0:T(8,128)(2,1)} collective-permute-done((bf16[128,2048]{1,0:T(8,128)(2,1)S(1)}, bf16[128,2048]{1,0:T(8,128)(2,1)}, u32[]{:S(2)}, u32[]{:S(2)}) %collective-permute-start.8) | collective-permute-done | bytes 524320 | tf_op jit(solution)/shard_map/ppermute | solution.py:98
  117.3 7.8 %collective-permute-done.12 = bf16[128,2048]{1,0:T(8,128)(2,1)S(1)} collective-permute-done((bf16[128,2048]{1,0:T(8,128)(2,1)S(1)}, bf16[128,2048]{1,0:T(8,128)(2,1)S(1)}, u32[]{:S(2)}, u32[]{:S(2)}) %collective-permute-start.12) | collective-permute-done | bytes 524320 | tf_op jit(solution)/shard_map/ppermute | solution.py:98
  140.6 14.7 %collective-permute-done.21 = bf16[128,2048]{1,0:T(8,128)(2,1)} collective-permute-done((bf16[128,2048]{1,0:T(8,128)(2,1)}, bf16[128,2048]{1,0:T(8,128)(2,1)}, u32[]{:S(2)}, u32[]{:S(2)}) %collective-permute-start.21) | collective-permute-done | bytes 524320 | tf_op jit(solution)/shard_map/ppermute | solution.py:182
  161.2 7.5 %all-gather.4.cloned.1.call-done = bf16[2048,1536]{1,0:T(8,128)(2,1)} async-done(((bf16[512,1536]{1,0:T(8,128)(2,1)}), bf16[2048,1536]{1,0:T(8,128)(2,1)}) %all-gather.4.cloned.1.call-update) | async-done | bytes 6291472 | tf_op jit(solution)/shard_map/all_gather | solution.py:53
  168.7 10.0 %fusion.212 = f32[1024,1536]{1,0:T(8,128)S(1)} fusion(bf16[1024,2048]{1,0:T(8,128)(2,1)} %copy-done.95, bf16[2048,1536]{1,0:T(8,128)(2,1)} %all-gather.4.cloned.1.call-done), kind=kOutput, calls=%fused_computation.395 | convolution fusion | flops 6442450944 | bytes 16777216 | tf_op jit(solution)/shard_map/dot_general | solution.py:23
  201.8 12.7 %all-gather.6.cloned.1.call-done = bf16[2048,512]{1,0:T(8,128)(2,1)} async-done(((bf16[512,512]{1,0:T(8,128)(2,1)}), bf16[2048,512]{1,0:T(8,128)(2,1)}) %all-gather.6.cloned.1.call-update) | async-done | bytes 2097168 | tf_op jit(solution)/shard_map/all_gather | solution.py:53
  214.5 6.2 %collective-permute-done.26 = bf16[128,2048]{1,0:T(8,128)(2,1)} collective-permute-done((bf16[128,2048]{1,0:T(8,128)(2,1)}, bf16[128,2048]{1,0:T(8,128)(2,1)}, u32[]{:S(2)}, u32[]{:S(2)}) %collective-permute-start.26) | collective-permute-done | bytes 524320 | tf_op jit(solution)/shard_map/ppermute | solution.py:98
  227.2 12.3 %collective-permute-done.34 = bf16[128,2048]{1,0:T(8,128)(2,1)S(1)} collective-permute-done((bf16[128,2048]{1,0:T(8,128)(2,1)S(1)}, bf16[128,2048]{1,0:T(8,128)(2,1)S(1)}, u32[]{:S(2)}, u32[]{:S(2)}) %collective-permute-start.34) | collective-permute-done | bytes 524320 | tf_op jit(solution)/shard_map/ppermute | solution.py:98
  239.6 9.0 %collective-permute-done.32 = bf16[128,2048]{1,0:T(8,128)(2,1)S(1)} collective-permute-done((bf16[128,2048]{1,0:T(8,128)(2,1)S(1)}, bf16[128,2048]{1,0:T(8,128)(2,1)S(1)}, u32[]{:S(2)}, u32[]{:S(2)}) %collective-permute-start.32) | collective-permute-done | bytes 524320 | tf_op jit(solution)/shard_map/ppermute | solution.py:98
  256.5 5.9 %convolution_convert_fusion.4 = bf16[512,2048]{1,0:T(8,128)(2,1)} fusion(bf16[1024,2048]{1,0:T(8,128)(2,1)} %constant_dynamic-update-slice_fusion.8, bf16[256,512]{1,0:T(8,128)(2,1)S(1)} %get-tuple-element.190, bf16[256,512]{1,0:T(8,128)(2,1)S(1)} %get-tuple-element.194, bf16[256,512]{1,0:T(8,128)(2,1)S(1)} %get-tuple-element.192, ...), kind=kOutput, calls=%fused_computation.4 | convolution fusion | flops 2152726528 | bytes 7340032 | tf_op jit(solution)/shard_map/dot_general | solution.py:31
  262.4 5.9 %fusion.5 = bf16[1024,512]{1,0:T(8,128)(2,1)S(1)} fusion(f32[256,512]{1,0:T(8,128)} %get-tuple-element.64, f32[256,512]{1,0:T(8,128)} %get-tuple-element.63, f32[256,512]{1,0:T(8,128)} %get-tuple-element.62, f32[256,512]{1,0:T(8,128)} %get-tuple-element.61, bf16[1024,2048]{1,0:T(8,128)(2,1)} %constant_dynamic-update-slice_fusion.8, ...), kind=kOutput, calls=%fused_computation.28 | convolution fusion | flops 2150105088 | bytes 9437184 | tf_op jit(solution)/shard_map/dot_general | solution.py:27
  298.3 10.5 %collective-permute-done.38 = bf16[128,2048]{1,0:T(8,128)(2,1)} collective-permute-done((bf16[128,2048]{1,0:T(8,128)(2,1)}, bf16[128,2048]{1,0:T(8,128)(2,1)}, u32[]{:S(2)}, u32[]{:S(2)}) %collective-permute-start.38) | collective-permute-done | bytes 524320 | tf_op jit(solution)/shard_map/ppermute | solution.py:98
  317.9 12.5 %collective-permute-done.46 = bf16[128,2048]{1,0:T(8,128)(2,1)} collective-permute-done((bf16[128,2048]{1,0:T(8,128)(2,1)}, bf16[128,2048]{1,0:T(8,128)(2,1)}, u32[]{:S(2)}, u32[]{:S(2)}) %collective-permute-start.46) | collective-permute-done | bytes 524320 | tf_op jit(solution)/shard_map/ppermute | solution.py:98
  330.3 9.8 %collective-permute-done.44 = bf16[128,2048]{1,0:T(8,128)(2,1)} collective-permute-done((bf16[128,2048]{1,0:T(8,128)(2,1)}, bf16[128,2048]{1,0:T(8,128)(2,1)}, u32[]{:S(2)}, u32[]{:S(2)}) %collective-permute-start.44) | collective-permute-done | bytes 524320 | tf_op jit(solution)/shard_map/ppermute | solution.py:98
  348.3 5.0 fusion.91
  375.3 9.5 %convolution_convert_fusion = bf16[2048,1024]{1,0:T(8,128)(2,1)} fusion(bf16[1024,2048]{1,0:T(8,128)(2,1)} %copy-done.95, bf16[1024,1024]{1,0:T(8,128)(2,1)} %pad_maximum_fusion.2), kind=kOutput, calls=%fused_computation | convolution fusion | flops 4297064448 | bytes 10485760 | tf_op jit(solution)/shard_map/dot_general | solution.py:31
  386.4 4.7 convolution_convert_fusion.12
  413.7 4.2 add_convert_fusion.3
  418.1 3.9 add_convert_fusion.4
  432.1 5.3 collective-permute-done.52
  438.1 11.0 %collective-permute-done.50 = bf16[128,2048]{1,0:T(8,128)(2,1)} collective-permute-done((bf16[128,2048]{1,0:T(8,128)(2,1)}, bf16[128,2048]{1,0:T(8,128)(2,1)}, u32[]{:S(2)}, u32[]{:S(2)}) %collective-permute-start.50) | collective-permute-done | bytes 524320 | tf_op jit(solution)/shard_map/ppermute | solution.py:98
  468.6 4.1 all-to-all-start.4
  475.1 19.6 %all-to-all-done.4 = bf16[8,64,512]{2,1,0:T(8,128)(2,1)} async-done(((bf16[8,64,512]{2,1,0:T(8,128)(2,1)}), bf16[8,64,512]{2,1,0:T(8,128)(2,1)}, u32[]{:S(2)}, u32[]{:S(2)}) %all-to-all-start.4) | async-done | bytes 524320 | tf_op jit(solution)/shard_map/all_to_all | solution.py:201
  501.4 5.6 %all-to-all-done.3 = bf16[8,64,512]{2,1,0:T(8,128)(2,1)S(1)} async-done(((bf16[8,64,512]{2,1,0:T(8,128)(2,1)}), bf16[8,64,512]{2,1,0:T(8,128)(2,1)S(1)}, u32[]{:S(2)}, u32[]{:S(2)}) %all-to-all-start.3) | async-done | bytes 524320 | tf_op jit(solution)/shard_map/all_to_all | solution.py:201
  517.0 13.2 %reduce-scatter.14.cloned.1.call-done = bf16[128,2048]{1,0:T(8,128)(2,1)} async-done(((bf16[512,2048]{1,0:T(8,128)(2,1)}), bf16[128,2048]{1,0:T(8,128)(2,1)}) %reduce-scatter.14.cloned.1.call-update) | async-done | bytes 524304 | tf_op jit(solution)/shard_map/reduce_scatter | solution.py:57
  (522 shorter events, 249.6 us)
Async XLA Ops:
  26.8 24.8 %all-to-all-start = ((bf16[8,64,1536]{2,1,0:T(8,128)(2,1)}), bf16[8,64,1536]{2,1,0:T(8,128)(2,1)}, u32[]{:S(2)}, u32[]{:S(2)}) async-start(bf16[8,64,1536]{2,1,0:T(8,128)(2,1)} %copy.49), calls=%async_computation | async-start | bytes 3145728 | tf_op jit(solution)/shard_map/all_to_all | solution.py:201
  31.2 137.5 %all-gather.4.cloned.1.call-start = ((), (), s32[]{:S(2)}) async-start(), calls=%async_computation.10 | async-start | bytes 7864320 | tf_op jit(solution)/shard_map/all_gather | solution.py:53
  58.7 155.8 %all-gather.6.cloned.1.call-start = ((), (), s32[]{:S(2)}) async-start(), calls=%async_computation.11 | async-start | bytes 2621440 | tf_op jit(solution)/shard_map/all_gather | solution.py:53
  69.0 64.2 %collective-permute-start.19 = (s32[4]{0:T(128)S(1)}, s32[4]{0:T(128)S(1)}, u32[]{:S(2)}, u32[]{:S(2)}) collective-permute-start(s32[4]{0:T(128)S(1)} %bitcast.224), channel_id=1, source_target_pairs={{0,4},{1,5},{2,6},{3,7},{4,0},{5,1},{6,2},{7,3},{8,12},{9,13},{10,... | collective-permute-start | bytes 56 | tf_op jit(solution)/shard_map/ppermute | solution.py:98
  71.1 24.9 %collective-permute-start.5 = (bf16[128,2048]{1,0:T(8,128)(2,1)S(1)}, bf16[128,2048]{1,0:T(8,128)(2,1)S(1)}, u32[]{:S(2)}, u32[]{:S(2)}) collective-permute-start(bf16[128,2048]{1,0:T(8,128)(2,1)S(1)} %fusion.14), channel_id=1, source_target_pairs={{0,6},{1,7},{2,4},{3,5},{4,2},{5,3},{6,0},{7,1},{8,14},{9,15},{10,... | collective-permute-start | bytes 1572872 | tf_op jit(solution)/shard_map/ppermute | solution.py:98
  102.5 22.6 %collective-permute-start.12 = (bf16[128,2048]{1,0:T(8,128)(2,1)S(1)}, bf16[128,2048]{1,0:T(8,128)(2,1)S(1)}, u32[]{:S(2)}, u32[]{:S(2)}) collective-permute-start(bf16[128,2048]{1,0:T(8,128)(2,1)S(1)} %bitcast.204), channel_id=1, source_target_pairs={{0,6},{1,7},{2,4},{3,5},{4,2},{5,3},{6,0},{7,1},{8,14},{9,15},{10,... | collective-permute-start | bytes 1572872 | tf_op jit(solution)/shard_map/ppermute | solution.py:98
  133.2 22.2 %collective-permute-start.21 = (bf16[128,2048]{1,0:T(8,128)(2,1)}, bf16[128,2048]{1,0:T(8,128)(2,1)}, u32[]{:S(2)}, u32[]{:S(2)}) collective-permute-start(bf16[128,2048]{1,0:T(8,128)(2,1)} %get-tuple-element.155), channel_id=1, source_target_pairs={{0,2},{1,0},{2,6},{3,4},{4,3},{5,1},{6,7},{7,5},{8,10},{9,8},{10,1... | collective-permute-start | bytes 1572872 | tf_op jit(solution)/shard_map/ppermute | solution.py:182
  136.6 21.9 %collective-permute-start.22 = (bf16[128,2048]{1,0:T(8,128)(2,1)}, bf16[128,2048]{1,0:T(8,128)(2,1)}, u32[]{:S(2)}, u32[]{:S(2)}) collective-permute-start(bf16[128,2048]{1,0:T(8,128)(2,1)} %get-tuple-element.154), channel_id=1, source_target_pairs={{0,4},{1,6},{2,0},{3,2},{4,5},{5,7},{6,1},{7,3},{8,12},{9,14},{10,... | collective-permute-start | bytes 1572872 | tf_op jit(solution)/shard_map/ppermute | solution.py:182
  138.0 124.4 %all-gather.8.cloned.1.call-start = ((), (), s32[]{:S(2)}) async-start(), calls=%async_computation.12 | async-start | bytes 2621440 | tf_op jit(solution)/shard_map/all_gather | solution.py:53
  138.0 23.1 %collective-permute-start.23 = (bf16[128,2048]{1,0:T(8,128)(2,1)}, bf16[128,2048]{1,0:T(8,128)(2,1)S(1)}, u32[]{:S(2)}, u32[]{:S(2)}) collective-permute-start(bf16[128,2048]{1,0:T(8,128)(2,1)} %get-tuple-element.153), channel_id=1, source_target_pairs={{0,6},{1,4},{2,2},{3,0},{4,7},{5,5},{6,3},{7,1},{8,14},{9,12},{10,... | collective-permute-start | bytes 1572872 | tf_op jit(solution)/shard_map/ppermute | solution.py:182
  192.7 21.7 %collective-permute-start.28 = (bf16[128,2048]{1,0:T(8,128)(2,1)}, bf16[128,2048]{1,0:T(8,128)(2,1)}, u32[]{:S(2)}, u32[]{:S(2)}) collective-permute-start(bf16[128,2048]{1,0:T(8,128)(2,1)} %fusion.2), channel_id=1, source_target_pairs={{0,2},{1,3},{2,0},{3,1},{4,6},{5,7},{6,4},{7,5},{8,10},{9,11},{10,... | collective-permute-start | bytes 1572872 | tf_op jit(solution)/shard_map/ppermute | solution.py:98
  198.2 22.5 %collective-permute-start.26 = (bf16[128,2048]{1,0:T(8,128)(2,1)}, bf16[128,2048]{1,0:T(8,128)(2,1)}, u32[]{:S(2)}, u32[]{:S(2)}) collective-permute-start(bf16[128,2048]{1,0:T(8,128)(2,1)} %fusion), channel_id=1, source_target_pairs={{0,6},{1,7},{2,4},{3,5},{4,2},{5,3},{6,0},{7,1},{8,14},{9,15},{10,... | collective-permute-start | bytes 1572872 | tf_op jit(solution)/shard_map/ppermute | solution.py:98
  198.8 115.5 %reduce-scatter.6.cloned.1.call-start = ((), (), s32[]{:S(2)}) async-start(), calls=%async_computation.13 | async-start | bytes 2621440 | tf_op jit(solution)/shard_map/reduce_scatter | solution.py:57
  226.1 22.4 %collective-permute-start.32 = (bf16[128,2048]{1,0:T(8,128)(2,1)S(1)}, bf16[128,2048]{1,0:T(8,128)(2,1)S(1)}, u32[]{:S(2)}, u32[]{:S(2)}) collective-permute-start(bf16[128,2048]{1,0:T(8,128)(2,1)S(1)} %fusion.60), channel_id=1, source_target_pairs={{0,4},{1,5},{2,6},{3,7},{4,0},{5,1},{6,2},{7,3},{8,12},{9,13},{10,... | collective-permute-start | bytes 1572872 | tf_op jit(solution)/shard_map/ppermute | solution.py:98
  226.7 21.9 %collective-permute-start.30 = (bf16[128,2048]{1,0:T(8,128)(2,1)S(1)}, bf16[128,2048]{1,0:T(8,128)(2,1)S(1)}, u32[]{:S(2)}, u32[]{:S(2)}) collective-permute-start(bf16[128,2048]{1,0:T(8,128)(2,1)S(1)} %fusion.60), channel_id=1, source_target_pairs={{0,2},{1,3},{2,0},{3,1},{4,6},{5,7},{6,4},{7,5},{8,10},{9,11},{10,... | collective-permute-start | bytes 1572872 | tf_op jit(solution)/shard_map/ppermute | solution.py:98
  227.2 21.8 %collective-permute-start.29 = (bf16[128,2048]{1,0:T(8,128)(2,1)S(1)}, bf16[128,2048]{1,0:T(8,128)(2,1)S(1)}, u32[]{:S(2)}, u32[]{:S(2)}) collective-permute-start(bf16[128,2048]{1,0:T(8,128)(2,1)S(1)} %fusion.60), channel_id=1, source_target_pairs={{0,1},{1,0},{2,3},{3,2},{4,5},{5,4},{6,7},{7,6},{8,9},{9,8},{10,11... | collective-permute-start | bytes 1572872 | tf_op jit(solution)/shard_map/ppermute | solution.py:98
  272.4 103.0 %reduce-scatter.8.cloned.1.call-start = ((), (), s32[]{:S(2)}) async-start(), calls=%async_computation.14 | async-start | bytes 2621440 | tf_op jit(solution)/shard_map/reduce_scatter | solution.py:57
  284.7 24.1 %collective-permute-start.38 = (bf16[128,2048]{1,0:T(8,128)(2,1)}, bf16[128,2048]{1,0:T(8,128)(2,1)}, u32[]{:S(2)}, u32[]{:S(2)}) collective-permute-start(bf16[128,2048]{1,0:T(8,128)(2,1)} %add_convert_fusion.8), channel_id=1, source_target_pairs={{0,6},{1,7},{2,4},{3,5},{4,2},{5,3},{6,0},{7,1},{8,14},{9,15},{10,... | collective-permute-start | bytes 1572872 | tf_op jit(solution)/shard_map/ppermute | solution.py:98
  316.6 23.6 %collective-permute-start.44 = (bf16[128,2048]{1,0:T(8,128)(2,1)}, bf16[128,2048]{1,0:T(8,128)(2,1)}, u32[]{:S(2)}, u32[]{:S(2)}) collective-permute-start(bf16[128,2048]{1,0:T(8,128)(2,1)} %get-tuple-element.85), channel_id=1, source_target_pairs={{0,4},{1,5},{2,6},{3,7},{4,0},{5,1},{6,2},{7,3},{8,12},{9,13},{10,... | collective-permute-start | bytes 1572872 | tf_op jit(solution)/shard_map/ppermute | solution.py:98
  317.1 157.9 %reduce-scatter.12.cloned.1.call-start = ((), (), s32[]{:S(2)}) async-start(), calls=%async_computation.16 | async-start | bytes 2621440 | tf_op jit(solution)/shard_map/reduce_scatter | solution.py:57
  317.2 25.7 %collective-permute-start.42 = (bf16[128,2048]{1,0:T(8,128)(2,1)}, bf16[128,2048]{1,0:T(8,128)(2,1)S(1)}, u32[]{:S(2)}, u32[]{:S(2)}) collective-permute-start(bf16[128,2048]{1,0:T(8,128)(2,1)} %get-tuple-element.85), channel_id=1, source_target_pairs={{0,2},{1,3},{2,0},{3,1},{4,6},{5,7},{6,4},{7,5},{8,10},{9,11},{10,... | collective-permute-start | bytes 1572872 | tf_op jit(solution)/shard_map/ppermute | solution.py:98
  358.2 143.1 %reduce-scatter.10.cloned.1.call-start = ((), (), s32[]{:S(2)}) async-start(), calls=%async_computation.15 | async-start | bytes 5242880 | tf_op jit(solution)/shard_map/reduce_scatter | solution.py:57
  384.9 145.3 %reduce-scatter.14.cloned.1.call-start = ((), (), s32[]{:S(2)}) async-start(), calls=%async_computation.17 | async-start | bytes 2621440 | tf_op jit(solution)/shard_map/reduce_scatter | solution.py:57
  391.2 22.5 %collective-permute-start.48 = (bf16[256,2048]{1,0:T(8,128)(2,1)S(1)}, bf16[256,2048]{1,0:T(8,128)(2,1)S(1)}, u32[]{:S(2)}, u32[]{:S(2)}) collective-permute-start(bf16[256,2048]{1,0:T(8,128)(2,1)S(1)} %convolution_convert_fusion.12), channel_id=1, source_target_pairs={{0,1},{1,0},{2,3},{3,2},{4,5},{5,4},{6,7},{7,6},{8,9},{9,8},{10,11... | collective-permute-start | bytes 3145736 | tf_op jit(solution)/shard_map/ppermute | solution.py:98
  403.9 25.1 %collective-permute-start.59 = (bf16[128,2048]{1,0:T(8,128)(2,1)S(1)}, bf16[128,2048]{1,0:T(8,128)(2,1)S(1)}, u32[]{:S(2)}, u32[]{:S(2)}) collective-permute-start(bf16[128,2048]{1,0:T(8,128)(2,1)S(1)} %get-tuple-element.137), channel_id=1, source_target_pairs={{2,0},{0,1},{6,2},{4,3},{3,4},{1,5},{7,6},{5,7},{10,8},{8,9},{14,1... | collective-permute-start | bytes 1572872 | tf_op jit(solution)/shard_map/ppermute | solution.py:196
  404.0 26.4 %collective-permute-start.60 = (bf16[128,2048]{1,0:T(8,128)(2,1)S(1)}, bf16[128,2048]{1,0:T(8,128)(2,1)S(1)}, u32[]{:S(2)}, u32[]{:S(2)}) collective-permute-start(bf16[128,2048]{1,0:T(8,128)(2,1)S(1)} %get-tuple-element.136), channel_id=1, source_target_pairs={{4,0},{6,1},{0,2},{2,3},{5,4},{7,5},{1,6},{3,7},{12,8},{14,9},{8,1... | collective-permute-start | bytes 1572872 | tf_op jit(solution)/shard_map/ppermute | solution.py:196
  409.1 22.2 %collective-permute-start.61 = (bf16[128,2048]{1,0:T(8,128)(2,1)S(1)}, bf16[128,2048]{1,0:T(8,128)(2,1)S(1)}, u32[]{:S(2)}, u32[]{:S(2)}) collective-permute-start(bf16[128,2048]{1,0:T(8,128)(2,1)S(1)} %get-tuple-element.135), channel_id=1, source_target_pairs={{6,0},{4,1},{2,2},{0,3},{7,4},{5,5},{3,6},{1,7},{14,8},{12,9},{10,... | collective-permute-start | bytes 1572872 | tf_op jit(solution)/shard_map/ppermute | solution.py:196
  460.8 37.4 %collective-permute-start.57 = (bf16[128,2048]{1,0:T(8,128)(2,1)}, bf16[128,2048]{1,0:T(8,128)(2,1)}, u32[]{:S(2)}, u32[]{:S(2)}) collective-permute-start(bf16[128,2048]{1,0:T(8,128)(2,1)} %add_convert_fusion), channel_id=1, source_target_pairs={{0,2},{1,3},{2,0},{3,1},{4,6},{5,7},{6,4},{7,5},{8,10},{9,11},{10,... | collective-permute-start | bytes 1572872 | tf_op jit(solution)/shard_map/ppermute | solution.py:98
  463.9 34.4 %collective-permute-start.56 = (bf16[128,2048]{1,0:T(8,128)(2,1)}, bf16[128,2048]{1,0:T(8,128)(2,1)}, u32[]{:S(2)}, u32[]{:S(2)}) collective-permute-start(bf16[128,2048]{1,0:T(8,128)(2,1)} %add_convert_fusion.1), channel_id=1, source_target_pairs={{0,4},{1,5},{2,6},{3,7},{4,0},{5,1},{6,2},{7,3},{8,12},{9,13},{10,... | collective-permute-start | bytes 1572872 | tf_op jit(solution)/shard_map/ppermute | solution.py:98
  467.2 31.0 %collective-permute-start.55 = (bf16[128,2048]{1,0:T(8,128)(2,1)}, bf16[128,2048]{1,0:T(8,128)(2,1)}, u32[]{:S(2)}, u32[]{:S(2)}) collective-permute-start(bf16[128,2048]{1,0:T(8,128)(2,1)} %add_convert_fusion.2), channel_id=1, source_target_pairs={{0,6},{1,7},{2,4},{3,5},{4,2},{5,3},{6,0},{7,1},{8,14},{9,15},{10,... | collective-permute-start | bytes 1572872 | tf_op jit(solution)/shard_map/ppermute | solution.py:98
  468.6 26.1 %all-to-all-start.4 = ((bf16[8,64,512]{2,1,0:T(8,128)(2,1)}), bf16[8,64,512]{2,1,0:T(8,128)(2,1)}, u32[]{:S(2)}, u32[]{:S(2)}) async-start(bf16[8,64,512]{2,1,0:T(8,128)(2,1)} %bitcast.215), calls=%async_computation.9 | async-start | bytes 1048576 | tf_op jit(solution)/shard_map/all_to_all | solution.py:201
  507.0 25.4 %all-to-all-start.2 = ((bf16[8,64,1024]{2,1,0:T(8,128)(2,1)}), bf16[8,64,1024]{2,1,0:T(8,128)(2,1)S(1)}, u32[]{:S(2)}, u32[]{:S(2)}) async-start(bf16[8,64,1024]{2,1,0:T(8,128)(2,1)} %bitcast.211), calls=%async_computation.5 | async-start | bytes 2097152 | tf_op jit(solution)/shard_map/all_to_all | solution.py:201
  (146 other events, 1049.5 us)
Sparse Core Ops, SparseCore 0:
  51.8 116.8 all-gather.3
  170.2 44.1 all-gather.5
  216.0 44.6 all-gather.7
  272.5 41.7 reduce-scatter.5
  317.3 42.3 reduce-scatter.7
  361.8 43.1 reduce-scatter.11
  407.4 76.0 reduce-scatter.9
  485.8 44.3 reduce-scatter.13

commit v4 on v3

--- a/solution.py
+++ b/solution.py
@@ -121,7 +121,7 @@
         rows = left.shape[0] // 8
         blocks = [left[i * rows : (i + 1) * rows] for i in range(8)]
         come = {}
-        for pair in ((6, 4), (2, 0)):
+        for pair in ((6,), (4,), (2,), (0,)):
             away = product(jnp.concatenate([blocks[m ^ 1] for m in pair], axis=0)).astype(BF16)
             away = self.swap(away, 1)
             for i, m in enumerate(pair):
@@ -143,9 +143,10 @@
         if not self.fast:
             whole = self.gather(own)
             return [whole], [whole]
-        held = {0: own}
-        for mask in (6, 4, 2):
-            held[mask] = self.swap(own, mask)
+        held = {0: own, 4: self.swap(own, 4), 2: self.swap(own, 2)}
+        half = own.shape[0] // 2
+        by_y, by_x = self.swap(held[4][:half], 2), self.swap(held[2][half:], 4)
+        held[6] = jnp.concatenate([by_y, by_x], axis=0)
         for mask in (0, 4, 2, 6):
             held[mask ^ 1] = self.swap(held[mask], 1)
         parts = [jnp.concatenate([held[m], held[m + 1]], axis=0) for m in (0, 4, 2, 6)]
@@ -324,7 +325,9 @@
         d_gate.append((d_gated * slope_at).astype(BF16))
         d_mixed.append(norm_back(d_gated * swish_at, n_at, scale_at).astype(BF16))
     d_mixed, d_gate = plane.joined(d_mixed), plane.joined(d_gate)
-    g_rows = summed_along(dot_tn(h1, d_gate))
+    g_parts = dot_tn(h1, d_gate).astype(BF16)
+    g_rows = summed_along(g_parts)
+    d_mixed = after(d_mixed, g_parts)
     d_mixed = d_mixed.reshape(nrow, row_len, HV)
     d_values = jnp.einsum("rnm,rne->rme", weights, d_mixed, preferred_element_type=F32)
     d_values = d_values.astype(BF16).reshape(-1, HV)

time: 553 us -> 545 us (0.986)
  waiting for transfers between devices: 238 us -> 216 us
  starting transfers between devices: 76.9 us -> 83.5 us
    ppermute x49 -> x59, waiting for transfers between devices: 127 us -> 109 us  [swap(): return lax.ppermute(v, TP, [(j, j ^ mask) for j in range(self.size)])]
    reduce_scatter x5, waiting for transfers between devices: 14.8 us -> 6.29 us  [summed_along(): lax.psum_scatter(parts.astype(BF16), 'z', scatter_dimension=0, tiled=True)]
    ppermute x49 -> x59, starting transfers between devices: 36.1 us -> 40.7 us  [swap(): return lax.ppermute(v, TP, [(j, j ^ mask) for j in range(self.size)])]
    dot_general x17 -> x21, matrix products: 52.9 us -> 57.4 us  [dot_nt(): lax.dot_general(a, b, (((1,), (1,)), ((), ())), preferred_element_type=F32)]
    dot_general x17 -> x21, matrix products: 35.5 us -> 34.2 us  [dot(): return jnp.dot(a, b, preferred_element_type=F32)]
    unnamed x247 -> x241, local copies, waits for them, and re-layouts: 29 us -> 29.5 us
  transfers between devices with their start and end apart: 75 -> 85, of which waited for: 34 -> 33; matrix products, arithmetic and copies ran while one was open for 34% -> 37% of each run, Pallas kernels for 0% -> 0%
where the time goes in v4:
time: 545 us; the launch traced here: 536 us
  waiting for transfers between devices  216 us (40%)
  matrix products  122 us (22%)
  starting transfers between devices  83.5 us (15%)
  other arithmetic  48.3 us (9%)
  local copies, waits for them, and re-layouts  47.2 us (9%)
  between operations  19.3 us (4%)
    ppermute x59, waiting for transfers between devices, swap(): return lax.ppermute(v, TP, [(j, j ^ mask) for j in range(self.size)])  109 us
    dot_general x21, matrix products, dot_nt(): lax.dot_general(a, b, (((1,), (1,)), ((), ())), preferred_element_type=F32)  57.4 us
    ppermute x59, starting transfers between devices, swap(): return lax.ppermute(v, TP, [(j, j ^ mask) for j in range(self.size)])  40.7 us
    all_to_all x5, waiting for transfers between devices, exchange(): return lax.all_to_all(v, TP, 0, 0, tiled=True)  34.6 us
    dot_general x21, matrix products, dot(): return jnp.dot(a, b, preferred_element_type=F32)  34.2 us
    unnamed x241, local copies, waits for them, and re-layouts  29.5 us
    dot_general x5, matrix products, dot_tn(): lax.dot_general(a, b, (((0,), (0,)), ((), ())), preferred_element_type=F32)  24.5 us
    ppermute x5, waiting for transfers between devices, hop(): return lax.ppermute(v, 'z', pairs)  23.8 us
  transfers between devices with their start and end apart: 85, of which 33 were waited for; matrix products, arithmetic and copies ran while one was open for 37% of the time, Pallas kernels for 0%

profile of v4, /device:TPU:0, one launch (start us, length us, event | category | flops | bytes accessed | tf_op | source)
XLA Modules:
  0.0 536.1 jit_solution(3670466746928016883)
XLA Ops:
  13.1 9.3 %collective-permute-done.14 = bf16[128,2048]{1,0:T(8,128)(2,1)S(1)} collective-permute-done((bf16[128,2048]{1,0:T(8,128)(2,1)}, bf16[128,2048]{1,0:T(8,128)(2,1)S(1)}, u32[]{:S(2)}, u32[]{:S(2)}) %collective-permute-start.14) | collective-permute-done | bytes 524320 | tf_op jit(solution)/shard_map/ppermute | solution.py:64
  26.8 4.3 all-to-all-start
  40.4 10.5 %collective-permute-done.18 = bf16[128,2048]{1,0:T(8,128)(2,1)S(1)} collective-permute-done((bf16[128,2048]{1,0:T(8,128)(2,1)S(1)}, bf16[128,2048]{1,0:T(8,128)(2,1)S(1)}, u32[]{:S(2)}, u32[]{:S(2)}) %collective-permute-start.18) | collective-permute-done | bytes 524320 | tf_op jit(solution)/shard_map/ppermute | solution.py:64
  54.6 4.2 all-to-all-start.1
  59.2 8.5 %all-to-all-done.1 = bf16[8,64,512]{2,1,0:T(8,128)(2,1)} async-done(((bf16[8,64,512]{2,1,0:T(8,128)(2,1)}), bf16[8,64,512]{2,1,0:T(8,128)(2,1)}, u32[]{:S(2)}, u32[]{:S(2)}) %all-to-all-start.1) | async-done | bytes 524320 | tf_op jit(solution)/shard_map/all_to_all | solution.py:202
  72.7 8.4 %collective-permute-done.1 = bf16[128,2048]{1,0:T(8,128)(2,1)S(1)} collective-permute-done((bf16[128,2048]{1,0:T(8,128)(2,1)S(1)}, bf16[128,2048]{1,0:T(8,128)(2,1)S(1)}, u32[]{:S(2)}, u32[]{:S(2)}) %collective-permute-start.1) | collective-permute-done | bytes 524320 | tf_op jit(solution)/shard_map/ppermute | solution.py:98
  84.5 11.7 %collective-permute-done.5 = bf16[128,2048]{1,0:T(8,128)(2,1)S(1)} collective-permute-done((bf16[128,2048]{1,0:T(8,128)(2,1)S(1)}, bf16[128,2048]{1,0:T(8,128)(2,1)S(1)}, u32[]{:S(2)}, u32[]{:S(2)}) %collective-permute-start.5) | collective-permute-done | bytes 524320 | tf_op jit(solution)/shard_map/ppermute | solution.py:98
  104.1 8.2 %collective-permute-done.8 = bf16[128,2048]{1,0:T(8,128)(2,1)} collective-permute-done((bf16[128,2048]{1,0:T(8,128)(2,1)S(1)}, bf16[128,2048]{1,0:T(8,128)(2,1)}, u32[]{:S(2)}, u32[]{:S(2)}) %collective-permute-start.8) | collective-permute-done | bytes 524320 | tf_op jit(solution)/shard_map/ppermute | solution.py:98
  117.5 7.8 %collective-permute-done.12 = bf16[128,2048]{1,0:T(8,128)(2,1)S(1)} collective-permute-done((bf16[128,2048]{1,0:T(8,128)(2,1)S(1)}, bf16[128,2048]{1,0:T(8,128)(2,1)S(1)}, u32[]{:S(2)}, u32[]{:S(2)}) %collective-permute-start.12) | collective-permute-done | bytes 524320 | tf_op jit(solution)/shard_map/ppermute | solution.py:98
  140.7 14.8 %collective-permute-done.21 = bf16[128,2048]{1,0:T(8,128)(2,1)} collective-permute-done((bf16[128,2048]{1,0:T(8,128)(2,1)}, bf16[128,2048]{1,0:T(8,128)(2,1)}, u32[]{:S(2)}, u32[]{:S(2)}) %collective-permute-start.21) | collective-permute-done | bytes 524320 | tf_op jit(solution)/shard_map/ppermute | solution.py:183
  161.4 7.3 %all-gather.4.cloned.1.call-done = bf16[2048,1536]{1,0:T(8,128)(2,1)} async-done(((bf16[512,1536]{1,0:T(8,128)(2,1)}), bf16[2048,1536]{1,0:T(8,128)(2,1)}) %all-gather.4.cloned.1.call-update) | async-done | bytes 6291472 | tf_op jit(solution)/shard_map/all_gather | solution.py:53
  168.7 10.0 %fusion.196 = f32[1024,1536]{1,0:T(8,128)S(1)} fusion(bf16[1024,2048]{1,0:T(8,128)(2,1)} %copy-done.89, bf16[2048,1536]{1,0:T(8,128)(2,1)} %all-gather.4.cloned.1.call-done), kind=kOutput, calls=%fused_computation.391 | convolution fusion | flops 6442450944 | bytes 16777216 | tf_op jit(solution)/shard_map/dot_general | solution.py:23
  201.8 12.6 %all-gather.6.cloned.1.call-done = bf16[2048,512]{1,0:T(8,128)(2,1)} async-done(((bf16[512,512]{1,0:T(8,128)(2,1)}), bf16[2048,512]{1,0:T(8,128)(2,1)}) %all-gather.6.cloned.1.call-update) | async-done | bytes 2097168 | tf_op jit(solution)/shard_map/all_gather | solution.py:53
  214.4 6.4 %collective-permute-done.26 = bf16[128,2048]{1,0:T(8,128)(2,1)} collective-permute-done((bf16[128,2048]{1,0:T(8,128)(2,1)}, bf16[128,2048]{1,0:T(8,128)(2,1)}, u32[]{:S(2)}, u32[]{:S(2)}) %collective-permute-start.26) | collective-permute-done | bytes 524320 | tf_op jit(solution)/shard_map/ppermute | solution.py:98
  226.9 9.6 %collective-permute-done.34 = bf16[128,2048]{1,0:T(8,128)(2,1)S(1)} collective-permute-done((bf16[128,2048]{1,0:T(8,128)(2,1)S(1)}, bf16[128,2048]{1,0:T(8,128)(2,1)S(1)}, u32[]{:S(2)}, u32[]{:S(2)}) %collective-permute-start.34) | collective-permute-done | bytes 524320 | tf_op jit(solution)/shard_map/ppermute | solution.py:98
  250.4 6.0 %convolution_convert_fusion.4 = bf16[512,2048]{1,0:T(8,128)(2,1)} fusion(bf16[1024,2048]{1,0:T(8,128)(2,1)} %constant_dynamic-update-slice_fusion.8, bf16[256,512]{1,0:T(8,128)(2,1)S(1)} %get-tuple-element.176, bf16[256,512]{1,0:T(8,128)(2,1)S(1)} %get-tuple-element.180, bf16[256,512]{1,0:T(8,128)(2,1)S(1)} %get-tuple-element.178, ...), kind=kOutput, calls=%fused_computation.4 | convolution fusion | flops 2152726528 | bytes 7340032 | tf_op jit(solution)/shard_map/dot_general | solution.py:31
  260.6 5.9 %fusion.5 = bf16[1024,512]{1,0:T(8,128)(2,1)S(1)} fusion(f32[256,512]{1,0:T(8,128)} %get-tuple-element.65, f32[256,512]{1,0:T(8,128)} %get-tuple-element.64, f32[256,512]{1,0:T(8,128)} %get-tuple-element.63, f32[256,512]{1,0:T(8,128)} %get-tuple-element.62, bf16[1024,2048]{1,0:T(8,128)(2,1)} %constant_dynamic-update-slice_fusion.8, ...), kind=kOutput, calls=%fused_computation.36 | convolution fusion | flops 2150105088 | bytes 9437184 | tf_op jit(solution)/shard_map/dot_general | solution.py:27
  292.6 9.9 %collective-permute-done.43 = bf16[128,2048]{1,0:T(8,128)(2,1)} collective-permute-done((bf16[128,2048]{1,0:T(8,128)(2,1)}, bf16[128,2048]{1,0:T(8,128)(2,1)}, u32[]{:S(2)}, u32[]{:S(2)}) %collective-permute-start.43) | collective-permute-done | bytes 524320 | tf_op jit(solution)/shard_map/ppermute | solution.py:98
  309.6 9.8 %collective-permute-done.49 = bf16[128,2048]{1,0:T(8,128)(2,1)} collective-permute-done((bf16[128,2048]{1,0:T(8,128)(2,1)}, bf16[128,2048]{1,0:T(8,128)(2,1)}, u32[]{:S(2)}, u32[]{:S(2)}) %collective-permute-start.49) | collective-permute-done | bytes 524320 | tf_op jit(solution)/shard_map/ppermute | solution.py:98
  334.8 5.1 fusion.89
  360.4 8.4 %convolution_convert_fusion = bf16[2048,1024]{1,0:T(8,128)(2,1)} fusion(bf16[1024,2048]{1,0:T(8,128)(2,1)} %copy-done.89, bf16[1024,1024]{1,0:T(8,128)(2,1)S(1)} %pad_maximum_fusion.2), kind=kOutput, calls=%fused_computation | convolution fusion | flops 4297064448 | bytes 10485760 | tf_op jit(solution)/shard_map/dot_general | solution.py:31
  372.8 5.5 %convolution_convert_fusion.9 = bf16[128,2048]{1,0:T(8,128)(2,1)S(1)} fusion(bf16[2048,1536]{1,0:T(8,128)(2,1)} %all-gather.4.cloned.1.call-done, bf16[1024,1536]{1,0:T(8,128)(2,1)} %fusion.109), kind=kOutput, calls=%fused_computation.18 | convolution fusion | flops 805568512 | bytes 7208960 | tf_op jit(solution)/shard_map/dot_general | solution.py:27
  396.1 4.1 fusion.106
  402.9 4.0 add_convert_fusion.3
  407.2 4.0 add_convert_fusion.4
  414.7 3.9 add_convert_fusion.5
  427.2 7.3 %collective-permute-done.60 = bf16[128,2048]{1,0:T(8,128)(2,1)S(1)} collective-permute-done((bf16[128,2048]{1,0:T(8,128)(2,1)}, bf16[128,2048]{1,0:T(8,128)(2,1)S(1)}, u32[]{:S(2)}, u32[]{:S(2)}) %collective-permute-start.60) | collective-permute-done | bytes 524320 | tf_op jit(solution)/shard_map/ppermute | solution.py:98
  435.8 12.2 %collective-permute-done.56 = bf16[128,2048]{1,0:T(8,128)(2,1)} collective-permute-done((bf16[128,2048]{1,0:T(8,128)(2,1)}, bf16[128,2048]{1,0:T(8,128)(2,1)}, u32[]{:S(2)}, u32[]{:S(2)}) %collective-permute-start.56) | collective-permute-done | bytes 524320 | tf_op jit(solution)/shard_map/ppermute | solution.py:98
  465.2 4.2 all-to-all-start.4
  471.7 20.5 %all-to-all-done.4 = bf16[8,64,512]{2,1,0:T(8,128)(2,1)} async-done(((bf16[8,64,512]{2,1,0:T(8,128)(2,1)}), bf16[8,64,512]{2,1,0:T(8,128)(2,1)}, u32[]{:S(2)}, u32[]{:S(2)}) %all-to-all-start.4) | async-done | bytes 524320 | tf_op jit(solution)/shard_map/all_to_all | solution.py:202
  498.9 5.6 %all-to-all-done.3 = bf16[8,64,512]{2,1,0:T(8,128)(2,1)S(1)} async-done(((bf16[8,64,512]{2,1,0:T(8,128)(2,1)}), bf16[8,64,512]{2,1,0:T(8,128)(2,1)S(1)}, u32[]{:S(2)}, u32[]{:S(2)}) %all-to-all-start.3) | async-done | bytes 524320 | tf_op jit(solution)/shard_map/all_to_all | solution.py:202
  515.1 6.3 %reduce-scatter.14.cloned.1.call-done = bf16[128,2048]{1,0:T(8,128)(2,1)} async-done(((bf16[512,2048]{1,0:T(8,128)(2,1)}), bf16[128,2048]{1,0:T(8,128)(2,1)}) %reduce-scatter.14.cloned.1.call-update) | async-done | bytes 524304 | tf_op jit(solution)/shard_map/reduce_scatter | solution.py:57
  (546 shorter events, 260.6 us)
Async XLA Ops:
  26.8 24.8 %all-to-all-start = ((bf16[8,64,1536]{2,1,0:T(8,128)(2,1)}), bf16[8,64,1536]{2,1,0:T(8,128)(2,1)}, u32[]{:S(2)}, u32[]{:S(2)}) async-start(bf16[8,64,1536]{2,1,0:T(8,128)(2,1)} %copy.49), calls=%async_computation | async-start | bytes 3145728 | tf_op jit(solution)/shard_map/all_to_all | solution.py:202
  31.1 137.5 %all-gather.4.cloned.1.call-start = ((), (), s32[]{:S(2)}) async-start(), calls=%async_computation.10 | async-start | bytes 7864320 | tf_op jit(solution)/shard_map/all_gather | solution.py:53
  31.9 19.0 %collective-permute-start.18 = (bf16[128,2048]{1,0:T(8,128)(2,1)S(1)}, bf16[128,2048]{1,0:T(8,128)(2,1)S(1)}, u32[]{:S(2)}, u32[]{:S(2)}) collective-permute-start(bf16[128,2048]{1,0:T(8,128)(2,1)S(1)} %collective-permute-done.17), channel_id=1, source_target_pairs={{8,0},{16,24},{9,1},{17,25},{10,2},{18,26},{11,3},{19,27},{12,4},{... | collective-permute-start | bytes 1572872 | tf_op jit(solution)/shard_map/ppermute | solution.py:64
  58.8 155.6 %all-gather.6.cloned.1.call-start = ((), (), s32[]{:S(2)}) async-start(), calls=%async_computation.11 | async-start | bytes 2621440 | tf_op jit(solution)/shard_map/all_gather | solution.py:53
  69.1 64.2 %collective-permute-start.19 = (s32[4]{0:T(128)S(1)}, s32[4]{0:T(128)S(1)}, u32[]{:S(2)}, u32[]{:S(2)}) collective-permute-start(s32[4]{0:T(128)S(1)} %bitcast.230), channel_id=1, source_target_pairs={{0,4},{1,5},{2,6},{3,7},{4,0},{5,1},{6,2},{7,3},{8,12},{9,13},{10,... | collective-permute-start | bytes 56 | tf_op jit(solution)/shard_map/ppermute | solution.py:98
  71.2 24.9 %collective-permute-start.5 = (bf16[128,2048]{1,0:T(8,128)(2,1)S(1)}, bf16[128,2048]{1,0:T(8,128)(2,1)S(1)}, u32[]{:S(2)}, u32[]{:S(2)}) collective-permute-start(bf16[128,2048]{1,0:T(8,128)(2,1)S(1)} %fusion.14), channel_id=1, source_target_pairs={{0,6},{1,7},{2,4},{3,5},{4,2},{5,3},{6,0},{7,1},{8,14},{9,15},{10,... | collective-permute-start | bytes 1572872 | tf_op jit(solution)/shard_map/ppermute | solution.py:98
  102.6 22.6 %collective-permute-start.12 = (bf16[128,2048]{1,0:T(8,128)(2,1)S(1)}, bf16[128,2048]{1,0:T(8,128)(2,1)S(1)}, u32[]{:S(2)}, u32[]{:S(2)}) collective-permute-start(bf16[128,2048]{1,0:T(8,128)(2,1)S(1)} %bitcast.210), channel_id=1, source_target_pairs={{0,6},{1,7},{2,4},{3,5},{4,2},{5,3},{6,0},{7,1},{8,14},{9,15},{10,... | collective-permute-start | bytes 1572872 | tf_op jit(solution)/shard_map/ppermute | solution.py:98
  133.4 22.2 %collective-permute-start.21 = (bf16[128,2048]{1,0:T(8,128)(2,1)}, bf16[128,2048]{1,0:T(8,128)(2,1)}, u32[]{:S(2)}, u32[]{:S(2)}) collective-permute-start(bf16[128,2048]{1,0:T(8,128)(2,1)} %get-tuple-element.153), channel_id=1, source_target_pairs={{0,2},{1,0},{2,6},{3,4},{4,3},{5,1},{6,7},{7,5},{8,10},{9,8},{10,1... | collective-permute-start | bytes 1572872 | tf_op jit(solution)/shard_map/ppermute | solution.py:183
  136.8 21.9 %collective-permute-start.22 = (bf16[128,2048]{1,0:T(8,128)(2,1)}, bf16[128,2048]{1,0:T(8,128)(2,1)}, u32[]{:S(2)}, u32[]{:S(2)}) collective-permute-start(bf16[128,2048]{1,0:T(8,128)(2,1)} %get-tuple-element.152), channel_id=1, source_target_pairs={{0,4},{1,6},{2,0},{3,2},{4,5},{5,7},{6,1},{7,3},{8,12},{9,14},{10,... | collective-permute-start | bytes 1572872 | tf_op jit(solution)/shard_map/ppermute | solution.py:183
  138.2 122.4 %all-gather.8.cloned.1.call-start = ((), (), s32[]{:S(2)}) async-start(), calls=%async_computation.12 | async-start | bytes 2621440 | tf_op jit(solution)/shard_map/all_gather | solution.py:53
  138.2 23.1 %collective-permute-start.23 = (bf16[128,2048]{1,0:T(8,128)(2,1)}, bf16[128,2048]{1,0:T(8,128)(2,1)S(1)}, u32[]{:S(2)}, u32[]{:S(2)}) collective-permute-start(bf16[128,2048]{1,0:T(8,128)(2,1)} %get-tuple-element.151), channel_id=1, source_target_pairs={{0,6},{1,4},{2,2},{3,0},{4,7},{5,5},{6,3},{7,1},{8,14},{9,12},{10,... | collective-permute-start | bytes 1572872 | tf_op jit(solution)/shard_map/ppermute | solution.py:183
  193.0 21.4 %collective-permute-start.30 = (bf16[128,2048]{1,0:T(8,128)(2,1)}, bf16[128,2048]{1,0:T(8,128)(2,1)}, u32[]{:S(2)}, u32[]{:S(2)}) collective-permute-start(bf16[128,2048]{1,0:T(8,128)(2,1)} %fusion.2), channel_id=1, source_target_pairs={{0,2},{1,3},{2,0},{3,1},{4,6},{5,7},{6,4},{7,5},{8,10},{9,11},{10,... | collective-permute-start | bytes 1572872 | tf_op jit(solution)/shard_map/ppermute | solution.py:98
  195.7 18.7 %collective-permute-start.28 = (bf16[128,2048]{1,0:T(8,128)(2,1)}, bf16[128,2048]{1,0:T(8,128)(2,1)}, u32[]{:S(2)}, u32[]{:S(2)}) collective-permute-start(bf16[128,2048]{1,0:T(8,128)(2,1)} %fusion.1), channel_id=1, source_target_pairs={{0,4},{1,5},{2,6},{3,7},{4,0},{5,1},{6,2},{7,3},{8,12},{9,13},{10,... | collective-permute-start | bytes 1572872 | tf_op jit(solution)/shard_map/ppermute | solution.py:98
  198.5 22.4 %collective-permute-start.26 = (bf16[128,2048]{1,0:T(8,128)(2,1)}, bf16[128,2048]{1,0:T(8,128)(2,1)}, u32[]{:S(2)}, u32[]{:S(2)}) collective-permute-start(bf16[128,2048]{1,0:T(8,128)(2,1)} %fusion), channel_id=1, source_target_pairs={{0,6},{1,7},{2,4},{3,5},{4,2},{5,3},{6,0},{7,1},{8,14},{9,15},{10,... | collective-permute-start | bytes 1572872 | tf_op jit(solution)/shard_map/ppermute | solution.py:98
  199.0 107.3 %reduce-scatter.6.cloned.1.call-start = ((), (), s32[]{:S(2)}) async-start(), calls=%async_computation.13 | async-start | bytes 2621440 | tf_op jit(solution)/shard_map/reduce_scatter | solution.py:57
  256.5 103.9 %reduce-scatter.8.cloned.1.call-start = ((), (), s32[]{:S(2)}) async-start(), calls=%async_computation.14 | async-start | bytes 2621440 | tf_op jit(solution)/shard_map/reduce_scatter | solution.py:57
  278.9 23.6 %collective-permute-start.43 = (bf16[128,2048]{1,0:T(8,128)(2,1)}, bf16[128,2048]{1,0:T(8,128)(2,1)}, u32[]{:S(2)}, u32[]{:S(2)}) collective-permute-start(bf16[128,2048]{1,0:T(8,128)(2,1)} %add_convert_fusion.8), channel_id=1, source_target_pairs={{0,6},{1,7},{2,4},{3,5},{4,2},{5,3},{6,0},{7,1},{8,14},{9,15},{10,... | collective-permute-start | bytes 1572872 | tf_op jit(solution)/shard_map/ppermute | solution.py:98
  309.3 162.4 %reduce-scatter.12.cloned.1.call-start = ((), (), s32[]{:S(2)}) async-start(), calls=%async_computation.16 | async-start | bytes 2621440 | tf_op jit(solution)/shard_map/reduce_scatter | solution.py:57
  344.8 154.1 %reduce-scatter.10.cloned.1.call-start = ((), (), s32[]{:S(2)}) async-start(), calls=%async_computation.15 | async-start | bytes 5242880 | tf_op jit(solution)/shard_map/reduce_scatter | solution.py:57
  368.8 152.6 %reduce-scatter.14.cloned.1.call-start = ((), (), s32[]{:S(2)}) async-start(), calls=%async_computation.17 | async-start | bytes 2621440 | tf_op jit(solution)/shard_map/reduce_scatter | solution.py:57
  378.3 21.8 %collective-permute-start.59 = (bf16[128,2048]{1,0:T(8,128)(2,1)S(1)}, bf16[128,2048]{1,0:T(8,128)(2,1)S(1)}, u32[]{:S(2)}, u32[]{:S(2)}) collective-permute-start(bf16[128,2048]{1,0:T(8,128)(2,1)S(1)} %convolution_convert_fusion.9), channel_id=1, source_target_pairs={{0,1},{1,0},{2,3},{3,2},{4,5},{5,4},{6,7},{7,6},{8,9},{9,8},{10,11... | collective-permute-start | bytes 1572872 | tf_op jit(solution)/shard_map/ppermute | solution.py:98
  381.9 24.9 %collective-permute-start.57 = (bf16[128,2048]{1,0:T(8,128)(2,1)S(1)}, bf16[128,2048]{1,0:T(8,128)(2,1)S(1)}, u32[]{:S(2)}, u32[]{:S(2)}) collective-permute-start(bf16[128,2048]{1,0:T(8,128)(2,1)S(1)} %convolution_convert_fusion.10), channel_id=1, source_target_pairs={{0,1},{1,0},{2,3},{3,2},{4,5},{5,4},{6,7},{7,6},{8,9},{9,8},{10,11... | collective-permute-start | bytes 1572872 | tf_op jit(solution)/shard_map/ppermute | solution.py:98
  385.3 25.9 %collective-permute-start.55 = (bf16[128,2048]{1,0:T(8,128)(2,1)S(1)}, bf16[128,2048]{1,0:T(8,128)(2,1)S(1)}, u32[]{:S(2)}, u32[]{:S(2)}) collective-permute-start(bf16[128,2048]{1,0:T(8,128)(2,1)S(1)} %convolution_convert_fusion.11), channel_id=1, source_target_pairs={{0,1},{1,0},{2,3},{3,2},{4,5},{5,4},{6,7},{7,6},{8,9},{9,8},{10,11... | collective-permute-start | bytes 1572872 | tf_op jit(solution)/shard_map/ppermute | solution.py:98
  389.7 37.5 %collective-permute-start.54 = (bf16[128,2048]{1,0:T(8,128)(2,1)}, bf16[128,2048]{1,0:T(8,128)(2,1)}, u32[]{:S(2)}, u32[]{:S(2)}) collective-permute-start(bf16[128,2048]{1,0:T(8,128)(2,1)} %convolution_convert_fusion.12), channel_id=1, source_target_pairs={{0,1},{1,0},{2,3},{3,2},{4,5},{5,4},{6,7},{7,6},{8,9},{9,8},{10,11... | collective-permute-start | bytes 1572872 | tf_op jit(solution)/shard_map/ppermute | solution.py:98
  395.4 23.3 %collective-permute-start.68 = (bf16[128,2048]{1,0:T(8,128)(2,1)S(1)}, bf16[128,2048]{1,0:T(8,128)(2,1)S(1)}, u32[]{:S(2)}, u32[]{:S(2)}) collective-permute-start(bf16[128,2048]{1,0:T(8,128)(2,1)S(1)} %get-tuple-element.136), channel_id=1, source_target_pairs={{0,0},{2,1},{4,2},{6,3},{1,4},{3,5},{5,6},{7,7},{8,8},{10,9},{12,1... | collective-permute-start | bytes 1572872 | tf_op jit(solution)/shard_map/ppermute | solution.py:197
  400.1 21.0 %collective-permute-start.69 = (bf16[128,2048]{1,0:T(8,128)(2,1)S(1)}, bf16[128,2048]{1,0:T(8,128)(2,1)S(1)}, u32[]{:S(2)}, u32[]{:S(2)}) collective-permute-start(bf16[128,2048]{1,0:T(8,128)(2,1)S(1)} %get-tuple-element.135), channel_id=1, source_target_pairs={{2,0},{0,1},{6,2},{4,3},{3,4},{1,5},{7,6},{5,7},{10,8},{8,9},{14,1... | collective-permute-start | bytes 1572872 | tf_op jit(solution)/shard_map/ppermute | solution.py:197
  423.2 24.7 %collective-permute-start.56 = (bf16[128,2048]{1,0:T(8,128)(2,1)}, bf16[128,2048]{1,0:T(8,128)(2,1)}, u32[]{:S(2)}, u32[]{:S(2)}) collective-permute-start(bf16[128,2048]{1,0:T(8,128)(2,1)} %add_convert_fusion.5), channel_id=1, source_target_pairs={{0,6},{1,7},{2,4},{3,5},{4,2},{5,3},{6,0},{7,1},{8,14},{9,15},{10,... | collective-permute-start | bytes 1572872 | tf_op jit(solution)/shard_map/ppermute | solution.py:98
  457.4 38.3 %collective-permute-start.61 = (bf16[128,2048]{1,0:T(8,128)(2,1)}, bf16[128,2048]{1,0:T(8,128)(2,1)}, u32[]{:S(2)}, u32[]{:S(2)}) collective-permute-start(bf16[128,2048]{1,0:T(8,128)(2,1)} %convolution_convert_fusion.8), channel_id=1, source_target_pairs={{0,1},{1,0},{2,3},{3,2},{4,5},{5,4},{6,7},{7,6},{8,9},{9,8},{10,11... | collective-permute-start | bytes 1572872 | tf_op jit(solution)/shard_map/ppermute | solution.py:98
  459.2 36.5 %collective-permute-start.67 = (bf16[128,2048]{1,0:T(8,128)(2,1)}, bf16[128,2048]{1,0:T(8,128)(2,1)}, u32[]{:S(2)}, u32[]{:S(2)}) collective-permute-start(bf16[128,2048]{1,0:T(8,128)(2,1)} %add_convert_fusion), channel_id=1, source_target_pairs={{0,2},{1,3},{2,0},{3,1},{4,6},{5,7},{6,4},{7,5},{8,10},{9,11},{10,... | collective-permute-start | bytes 1572872 | tf_op jit(solution)/shard_map/ppermute | solution.py:98
  461.0 34.7 %collective-permute-start.65 = (bf16[128,2048]{1,0:T(8,128)(2,1)}, bf16[128,2048]{1,0:T(8,128)(2,1)}, u32[]{:S(2)}, u32[]{:S(2)}) collective-permute-start(bf16[128,2048]{1,0:T(8,128)(2,1)} %add_convert_fusion.1), channel_id=1, source_target_pairs={{0,4},{1,5},{2,6},{3,7},{4,0},{5,1},{6,2},{7,3},{8,12},{9,13},{10,... | collective-permute-start | bytes 1572872 | tf_op jit(solution)/shard_map/ppermute | solution.py:98
  464.5 31.3 %collective-permute-start.63 = (bf16[128,2048]{1,0:T(8,128)(2,1)}, bf16[128,2048]{1,0:T(8,128)(2,1)}, u32[]{:S(2)}, u32[]{:S(2)}) collective-permute-start(bf16[128,2048]{1,0:T(8,128)(2,1)} %add_convert_fusion.2), channel_id=1, source_target_pairs={{0,6},{1,7},{2,4},{3,5},{4,2},{5,3},{6,0},{7,1},{8,14},{9,15},{10,... | collective-permute-start | bytes 1572872 | tf_op jit(solution)/shard_map/ppermute | solution.py:98
  465.2 27.0 %all-to-all-start.4 = ((bf16[8,64,512]{2,1,0:T(8,128)(2,1)}), bf16[8,64,512]{2,1,0:T(8,128)(2,1)}, u32[]{:S(2)}, u32[]{:S(2)}) async-start(bf16[8,64,512]{2,1,0:T(8,128)(2,1)} %bitcast.221), calls=%async_computation.9 | async-start | bytes 1048576 | tf_op jit(solution)/shard_map/all_to_all | solution.py:202
  (152 other events, 1066.1 us)
Sparse Core Ops, SparseCore 0:
  51.8 116.8 all-gather.3
  170.2 44.1 all-gather.5
  216.0 44.5 all-gather.7
  262.8 42.6 reduce-scatter.5
  309.5 41.3 reduce-scatter.7
  353.0 43.1 reduce-scatter.11
  398.6 76.0 reduce-scatter.9
  477.0 44.3 reduce-scatter.13
